TPU v7x, 32 devices: a whole 2x2x4 slice. The times are simulated.
32 devices in a mesh: band: 2 (over x), wide: 16 (over z, y, core).
Axes of the slice: x: 2, y: 2, z: 4, core: 2. Of those that a mesh axis runs over, the one named last changes fastest.
Arguments:
- visibilities: bfloat16 [2, 1, 256, 40960], P(None, None, ('band', 'wide')), parts along dimension 2, may hold values from -1 to 2.5, as said below
- kept_baseline_mask: int32 [81920], P('band'), parts along dimension 0, may hold values 0 or 1
- fitted_mode_count: int32 [40960], P('wide'), may hold values from 4 to 16
- station_order: int32 [256], replicated, may hold values from 0 to 255, each once
- station_xy: float32 [1, 2, 256], replicated, may hold values from -8 to 8
- comp_lm: float32 [2, 512], replicated, may hold values from -0.5 to 0.5
- comp_flux: float32 [512], replicated, may hold values from 0.2 to 2
- centre_flux: float32 [256], P(('band', 'wide')), parts along dimension 0, may hold values from 1 to 3
Outputs:
- gains: float32 [2, 512], P(None, 'band'), parts along dimension 1
- residual: bfloat16 [2, 1, 256, 40960], P(None, None, 'band', 'wide'), parts along dimension 2
There are 2 independent parts, one for each index of `band`. A program takes and returns all parts, laid end to end along the dimension named above; an argument that names none is the same for every part. Nothing has to cross between parts.
Inputs may be any that keep to these rules, and one draw needn't show every extreme that they name: `visibilities`: real parts lie in 0.5 to 2.5, imaginary parts in -1 to 1. Each baseline fits its fitted_mode_count lowest modes.
All inputs are finite; a program needn't handle non-finite values.
Results may differ from a plain program's by a relative error of at most 0.011.
Values may be sent and summed in bfloat16 or wider, within the bound.
No kernel may reach another device: no remote copies, remote signals or barrier semaphores. Data moves between devices by JAX's collectives and lax.ppermute only.
A program may use at most 128 MiB of HBM per device.

v0:
```python
import math

import jax
import jax.numpy as jnp
import numpy as np
from jax import lax
from jax.sharding import PartitionSpec as P

GROUP = 64
COMPS = 512
FREQ_CHANNELS = 128
FOREGROUND_MODES = 16
CAL_ITERS = 3
ROUNDS = 3


def block_pairs(groups):
    row_list = []
    col_list = []
    for first_group in range(groups):
        for second_group in range(first_group, groups):
            row_list.append(first_group)
            col_list.append(second_group)
    return (np.array(row_list, np.int32), np.array(col_list, np.int32))


def baseline_tables(groups, group_size):
    row_groups, col_groups = block_pairs(groups)
    inside = np.arange(group_size * group_size)
    row_inside = inside // group_size
    col_inside = inside % group_size
    row_station = (
        (row_groups[:, None] * group_size + row_inside[None, :]).reshape(-1).astype(np.int32)
    )
    col_station = (
        (col_groups[:, None] * group_size + col_inside[None, :]).reshape(-1).astype(np.int32)
    )
    usable = (
        (row_groups[:, None] != col_groups[:, None]) | (row_inside[None, :] < col_inside[None, :])
    ).reshape(-1)
    return (row_station, col_station, usable.astype(np.float32))


def cosine_basis(channels, mode_total):
    channel_mid = jnp.arange(channels, dtype=jnp.float32)[:, None] + 0.5
    mode_order = jnp.arange(mode_total, dtype=jnp.float32)[None, :]
    mode_scale = jnp.where(mode_order == 0, math.sqrt(1.0 / channels), math.sqrt(2.0 / channels))
    return mode_scale * jnp.cos(math.pi / channels * channel_mid * mode_order)


def block_products(row_cos, row_sin, col_cos, col_sin):
    real_part = jnp.einsum(
        "bik,bjk->bij", row_cos, col_cos, preferred_element_type=jnp.float32
    ) + jnp.einsum("bik,bjk->bij", row_sin, col_sin, preferred_element_type=jnp.float32)
    imag_part = jnp.einsum(
        "bik,bjk->bij", row_sin, col_cos, preferred_element_type=jnp.float32
    ) - jnp.einsum("bik,bjk->bij", row_cos, col_sin, preferred_element_type=jnp.float32)
    return (real_part.reshape(-1), imag_part.reshape(-1))


def predict_channel(
    xy_pair, comp_lm, flux_weight, centre, frequency, row_groups, col_groups, groups
):
    offset = xy_pair[0][:, None] * comp_lm[0][None, :] + xy_pair[1][:, None] * comp_lm[1][None, :]
    phase_angle = 2.0 * math.pi * frequency * offset
    cosine = jnp.cos(phase_angle)
    sine_part = jnp.sin(phase_angle)
    plain_cos = cosine.astype(jnp.bfloat16).reshape(groups, GROUP, -1)
    plain_sin = sine_part.astype(jnp.bfloat16).reshape(groups, GROUP, -1)
    bright_cos = (cosine * flux_weight[None, :]).astype(jnp.bfloat16).reshape(groups, GROUP, -1)
    bright_sin = (sine_part * flux_weight[None, :]).astype(jnp.bfloat16).reshape(groups, GROUP, -1)
    real_part, imag_part = block_products(
        bright_cos[row_groups], bright_sin[row_groups], plain_cos[col_groups], plain_sin[col_groups]
    )
    return jnp.stack([real_part + centre, imag_part]).astype(jnp.bfloat16)


def channel_sums(observed, model_visibility, weights):
    obs_re = observed[0].astype(jnp.float32)
    obs_im = observed[1].astype(jnp.float32)
    mod_re = model_visibility[0].astype(jnp.float32)
    mod_im = model_visibility[1].astype(jnp.float32)
    cross_re = jnp.sum(obs_re * mod_re + obs_im * mod_im, axis=(0, 1)) * weights
    cross_im = jnp.sum(obs_im * mod_re - obs_re * mod_im, axis=(0, 1)) * weights
    model_power = jnp.sum(mod_re * mod_re + mod_im * mod_im, axis=(0, 1)) * weights
    return jnp.stack([cross_re, cross_im, model_power])


def block_gains(gain_pair, row_groups, col_groups, groups):
    grouped = gain_pair.reshape(2, groups, GROUP)
    row_re = grouped[0][row_groups][:, :, None]
    row_im = grouped[1][row_groups][:, :, None]
    col_re = grouped[0][col_groups][:, None, :]
    col_im = grouped[1][col_groups][:, None, :]
    return (row_re, row_im, col_re, col_im)


def block_station_sums(baseline_totals, gain_pair, row_groups, col_groups, groups):
    block_total = row_groups.shape[0]
    blocked = baseline_totals.reshape(3, block_total, GROUP, GROUP)
    cross_re = blocked[0]
    cross_im = blocked[1]
    model_power = blocked[2]
    row_re, row_im, col_re, col_im = block_gains(gain_pair, row_groups, col_groups, groups)
    row_terms = jnp.stack(
        [
            jnp.sum(cross_re * col_re - cross_im * col_im, axis=2),
            jnp.sum(cross_re * col_im + cross_im * col_re, axis=2),
            jnp.sum(model_power * (col_re * col_re + col_im * col_im), axis=2),
        ]
    )
    col_terms = jnp.stack(
        [
            jnp.sum(cross_re * row_re + cross_im * row_im, axis=1),
            jnp.sum(cross_re * row_im - cross_im * row_re, axis=1),
            jnp.sum(model_power * (row_re * row_re + row_im * row_im), axis=1),
        ]
    )
    group_ids = jnp.arange(groups, dtype=jnp.int32)[:, None]
    row_member = (group_ids == jnp.asarray(row_groups)[None, :]).astype(jnp.float32)
    col_member = (group_ids == jnp.asarray(col_groups)[None, :]).astype(jnp.float32)
    totals = jnp.einsum(
        "gb,tbi->tgi", row_member, row_terms, precision=lax.Precision.HIGHEST
    ) + jnp.einsum("gb,tbi->tgi", col_member, col_terms, precision=lax.Precision.HIGHEST)
    return totals.reshape(3, groups * GROUP)


def gain_products(gain_pair, row_groups, col_groups, groups):
    row_re, row_im, col_re, col_im = block_gains(gain_pair, row_groups, col_groups, groups)
    prod_re = row_re * col_re + row_im * col_im
    prod_im = row_im * col_re - row_re * col_im
    return (prod_re.reshape(-1), prod_im.reshape(-1))


def gain_update(station_terms, gain_pair, iteration):
    updated = jnp.stack([station_terms[0] / station_terms[2], station_terms[1] / station_terms[2]])
    if iteration % 2 == 1:
        updated = 0.5 * (updated + gain_pair)
    return updated


def corrupted_gap(observed, model_visibility, prod_re, prod_im, weights):
    mod_re = model_visibility[0].astype(jnp.float32)
    mod_im = model_visibility[1].astype(jnp.float32)
    pred_re = prod_re * mod_re - prod_im * mod_im
    pred_im = prod_re * mod_im + prod_im * mod_re
    data_gap = (
        jnp.stack(
            [observed[0].astype(jnp.float32) - pred_re, observed[1].astype(jnp.float32) - pred_im]
        )
        * weights
    )
    return lax.optimization_barrier(data_gap.astype(jnp.bfloat16))


def fit_modes(data_gap, counts, weights):
    channels = data_gap.shape[2]
    mode_basis = cosine_basis(channels, FOREGROUND_MODES)
    coefficients = jnp.einsum(
        "fk,csfb->cskb", mode_basis, data_gap.astype(jnp.float32), precision=lax.Precision.HIGHEST
    )
    kept_modes = (jnp.arange(FOREGROUND_MODES, dtype=jnp.int32)[:, None] < counts[None, :]).astype(
        jnp.float32
    )
    fitted = jnp.einsum(
        "fk,cskb->csfb", mode_basis, coefficients * kept_modes, precision=lax.Precision.HIGHEST
    )
    return lax.optimization_barrier((fitted * weights).astype(jnp.bfloat16))


def solve_gains(partial_totals, gain_pair, row_groups, col_groups, groups):
    for iteration in range(CAL_ITERS):
        local_terms = block_station_sums(partial_totals, gain_pair, row_groups, col_groups, groups)
        station_terms = lax.psum(local_terms, "wide")
        gain_pair = gain_update(station_terms, gain_pair, iteration)
    return gain_pair


def send_gap(data_gap):
    return lax.all_to_all(data_gap, "wide", split_axis=3, concat_axis=2, tiled=True)


def body(
    visibilities,
    kept_baseline_mask,
    fitted_mode_count,
    station_order,
    station_xy,
    comp_lm,
    comp_flux,
    centre_flux,
):
    wide_count = lax.axis_size("wide")
    wide_rank = lax.axis_index("wide")
    slabs = visibilities.shape[1]
    local_chan = visibilities.shape[2]
    total_base = visibilities.shape[3]
    local_base = total_base // wide_count
    stations = station_order.shape[0]
    groups = stations // GROUP
    row_groups, col_groups = block_pairs(groups)
    row_np, col_np, usable_np = baseline_tables(groups, GROUP)
    weights_all = kept_baseline_mask.astype(jnp.float32) * jnp.asarray(usable_np)
    first_base = wide_rank * local_base
    weights_mine = lax.dynamic_slice_in_dim(weights_all, first_base, local_base)
    xy_ordered = station_xy[:, :, station_order]
    flux_weight = comp_flux * (1.0 / math.sqrt(COMPS))
    gain_start = jnp.stack(
        [jnp.ones((stations,), jnp.float32), jnp.zeros((stations,), jnp.float32)]
    )

    def predict_item(item_index):
        slab_id = item_index // local_chan
        chan_local = item_index % local_chan
        channel = wide_rank * local_chan + chan_local
        frequency = 1.0 + 0.25 * channel.astype(jnp.float32) / FREQ_CHANNELS
        return predict_channel(
            xy_ordered[slab_id],
            comp_lm,
            flux_weight,
            centre_flux[chan_local],
            frequency,
            row_groups,
            col_groups,
            groups,
        )

    model_visibility = lax.map(predict_item, jnp.arange(slabs * local_chan, dtype=jnp.int32))
    model_visibility = model_visibility.reshape(slabs, local_chan, 2, total_base).transpose(
        2, 0, 1, 3
    )
    gain_pair = solve_gains(
        channel_sums(visibilities, model_visibility, weights_all),
        gain_start,
        row_groups,
        col_groups,
        groups,
    )
    for round_id in range(ROUNDS - 1):
        prod_re, prod_im = gain_products(gain_pair, row_groups, col_groups, groups)
        data_gap = send_gap(
            corrupted_gap(visibilities, model_visibility, prod_re, prod_im, weights_all)
        )
        fitted = fit_modes(data_gap, fitted_mode_count, weights_mine)
        fitted_back = lax.all_to_all(fitted, "wide", split_axis=2, concat_axis=3, tiled=True)
        model_visibility = (
            model_visibility.astype(jnp.float32) + fitted_back.astype(jnp.float32)
        ).astype(jnp.bfloat16)
        gain_pair = solve_gains(
            channel_sums(visibilities, model_visibility, weights_all),
            gain_pair,
            row_groups,
            col_groups,
            groups,
        )
    prod_re, prod_im = gain_products(gain_pair, row_groups, col_groups, groups)
    residual = send_gap(
        corrupted_gap(visibilities, model_visibility, prod_re, prod_im, weights_all)
    )
    gains = jnp.zeros((2, stations), jnp.float32).at[:, station_order].set(gain_pair)
    return (gains, residual)


def solution(mesh):
    placed = (
        P(None, None, ("band", "wide"), None),
        P("band"),
        P("wide"),
        P(),
        P(),
        P(),
        P(),
        P(("band", "wide")),
    )
    return jax.shard_map(
        body,
        mesh=mesh,
        in_specs=placed,
        out_specs=(P(None, "band"), P(None, None, "band", "wide")),
        check_vma=False,
    )
```

profile of v0, /device:TPU:0, one launch (start us, length us, event | category | flops | bytes accessed | tf_op | source)
XLA Modules:
  0.0 1008.5 jit_solution(6151701743533401194)
XLA Ops:
  5.0 98.8 %while.14 = (s32[]{:T(128)}, bf16[8,2,40960]{2,1,0:T(2,128)(2,1)}, s32[8]{0:T(128)S(1)}, s32[]{:T(128)}, f32[1,2,256]{2,1,0:T(2,128)S(1)}, /*index=5*/f32[2,512]...) while((s32[]{:T(128)}, bf16[8,2,40960]{2,1,0:T(2,128)(2,1)}, ...), condition=%wide.region_1.2_spmd.clone.clone, body=%wide.region_0.1_spmd.sunk.clone.clone.sunk | while | flops 169617424 | bytes 13043148 | solution.py:228
  114.0 34.9 %psum.63 = f32[3,256]{1,0:T(4,128)S(1)} all-reduce(f32[3,256]{1,0:T(4,128)S(1)} %reshape.1557), channel_id=1, replica_groups=mesh['band'=2,'wide'=16] {'wide'}, use_global_device_ids=true, to_apply=%region_11.12 | all-reduce | flops 768 | bytes 6144 | tf_op jit(solution)/shard_map/psum | solution.py:174
  154.6 29.5 %psum.64 = f32[3,256]{1,0:T(4,128)S(1)} all-reduce(f32[3,256]{1,0:T(4,128)S(1)} %reshape.1558), channel_id=1, replica_groups=mesh['band'=2,'wide'=16] {'wide'}, use_global_device_ids=true, to_apply=%region_18.19 | all-reduce | flops 768 | bytes 6144 | tf_op jit(solution)/shard_map/psum | solution.py:174
  188.6 29.5 %psum.65 = f32[3,256]{1,0:T(4,128)S(1)} all-reduce(f32[3,256]{1,0:T(4,128)S(1)} %reshape.1559), channel_id=1, replica_groups=mesh['band'=2,'wide'=16] {'wide'}, use_global_device_ids=true, to_apply=%region_25.26 | all-reduce | flops 768 | bytes 6144 | tf_op jit(solution)/shard_map/psum | solution.py:174
  223.2 30.8 %copy.118 = bf16[2,1,8,40960]{2,0,1,3:T(2,128)(2,1)} copy(bf16[2,1,8,40960]{3,2,0,1:T(8,128)(2,1)S(1)} %fusion.17) | data formatting | bytes 2621440 | tf_op jit(solution)/shard_map/optimization_barrier | solution.py:153
  282.5 27.2 %all-to-all-done = bf16[16,2,20480]{2,1,0:T(2,128)(2,1)S(1)} async-done(((bf16[16,2,20480]{2,1,0:T(2,128)(2,1)}), bf16[16,2,20480]{2,1,0:T(2,128)(2,1)S(1)}, u32[]{:S(2)}, u32[]{:S(2)}) %all-to-all-start) | async-done | bytes 1310752 | tf_op jit(solution)/shard_map/all_to_all | solution.py:180
  309.7 25.6 %reshape.2060 = bf16[40960,1,2,8]{3,2,1,0:T(2,128)(2,1)} reshape(bf16[16,2,20480]{2,1,0:T(2,128)(2,1)S(1)} %all-to-all-done) | data formatting | bytes 2621440
  335.3 37.4 %copy.119 = bf16[2,1,8,16,2560]{4,2,3,0,1:T(8,128)(2,1)S(1)} copy(bf16[2,1,8,16,2560]{2,0,4,3,1:T(2,128)(2,1)} %bitcast.231) | data formatting | bytes 2621440 | tf_op jit(solution)/shard_map/all_to_all | solution.py:180
  388.7 27.4 %all-to-all-done.1 = bf16[2,1,128,2560]{3,0,1,2:T(2,128)(2,1)S(1)} async-done(((bf16[2,1,128,2560]{3,0,1,2:T(2,128)(2,1)}), bf16[2,1,128,2560]{3,0,1,2:T(2,128)(2,1)S(1)}, u32[]{:S(2)}, u32[]{:S(2)}) %all-to-all-start.1) | async-done | bytes 1310752 | tf_op jit(solution)/shard_map/all_to_all | solution.py:245
  426.6 36.0 %psum.66 = f32[3,256]{1,0:T(4,128)S(1)} all-reduce(f32[3,256]{1,0:T(4,128)S(1)} %reshape.1562), channel_id=1, replica_groups=mesh['band'=2,'wide'=16] {'wide'}, use_global_device_ids=true, to_apply=%region_35.36 | all-reduce | flops 768 | bytes 6144 | tf_op jit(solution)/shard_map/psum | solution.py:174
  467.7 29.7 %psum.67 = f32[3,256]{1,0:T(4,128)S(1)} all-reduce(f32[3,256]{1,0:T(4,128)S(1)} %reshape.1563), channel_id=1, replica_groups=mesh['band'=2,'wide'=16] {'wide'}, use_global_device_ids=true, to_apply=%region_42.43 | all-reduce | flops 768 | bytes 6144 | tf_op jit(solution)/shard_map/psum | solution.py:174
  502.0 29.5 %psum.68 = f32[3,256]{1,0:T(4,128)S(1)} all-reduce(f32[3,256]{1,0:T(4,128)S(1)} %reshape.1564), channel_id=1, replica_groups=mesh['band'=2,'wide'=16] {'wide'}, use_global_device_ids=true, to_apply=%region_49.50 | all-reduce | flops 768 | bytes 6144 | tf_op jit(solution)/shard_map/psum | solution.py:174
  537.7 36.9 %copy.122 = bf16[2,1,8,40960]{2,0,1,3:T(2,128)(2,1)} copy(bf16[2,1,8,40960]{3,2,0,1:T(8,128)(2,1)} %fusion.18) | data formatting | bytes 2621440 | tf_op jit(solution)/shard_map/optimization_barrier | solution.py:153
  598.9 35.9 %all_to_all.66 = bf16[16,2,20480]{2,1,0:T(2,128)(2,1)} all-to-all(bf16[16,2,20480]{2,1,0:T(2,128)(2,1)} %reshape.2061), channel_id=1, replica_groups=mesh['band'=2,'wide'=16] {'wide'}, dimensions={0} | all-to-all | bytes 2621440 | tf_op jit(solution)/shard_map/all_to_all | solution.py:180
  634.8 26.3 %reshape.2062 = bf16[40960,1,2,8]{3,2,1,0:T(2,128)(2,1)} reshape(bf16[16,2,20480]{2,1,0:T(2,128)(2,1)} %all_to_all.66) | data formatting | bytes 2621440
  661.1 38.8 %copy.123 = bf16[2,1,8,16,2560]{4,2,3,0,1:T(8,128)(2,1)} copy(bf16[2,1,8,16,2560]{2,0,4,3,1:T(2,128)(2,1)} %bitcast.233) | data formatting | bytes 2621440 | tf_op jit(solution)/shard_map/all_to_all | solution.py:180
  716.4 27.4 %all-to-all-done.3 = bf16[2,1,128,2560]{3,0,1,2:T(2,128)(2,1)} async-done(((bf16[2,1,128,2560]{3,0,1,2:T(2,128)(2,1)}), bf16[2,1,128,2560]{3,0,1,2:T(2,128)(2,1)}, u32[]{:S(2)}, u32[]{:S(2)}) %all-to-all-start.3) | async-done | bytes 1310752 | tf_op jit(solution)/shard_map/all_to_all | solution.py:245
  749.0 36.0 %psum.69 = f32[3,256]{1,0:T(4,128)S(1)} all-reduce(f32[3,256]{1,0:T(4,128)S(1)} %reshape.1567), channel_id=1, replica_groups=mesh['band'=2,'wide'=16] {'wide'}, use_global_device_ids=true, to_apply=%region_59.60 | all-reduce | flops 768 | bytes 6144 | tf_op jit(solution)/shard_map/psum | solution.py:174
  789.1 29.5 %psum.70 = f32[3,256]{1,0:T(4,128)S(1)} all-reduce(f32[3,256]{1,0:T(4,128)S(1)} %reshape.1568), channel_id=1, replica_groups=mesh['band'=2,'wide'=16] {'wide'}, use_global_device_ids=true, to_apply=%region_66.67 | all-reduce | flops 768 | bytes 6144 | tf_op jit(solution)/shard_map/psum | solution.py:174
  822.2 29.5 %psum.71 = f32[3,256]{1,0:T(4,128)S(1)} all-reduce(f32[3,256]{1,0:T(4,128)S(1)} %reshape.1569), channel_id=1, replica_groups=mesh['band'=2,'wide'=16] {'wide'}, use_global_device_ids=true, to_apply=%region_73.74 | all-reduce | flops 768 | bytes 6144 | tf_op jit(solution)/shard_map/psum | solution.py:174
  857.5 30.8 %copy.127 = bf16[2,1,8,40960]{2,0,1,3:T(2,128)(2,1)} copy(bf16[2,1,8,40960]{3,2,0,1:T(8,128)(2,1)S(1)} %fusion.19) | data formatting | bytes 2621440 | tf_op jit(solution)/shard_map/optimization_barrier | solution.py:153
  918.3 25.3 %all-to-all-done.4 = bf16[16,2,20480]{2,1,0:T(2,128)(2,1)S(1)} async-done(((bf16[16,2,20480]{2,1,0:T(2,128)(2,1)}), bf16[16,2,20480]{2,1,0:T(2,128)(2,1)S(1)}, u32[]{:S(2)}, u32[]{:S(2)}) %all-to-all-start.4) | async-done | bytes 1310752 | tf_op jit(solution)/shard_map/all_to_all | solution.py:180
  943.7 25.6 %reshape.2064 = bf16[40960,1,2,8]{3,2,1,0:T(2,128)(2,1)} reshape(bf16[16,2,20480]{2,1,0:T(2,128)(2,1)S(1)} %all-to-all-done.4) | data formatting | bytes 2621440
  969.3 38.8 %copy.128 = bf16[2,1,16,8,2560]{4,3,2,0,1:T(8,128)(2,1)} copy(bf16[2,1,16,8,2560]{3,0,4,2,1:T(2,128)(2,1)} %bitcast.235) | data formatting | bytes 2621440 | tf_op jit(solution)/shard_map/all_to_all | solution.py:180
  (418 shorter events, 274.0 us)
Async XLA Ops:
  5.0 6.8 copy-start.13
  17.3 6.8 copy-start.13
  29.7 6.8 copy-start.13
  42.0 6.8 copy-start.13
  54.4 6.8 copy-start.13
  66.7 6.8 copy-start.13
  79.1 6.8 copy-start.13
  91.4 6.8 copy-start.13
  103.7 2.1 copy-start
  105.9 1.6 copy-start.6
  108.4 5.2 copy-start.14
  108.4 5.4 copy-start.12
  278.3 4.1 copy-start.15
  278.3 31.3 %all-to-all-start = ((bf16[16,2,20480]{2,1,0:T(2,128)(2,1)}), bf16[16,2,20480]{2,1,0:T(2,128)(2,1)S(1)}, u32[]{:S(2)}, u32[]{:S(2)}) async-start(bf16[16,2,20480]{2,1,0:T(2,128)(2,1)} %reshape.2059), calls=%async_computation | async-start | bytes 2621440 | tf_op jit(solution)/shard_map/all_to_all | solution.py:180
  282.5 90.2 %copy-start.4 = (f32[16,2560]{1,0:T(8,128)}, f32[16,2560]{1,0:T(8,128)S(1)}, u32[]{:S(2)}) copy-start(f32[16,2560]{1,0:T(8,128)S(1)} %fusion.55) | copy-start | bytes 491524
  380.7 35.4 %all-to-all-start.1 = ((bf16[2,1,128,2560]{3,0,1,2:T(2,128)(2,1)}), bf16[2,1,128,2560]{3,0,1,2:T(2,128)(2,1)S(1)}, u32[]{:S(2)}, u32[]{:S(2)}) async-start(bf16[2,1,128,2560]{3,0,1,2:T(2,128)(2,1)} %copy.120), calls=%async_computation.1 | async-start | bytes 2621440 | tf_op jit(solution)/shard_map/all_to_all | solution.py:245
  418.3 1.6 copy-start.7
  661.1 38.8 %copy-start.5 = (f32[16,2560]{1,0:T(8,128)S(1)}, f32[16,2560]{1,0:T(8,128)}, u32[]{:S(2)}) copy-start(f32[16,2560]{1,0:T(8,128)} %copy-done.4) | copy-start | bytes 491524
  711.8 32.0 %all-to-all-start.3 = ((bf16[2,1,128,2560]{3,0,1,2:T(2,128)(2,1)}), bf16[2,1,128,2560]{3,0,1,2:T(2,128)(2,1)}, u32[]{:S(2)}, u32[]{:S(2)}) async-start(bf16[2,1,128,2560]{3,0,1,2:T(2,128)(2,1)} %copy.124), calls=%async_computation.3 | async-start | bytes 2621440 | tf_op jit(solution)/shard_map/all_to_all | solution.py:245
  745.8 1.6 copy-start.1
  745.8 1.6 copy-start.8
  745.8 1.6 copy-start.11
  821.5 34.3 %copy-start.2 = (bf16[2,1,8,40960]{3,2,0,1:T(8,128)(2,1)S(1)}, bf16[2,1,8,40960]{3,2,0,1:T(8,128)(2,1)}, u32[]{:S(2)}) copy-start(bf16[2,1,8,40960]{3,2,0,1:T(8,128)(2,1)} %copy-done.1) | copy-start | bytes 3932164
  912.6 31.1 %all-to-all-start.4 = ((bf16[16,2,20480]{2,1,0:T(2,128)(2,1)}), bf16[16,2,20480]{2,1,0:T(2,128)(2,1)S(1)}, u32[]{:S(2)}, u32[]{:S(2)}) async-start(bf16[16,2,20480]{2,1,0:T(2,128)(2,1)} %reshape.2063), calls=%async_computation.4 | async-start | bytes 2621440 | tf_op jit(solution)/shard_map/all_to_all | solution.py:180
  (11 other events, 14.3 us)
where the time goes:
time: 1030 us; the launch traced here: 1010 us
  local copies, waits for them, and re-layouts  449 us (44%)
  blocking collectives  320 us (31%)
  waiting for transfers between devices  107 us (10%)
  other arithmetic  65.8 us (6%)
  matrix products  29.8 us (3%)
  starting transfers between devices  20.3 us (2%)
  loops' own time  14.6 us (1%)
    psum x9, blocking collectives, solve_gains(): station_terms = lax.psum(local_terms, 'wide')  284 us
    unnamed x39, local copies, waits for them, and re-layouts  153 us
    all_to_all x3, local copies, waits for them, and re-layouts, send_gap(): lax.all_to_all(data_gap, 'wide', split_axis=3, concat_axis=2, tiled=True)  115 us
    optimization_barrier x3, local copies, waits for them, and re-layouts, corrupted_gap(): return lax.optimization_barrier(data_gap.astype(jnp.bfloat16))  98.4 us
    all_to_all x2, waiting for transfers between devices, body(): lax.all_to_all(fitted, 'wide', split_axis=2, concat_axis=3, tiled=True)  54.8 us
    all_to_all x2, waiting for transfers between devices, send_gap(): lax.all_to_all(data_gap, 'wide', split_axis=3, concat_axis=2, tiled=True)  52.5 us
    all_to_all x1, blocking collectives, send_gap(): lax.all_to_all(data_gap, 'wide', split_axis=3, concat_axis=2, tiled=True)  35.9 us
  transfers between devices with their start and end apart: 4, of which 4 were waited for; matrix products, arithmetic and copies ran while one was open for 0% of the time, Pallas kernels for 0%

commit v1 on v0

v1 whole, which is shorter than its diff:
```python
import math

import jax
import jax.numpy as jnp
import numpy as np
from jax import lax
from jax.experimental import pallas as pl
from jax.experimental.pallas import tpu as pltpu
from jax.sharding import PartitionSpec as P

GROUP = 64
FREQ_CHANNELS = 128
MODES = 16
CAL_ITERS = 3
ROUNDS = 3
STATS = 7
LANES = 128
UNROLL = 4
VMEM = pltpu.MemorySpace.VMEM
SMEM = pltpu.MemorySpace.SMEM
F32 = jnp.float32
BF16 = jnp.bfloat16


def row_groups_of(row, groups):
    block = row >> 6
    first = jnp.zeros_like(block)
    start = jnp.zeros_like(block)
    edge = 0
    for group in range(1, groups):
        edge += groups - group + 1
        past = (block >= edge).astype(jnp.int32)
        first = first + past
        start = start + past * (groups - group + 1)
    return first, block - start + first


def basis_tables():
    mid = np.arange(FREQ_CHANNELS)[:, None] + 0.5
    order = np.arange(MODES)[None, :]
    scale = np.where(order == 0, math.sqrt(1.0 / FREQ_CHANNELS), math.sqrt(2.0 / FREQ_CHANNELS))
    basis = (scale * np.cos(math.pi / FREQ_CHANNELS * mid * order)).astype(np.float32)
    high = np.asarray(jnp.dtype(BF16).type(0)).dtype
    basis_hi = basis.astype(high)
    basis_lo = (basis - basis_hi.astype(np.float32)).astype(high)
    rows = 2 * FREQ_CHANNELS
    blank = np.zeros((rows, MODES), np.float32)
    parts = {}
    for name, table in (("hi", basis_hi), ("lo", basis_lo)):
        for side in range(2):
            spread = blank.copy().reshape(FREQ_CHANNELS // 8, 2, 8, MODES)
            spread[:, side] = table.astype(np.float32).reshape(FREQ_CHANNELS // 8, 8, MODES)
            parts[name, side] = spread.reshape(rows, MODES)
    fit = np.concatenate(
        [parts["hi", 0], parts["lo", 0], parts["hi", 1], parts["lo", 1]], axis=1
    ).T.astype(high)
    expand = np.concatenate(
        [parts["hi", 0], parts["hi", 0], parts["hi", 1], parts["hi", 1], parts["lo", 0], parts["lo", 1]],
        axis=1,
    ).astype(high)
    return fit, expand


def turn_trig(turns):
    quarter = jnp.floor(turns * 4.0 + 0.5)
    angle = (turns - 0.25 * quarter) * (2.0 * math.pi)
    square = angle * angle
    sine = angle * (
        1.0
        + square
        * (-1.0 / 6 + square * (1.0 / 120 + square * (-1.0 / 5040 + square * (1.0 / 362880))))
    )
    cosine = 1.0 + square * (
        -0.5
        + square
        * (1.0 / 24 + square * (-1.0 / 720 + square * (1.0 / 40320 + square * (-1.0 / 3628800))))
    )
    phase = quarter - 4.0 * jnp.floor(quarter * 0.25)
    odd = (phase == 1.0) | (phase == 3.0)
    cos_out = jnp.where(odd, sine, cosine)
    sin_out = jnp.where(odd, cosine, sine)
    cos_out = jnp.where((phase == 1.0) | (phase == 2.0), -cos_out, cos_out)
    sin_out = jnp.where(phase >= 2.0, -sin_out, sin_out)
    return cos_out, sin_out


def pack_kernel(wide, base, source, centre, target):
    chan = centre.shape[0]
    row = lax.broadcasted_iota(jnp.int32, (2 * chan, LANES), 0)
    lane = lax.broadcasted_iota(jnp.int32, (2 * chan, LANES), 1)
    value = jnp.zeros(row.shape, F32)
    for c in range(chan):
        value = jnp.where(row == c, centre[c], value)
    high = value.astype(BF16).astype(F32)
    middle = (value - high).astype(BF16).astype(F32)
    low = value - high - middle
    tail = jnp.where(lane == 0, high, jnp.where(lane == 1, middle, jnp.where(lane == 2, low, 0.0)))
    tail = tail.astype(BF16)
    for peer in range(wide):
        target[peer, :, 0:base] = source[:, peer * base : (peer + 1) * base]
        target[peer, :, base : base + LANES] = tail


def predict_kernel(
    groups,
    tiles,
    padded,
    order,
    xy,
    lm,
    flux,
    model,
    pos_x,
    pos_y,
    row_c,
    row_s,
    row_dc,
    row_ds,
    col_c,
    col_s,
    col_dc,
    col_ds,
    left_a,
    right_a,
    left_b,
    right_b,
):
    comps = lm.shape[1]
    rank = lax.axis_index("wide")
    first_row = rank * (2 * tiles)
    last_row = first_row + (2 * tiles - 1)
    col_a = row_groups_of(first_row, groups)[1] * GROUP
    col_b = row_groups_of(last_row, groups)[1] * GROUP
    edge = jnp.minimum((((first_row >> 6) + 1) * GROUP - first_row) >> 1, tiles)
    pos_x[...] = jnp.zeros_like(pos_x)
    pos_y[...] = jnp.zeros_like(pos_y)

    def place(slot, position):
        station = order[position]
        pos_x[pl.ds(slot, 1), :] = jnp.full((1, LANES), xy[0, station], F32)
        pos_y[pl.ds(slot, 1), :] = jnp.full((1, LANES), xy[1, station], F32)

    def place_row(t, carry):
        for half in range(2):
            row = first_row + 2 * t + half
            place(half * padded + t, row_groups_of(row, groups)[0] * GROUP + (row & 63))
        return carry

    def place_col(j, carry):
        place(2 * padded + j, col_a + j)
        place(2 * padded + GROUP + j, col_b + j)
        return carry

    lax.fori_loop(0, tiles, place_row, 0, unroll=2)
    lax.fori_loop(0, GROUP, place_col, 0, unroll=4)
    step = 0.25 / FREQ_CHANNELS
    rows = 2 * padded
    weight = flux[...] * (1.0 / math.sqrt(comps))
    for k in range(0, comps, LANES):
        lane = slice(k, k + LANES)
        axis_l = lm[0:1, lane]
        axis_m = lm[1:2, lane]
        turns = pos_x[0:rows, :] * axis_l + pos_y[0:rows, :] * axis_m
        cosine, sine = turn_trig(turns)
        row_c[:, lane] = cosine * weight[:, lane]
        row_s[:, lane] = sine * weight[:, lane]
        row_dc[:, lane], row_ds[:, lane] = turn_trig(turns * step)
        turns = (
            pos_x[rows : rows + LANES, :] * axis_l + pos_y[rows : rows + LANES, :] * axis_m
        ).T
        col_c[lane, :], col_s[lane, :] = turn_trig(turns)
        col_dc[lane, :], col_ds[lane, :] = turn_trig(turns * step)

    def fill(left, right):
        for k in range(0, comps, 16):
            part = slice(k, k + 16)
            c, s, dc, ds = col_c[part, :], col_s[part, :], col_dc[part, :], col_ds[part, :]
            for u in range(UNROLL):
                right[u, part, :] = c.astype(BF16)
                right[u, comps + k : comps + k + 16, :] = s.astype(BF16)
                c, s = c * dc - s * ds, s * dc + c * ds
            col_c[part, :], col_s[part, :] = c, s
        for r in range(0, rows, 16):
            part = slice(r, r + 16)
            low = slice(rows + r, rows + r + 16)
            for k in range(0, comps, LANES):
                lane = slice(k, k + LANES)
                high = slice(comps + k, comps + k + LANES)
                c, s, dc, ds = row_c[part, lane], row_s[part, lane], row_dc[part, lane], row_ds[part, lane]
                for u in range(UNROLL):
                    c16, s16 = c.astype(BF16), s.astype(BF16)
                    left[u, part, lane] = c16
                    left[u, part, high] = s16
                    left[u, low, lane] = s16
                    left[u, low, high] = -c16
                    c, s = c * dc - s * ds, s * dc + c * ds
                row_c[part, lane], row_s[part, lane] = c, s

    lane_id = lax.broadcasted_iota(jnp.int32, (padded, LANES), 1)
    first_half = lane_id < GROUP
    in_a = lax.broadcasted_iota(jnp.int32, (padded, LANES), 0) < edge

    def multiply(left, right, group):
        for u in range(UNROLL):
            product = jnp.dot(left[u], right[u], preferred_element_type=F32)
            channel = group * UNROLL + u
            base = (channel >> 3) * 16 + (channel & 7)
            for side in range(2):
                even = product[side * rows : side * rows + padded]
                odd = product[side * rows + padded : side * rows + 2 * padded]
                even = jnp.where(in_a, even, pltpu.roll(even, GROUP, 1))
                odd = jnp.where(in_a, pltpu.roll(odd, GROUP, 1), odd)
                model[pl.ds(base + 8 * side, padded, stride=256), :] = jnp.where(
                    first_half, even, odd
                )

    fill(left_a, right_a)

    def two_groups(pair, carry):
        fill(left_b, right_b)
        multiply(left_a, right_a, 2 * pair)
        fill(left_a, right_a)
        multiply(left_b, right_b, 2 * pair + 1)
        return carry

    lax.fori_loop(0, FREQ_CHANNELS // (2 * UNROLL), two_groups, 0)


def coefficients(fit, block):
    raw = jnp.dot(fit, block, preferred_element_type=F32)
    return raw[0:16] + raw[16:32], raw[32:48] + raw[48:64]


def tile_weights(groups, tiles, first_row, t, kept):
    lane = lax.broadcasted_iota(jnp.int32, (1, LANES), 1)
    row = first_row + 2 * t
    first, second = row_groups_of(row, groups)
    inside = (row & 63) + (lane >> 6)
    usable = (first != second) | (inside < (lane & 63))
    mask = kept[pl.ds((first_row >> 1) + t, 1), :].astype(F32)
    return jnp.where(usable, mask, 0.0)


def stats_kernel(
    groups, tiles, observed, predicted, kept, counts, fit, stats, model, model_modes, data_modes, shift
):
    rank = lax.axis_index("wide")
    first_row = rank * (2 * tiles)
    mode = lax.broadcasted_iota(jnp.int32, (MODES, LANES), 0)
    tail = observed[:, :, tiles * LANES : (tiles + 1) * LANES].reshape(256, LANES).astype(F32)
    shift[...] = jnp.broadcast_to(jnp.sum(tail, axis=1, keepdims=True), (256, LANES))

    def one(t):
        data = observed[:, :, pl.ds(pl.multiple_of(t * LANES, LANES), LANES)].reshape(256, LANES)
        part = pl.ds(pl.multiple_of(t * 256, 256), 256)
        block = (predicted[part, :] + shift[...]).astype(BF16)
        model[part, :] = block
        data_parts = data.astype(F32).reshape(FREQ_CHANNELS // 8, 2, 8, LANES)
        mod_parts = block.astype(F32).reshape(FREQ_CHANNELS // 8, 2, 8, LANES)
        obs_re, obs_im = data_parts[:, 0], data_parts[:, 1]
        mod_re, mod_im = mod_parts[:, 0], mod_parts[:, 1]

        def total(terms):
            return jnp.sum(jnp.sum(terms, axis=0), axis=0, keepdims=True)

        cross_re = total(obs_re * mod_re + obs_im * mod_im)
        cross_im = total(obs_im * mod_re - obs_re * mod_im)
        power = total(mod_re * mod_re + mod_im * mod_im)
        v_re, v_im = coefficients(fit[...], data)
        m_re, m_im = coefficients(fit[...], block)
        part32 = pl.ds(pl.multiple_of(t * 32, 32), 32)
        data_modes[part32, :] = jnp.concatenate([v_re, v_im])
        model_modes[part32, :] = jnp.concatenate([m_re, m_im])
        inside = (mode < counts[pl.ds(t, 1), :]).astype(F32)
        vv = jnp.sum(inside * (v_re * v_re + v_im * v_im), axis=0, keepdims=True)
        vm_re = jnp.sum(inside * (v_re * m_re + v_im * m_im), axis=0, keepdims=True)
        vm_im = jnp.sum(inside * (v_im * m_re - v_re * m_im), axis=0, keepdims=True)
        mm = jnp.sum(inside * (m_re * m_re + m_im * m_im), axis=0, keepdims=True)
        weight = tile_weights(groups, tiles, first_row, t, kept)
        rows = jnp.concatenate(
            [cross_re, cross_im, vv, vm_re, vm_im, power, mm, jnp.zeros((1, LANES), F32)]
        )
        return rows * weight

    def two(pair, carry):
        stats[pl.ds(pl.multiple_of(pair * 16, 16), 16), :] = jnp.concatenate(
            [one(2 * pair), one(2 * pair + 1)]
        ).astype(BF16)
        return carry

    lax.fori_loop(0, tiles // 2, two, 0)


def split_rows(values):
    row = lax.broadcasted_iota(jnp.int32, (16, values[0].shape[1]), 0)
    out = jnp.zeros(row.shape, F32)
    for at, value in enumerate(values):
        high = value.astype(BF16).astype(F32)
        out = jnp.where(row == 2 * at, high, out)
        out = jnp.where(row == 2 * at + 1, value - high, out)
    return out.astype(BF16)


def solve_kernel(
    groups,
    tiles,
    wide,
    gathered,
    observed,
    model,
    model_modes,
    data_modes,
    kept,
    counts,
    order,
    expand,
    gains,
    residual,
    flat,
    upper,
    full,
    state,
    weights,
    row_gain_re,
    row_gain_im,
    col_gain_re,
    col_gain_im,
):
    stations = groups * GROUP
    rank = lax.axis_index("wide")
    first_row = rank * (2 * tiles)
    chunk = 8 * tiles
    for k in range(wide):
        flip = 0
        bit, distance = 1, wide // 2
        while distance:
            flip += distance if k & bit else 0
            bit, distance = bit * 2, distance // 2
        owner = rank ^ flip
        flat[pl.ds(pl.multiple_of(owner * chunk, 16), chunk), :] = gathered[k].astype(F32)
    halves = stations // LANES
    lane32 = lax.broadcasted_iota(jnp.int32, (32, LANES), 1) < GROUP
    block_id = {}
    for first in range(groups):
        for second in range(first, groups):
            block_id[first, second] = len(block_id)
    for stat in range(STATS):
        for first in range(groups):
            for half in range(halves):
                pair = []
                for side in range(2):
                    index = block_id.get((first, 2 * half + side))
                    pair.append(
                        jnp.zeros((32, LANES), F32)
                        if index is None
                        else flat[pl.ds(256 * index + stat, 32, stride=8), :]
                    )
                if block_id.get((first, 2 * half + 1)) is None:
                    continue
                even = jnp.where(lane32, pair[0], pltpu.roll(pair[1], GROUP, 1))
                odd = jnp.where(lane32, pltpu.roll(pair[0], GROUP, 1), pair[1])
                upper[half, pl.ds(GROUP * first, 32, stride=2), :] = even
                upper[half, pl.ds(GROUP * first + 1, 32, stride=2), :] = odd
        sign = -1.0 if stat in (1, 4) else 1.0
        for a in range(halves):
            rows_a = slice(LANES * a, LANES * (a + 1))
            for b in range(a, halves):
                rows_b = slice(LANES * b, LANES * (b + 1))
                block = upper[b, rows_a, :]
                turned = block.T * sign
                if a == b:
                    full[stat, rows_a, rows_a] = block + turned
                else:
                    full[stat, rows_a, rows_b] = block
                    full[stat, rows_b, rows_a] = turned

    def put_weights(part, chunk_rows, value):
        high = value.astype(BF16)
        low = (value - high.astype(F32)).astype(BF16)
        weights[chunk_rows, (2 * part) * stations : (2 * part + 1) * stations] = high
        weights[chunk_rows, (2 * part + 1) * stations : (2 * part + 2) * stations] = low

    gain_re = jnp.ones((1, stations), F32)
    gain_im = jnp.zeros((1, stations), F32)
    for round_id in range(ROUNDS):

        def build(step, carry):
            rows = pl.ds(pl.multiple_of(step * 16, 16), 16)
            cross_re, cross_im, power = full[0, rows, :], full[1, rows, :], full[5, rows, :]
            if round_id:
                vv, vm_re, vm_im, mm = (full[i, rows, :] for i in (2, 3, 4, 6))
                col_re = jnp.concatenate([col_gain_re[rows, round_id - 1, :]] * halves, axis=1)
                col_im = jnp.concatenate([col_gain_im[rows, round_id - 1, :]] * halves, axis=1)
                rest_re = 1.0 - (col_re * gain_re + col_im * gain_im)
                rest_im = -(col_im * gain_re - col_re * gain_im)
                if round_id == 1:
                    a_re, a_im = jnp.ones_like(rest_re), jnp.zeros_like(rest_re)
                    b_re, b_im = rest_re, rest_im
                else:
                    a_re, a_im, b_re, b_im = (state[i, rows, :] for i in range(4))
                    a_re, a_im = 1.0 + rest_re * a_re - rest_im * a_im, rest_re * a_im + rest_im * a_re
                    b_re, b_im = rest_re * b_re - rest_im * b_im, rest_re * b_im + rest_im * b_re
                if round_id + 1 < ROUNDS:
                    for i, value in enumerate((a_re, a_im, b_re, b_im)):
                        state[i, rows, :] = value
                turn_re = b_re - 1.0
                cross_re = cross_re + a_re * vv + turn_re * vm_re + b_im * vm_im
                cross_im = cross_im - a_im * vv + turn_re * vm_im - b_im * vm_re
                mix_re = a_re * b_re + a_im * b_im
                mix_im = a_im * b_re - a_re * b_im
                power = (
                    power
                    + (a_re * a_re + a_im * a_im) * vv
                    + (b_re * b_re + b_im * b_im - 1.0) * mm
                    + 2.0 * (mix_re * vm_re - mix_im * vm_im)
                )
            put_weights(0, rows, cross_re)
            put_weights(1, rows, cross_im)
            put_weights(2, rows, power)
            return carry

        lax.fori_loop(0, stations // 16, build, 0)
        for iteration in range(CAL_ITERS):
            left = split_rows([gain_re, gain_im, gain_re * gain_re + gain_im * gain_im])
            raw = jnp.dot(left, weights[...], preferred_element_type=F32)

            def product(vector, part):
                at = 2 * part * stations
                high = raw[2 * vector : 2 * vector + 1, at : at + stations]
                low = raw[2 * vector + 1 : 2 * vector + 2, at : at + stations]
                return high + low + raw[2 * vector : 2 * vector + 1, at + stations : at + 2 * stations]

            below = product(2, 2)
            next_re = (product(0, 0) + product(1, 1)) / below
            next_im = (product(1, 0) - product(0, 1)) / below
            if iteration % 2 == 1:
                next_re = 0.5 * (next_re + gain_re)
                next_im = 0.5 * (next_im + gain_im)
            gain_re, gain_im = next_re, next_im
        lane1 = lax.broadcasted_iota(jnp.int32, (1, LANES), 1) < GROUP
        for value, row_gain, col_gain in (
            (gain_re, row_gain_re, col_gain_re),
            (gain_im, row_gain_im, col_gain_im),
        ):
            for half in range(halves):
                part = value[:, LANES * half : LANES * (half + 1)]
                turned = pltpu.roll(jnp.broadcast_to(part, (8, LANES)), GROUP, 1)[0:1]
                row_gain[2 * half, round_id : round_id + 1, :] = jnp.where(lane1, part, turned)
                row_gain[2 * half + 1, round_id : round_id + 1, :] = jnp.where(lane1, turned, part)
                col_gain[LANES * half : LANES * (half + 1), round_id, :] = jnp.broadcast_to(
                    part, (LANES, LANES)
                ).T

    hot = (
        lax.broadcasted_iota(jnp.int32, (stations, stations), 0) == order[...]
    ).astype(BF16)
    pieces = []
    for value in (gain_re, gain_im):
        high = value.astype(BF16).astype(F32)
        middle = (value - high).astype(BF16).astype(F32)
        pieces += [high, middle, value - high - middle]
    row16 = lax.broadcasted_iota(jnp.int32, (16, stations), 0)
    left = jnp.zeros((16, stations), F32)
    for at, piece in enumerate(pieces):
        left = jnp.where(row16 == at, piece, left)
    spread = lax.dot_general(
        left.astype(BF16), hot, (((1,), (1,)), ((), ())), preferred_element_type=F32
    )
    gains[0:1, :] = spread[0:1] + spread[1:2] + spread[2:3]
    gains[1:2, :] = spread[3:4] + spread[4:5] + spread[5:6]

    mode = lax.broadcasted_iota(jnp.int32, (MODES, LANES), 0)
    lane8 = lax.broadcasted_iota(jnp.int32, (8, LANES), 1) < GROUP

    def tile(t, carry):
        row = first_row + 2 * t
        first, second = row_groups_of(row, groups)
        station = first * GROUP + (row & 63)
        p_re = jnp.where(lane8, col_gain_re[station], col_gain_re[station + 1])
        p_im = jnp.where(lane8, col_gain_im[station], col_gain_im[station + 1])
        q_re, q_im = row_gain_re[second], row_gain_im[second]
        prod_re = p_re * q_re + p_im * q_im
        prod_im = p_im * q_re - p_re * q_im
        a_re, a_im = jnp.zeros((1, LANES), F32), jnp.zeros((1, LANES), F32)
        b_re, b_im = jnp.ones((1, LANES), F32), jnp.zeros((1, LANES), F32)
        for round_id in range(ROUNDS - 1):
            rest_re = 1.0 - prod_re[round_id : round_id + 1]
            rest_im = -prod_im[round_id : round_id + 1]
            a_re, a_im = 1.0 + rest_re * a_re - rest_im * a_im, rest_re * a_im + rest_im * a_re
            b_re, b_im = rest_re * b_re - rest_im * b_im, rest_re * b_im + rest_im * b_re
        b_re = b_re - 1.0
        inside = (mode < counts[pl.ds(t, 1), :]).astype(F32)
        part32 = pl.ds(pl.multiple_of(t * 32, 32), 32)
        v_re, v_im = data_modes[part32, :][0:16], data_modes[part32, :][16:32]
        m_re, m_im = model_modes[part32, :][0:16], model_modes[part32, :][16:32]
        f_re = inside * (a_re * v_re - a_im * v_im + b_re * m_re - b_im * m_im)
        f_im = inside * (a_re * v_im + a_im * v_re + b_re * m_im + b_im * m_re)
        f_re16, f_im16 = f_re.astype(BF16), f_im.astype(BF16)
        stack = jnp.concatenate(
            [
                f_re16,
                (f_re - f_re16.astype(F32)).astype(BF16),
                f_im16,
                (f_im - f_im16.astype(F32)).astype(BF16),
                f_re16,
                f_im16,
            ]
        )
        fitted = jnp.dot(expand[...], stack, preferred_element_type=F32)
        current = model[pl.ds(pl.multiple_of(t * 256, 256), 256), :].astype(F32) + fitted
        current = current.reshape(FREQ_CHANNELS // 8, 2, 8, LANES)
        lanes = pl.ds(pl.multiple_of(t * LANES, LANES), LANES)
        data = (
            observed[:, :, lanes]
            .reshape(256, LANES)
            .astype(F32)
            .reshape(FREQ_CHANNELS // 8, 2, 8, LANES)
        )
        weight = tile_weights(groups, tiles, first_row, t, kept)
        last_re, last_im = prod_re[ROUNDS - 1 : ROUNDS], prod_im[ROUNDS - 1 : ROUNDS]
        mod_re, mod_im = current[:, 0], current[:, 1]
        left_re = weight * (data[:, 0] - (last_re * mod_re - last_im * mod_im))
        left_im = weight * (data[:, 1] - (last_re * mod_im + last_im * mod_re))
        residual[0, 0, :, lanes] = left_re.reshape(FREQ_CHANNELS, LANES).astype(BF16)
        residual[1, 0, :, lanes] = left_im.reshape(FREQ_CHANNELS, LANES).astype(BF16)
        return carry

    lax.fori_loop(0, tiles, tile, 0)


def call(kernel, out_shape, scratch, name, in_spaces, mib, flops=0, moved=0):
    return pl.pallas_call(
        kernel,
        out_shape=out_shape,
        in_specs=[pl.BlockSpec(memory_space=space) for space in in_spaces],
        out_specs=jax.tree.map(lambda _: pl.BlockSpec(memory_space=VMEM), out_shape),
        scratch_shapes=scratch,
        compiler_params=pltpu.CompilerParams(vmem_limit_bytes=mib << 20),
        cost_estimate=pl.CostEstimate(flops=flops, bytes_accessed=moved, transcendentals=0),
        name=name,
    )


def gather_stats(stats, wide):
    held = stats[None]
    distance = wide // 2
    while distance:
        other = lax.ppermute(held, "wide", [(i, i ^ distance) for i in range(wide)])
        held = jnp.concatenate([held, other])
        distance //= 2
    return held


def body(
    visibilities,
    kept_baseline_mask,
    fitted_mode_count,
    station_order,
    station_xy,
    comp_lm,
    comp_flux,
    centre_flux,
):
    wide = lax.axis_size("wide")
    local_chan = visibilities.shape[2]
    total = visibilities.shape[3]
    base = total // wide
    tiles = base // LANES
    padded = -(-tiles // 8) * 8
    stations = station_order.shape[0]
    groups = stations // GROUP
    comps = comp_lm.shape[1]
    rows = 2 * padded
    fit, expand = (jnp.asarray(table) for table in basis_tables())
    kept = kept_baseline_mask.reshape(total // LANES, LANES)
    counts = fitted_mode_count.reshape(tiles, LANES)

    packed = call(
        lambda *refs: pack_kernel(wide, base, *refs),
        jax.ShapeDtypeStruct((wide, 2 * local_chan, base + LANES), BF16),
        [],
        "pack",
        [VMEM, SMEM],
        16,
        moved=8 * local_chan * total,
    )(visibilities.reshape(2 * local_chan, total), centre_flux)
    observed = lax.all_to_all(packed, "wide", 0, 0, tiled=True)
    if local_chan != 8:
        pairs = 8 // local_chan
        observed = observed.reshape(wide // pairs, pairs, 2, local_chan, base + LANES)
        observed = observed.transpose(0, 2, 1, 3, 4).reshape(wide // pairs, 16, base + LANES)

    state_row = pltpu.VMEM((rows, comps), F32)
    state_col = pltpu.VMEM((comps, LANES), F32)
    left = pltpu.VMEM((UNROLL, 2 * rows, 2 * comps), BF16)
    right = pltpu.VMEM((UNROLL, 2 * comps, LANES), BF16)
    predicted = call(
        lambda *refs: predict_kernel(groups, tiles, padded, *refs),
        jax.ShapeDtypeStruct((padded * 256, LANES), F32),
        [pltpu.VMEM((rows + LANES, LANES), F32)] * 2
        + [state_row] * 4
        + [state_col] * 4
        + [left, right, left, right],
        "predict",
        [SMEM, SMEM, VMEM, VMEM],
        24,
        FREQ_CHANNELS * 2 * 2 * rows * 2 * comps * 256,
        padded * 256 * LANES * 4,
    )(station_order, station_xy.reshape(2, stations), comp_lm, comp_flux.reshape(1, comps))
    stats, model, model_modes, data_modes = call(
        lambda *refs: stats_kernel(groups, tiles, *refs),
        (
            jax.ShapeDtypeStruct((tiles * 8, LANES), BF16),
            jax.ShapeDtypeStruct((tiles * 256, LANES), BF16),
            jax.ShapeDtypeStruct((tiles * 32, LANES), F32),
            jax.ShapeDtypeStruct((tiles * 32, LANES), F32),
        ),
        [pltpu.VMEM((256, LANES), F32)],
        "stats",
        [VMEM] * 5,
        16,
        moved=tiles * 256 * LANES * 8,
    )(observed, predicted, kept, counts, fit)
    gathered = gather_stats(stats, wide)
    gains, residual = call(
        lambda *refs: solve_kernel(groups, tiles, wide, *refs),
        (
            jax.ShapeDtypeStruct((2, stations), F32),
            jax.ShapeDtypeStruct((2, 1, FREQ_CHANNELS, base), BF16),
        ),
        [
            pltpu.VMEM((wide * tiles * 8, LANES), F32),
            pltpu.VMEM((stations // LANES, stations, LANES), F32),
            pltpu.VMEM((STATS, stations, stations), F32),
            pltpu.VMEM((4, stations, stations), F32),
            pltpu.VMEM((stations, 6 * stations), BF16),
            pltpu.VMEM((groups, 8, LANES), F32),
            pltpu.VMEM((groups, 8, LANES), F32),
            pltpu.VMEM((stations, 8, LANES), F32),
            pltpu.VMEM((stations, 8, LANES), F32),
        ],
        "solve",
        [VMEM] * 9,
        32,
        moved=tiles * 256 * LANES * 6,
    )(
        gathered,
        observed,
        model,
        model_modes,
        data_modes,
        kept,
        counts,
        station_order.reshape(1, stations),
        expand,
    )
    return gains, residual


def solution(mesh):
    placed = (
        P(None, None, ("band", "wide"), None),
        P("band"),
        P("wide"),
        P(),
        P(),
        P(),
        P(),
        P(("band", "wide")),
    )
    return jax.shard_map(
        body,
        mesh=mesh,
        in_specs=placed,
        out_specs=(P(None, "band"), P(None, None, "band", "wide")),
        check_vma=False,
    )
```

time: 1030 us -> 76.6 us (0.07); the launches traced: 1010 us -> 76.3 us
  local copies, waits for them, and re-layouts: 449 us -> 5.63 us
  blocking collectives: 320 us -> 0 us
  waiting for transfers between devices: 107 us -> 13.6 us
  other arithmetic: 65.8 us -> 0.06 us
  Pallas kernels: 0 us -> 43.5 us
  matrix products: 29.8 us -> 0 us
  loops' own time: 14.6 us -> 0 us
    psum x9 -> x0, blocking collectives: 284 us -> none  [solve_gains(): station_terms = lax.psum(local_terms, 'wide')]
    unnamed x39 -> x28, local copies, waits for them, and re-layouts: 153 us -> 5.58 us
    all_to_all x3 -> x0, local copies, waits for them, and re-layouts: 115 us -> none  [send_gap(): lax.all_to_all(data_gap, 'wide', split_axis=3, concat_axis=2, tiled=True)]
    all_to_all x4 -> x1, waiting for transfers between devices: 107 us -> 0.01 us  [body(): observed = lax.all_to_all(packed, 'wide', 0, 0, tiled=True)]
    optimization_barrier x5 -> x0, local copies, waits for them, and re-layouts: 106 us -> none  [the longest x3 98.4 us: corrupted_gap(): return lax.optimization_barrier(data_gap.astype(jnp.bfloat16))]
    pallas_call x0 -> x4, Pallas kernels: none -> 43.5 us  [the longest x1 28.9 us: body(): call(lambda *refs: predict_kernel(groups, tiles, padded, *refs), jax.Shap...]
    gather x69 -> x0, local copies, waits for them, and re-layouts: 39.6 us -> none  [the longest x9 5.01 us: block_gains(): row_re = grouped[0][row_groups][:, :, None]]
    all_to_all x1 -> x0, blocking collectives: 35.9 us -> none  [send_gap(): lax.all_to_all(data_gap, 'wide', split_axis=3, concat_axis=2, tiled=True)]
  transfers between devices with their start and end apart: 4 -> 5, of which waited for: 4 -> 4; matrix products, arithmetic and copies ran while one was open for 0% -> 0% of each run, Pallas kernels for 0% -> 38%
where the time goes in v1:
time: 76.6 us; the launch traced here: 76.3 us
  Pallas kernels  43.5 us (57%)
  waiting for transfers between devices  13.6 us (18%)
  starting transfers between devices  12.7 us (17%)
  local copies, waits for them, and re-layouts  5.63 us (7%)
  between operations  0.81 us (1%)
    pallas_call x1, Pallas kernels, body(): call(lambda *refs: predict_kernel(groups, tiles, padded, *refs), jax.Shap...  28.9 us
    ppermute x4, waiting for transfers between devices, gather_stats(): other = lax.ppermute(held, 'wide', [(i, i ^ distance) for i in range(wide)])  13.6 us
    pallas_call x1, Pallas kernels, body(): call(lambda *refs: solve_kernel(groups, tiles, wide, *refs), (jax.ShapeDt...  10.3 us
    all_to_all x1, starting transfers between devices, body(): observed = lax.all_to_all(packed, 'wide', 0, 0, tiled=True)  7.53 us
    unnamed x28, local copies, waits for them, and re-layouts  5.58 us
    ppermute x4, starting transfers between devices, gather_stats(): other = lax.ppermute(held, 'wide', [(i, i ^ distance) for i in range(wide)])  5.18 us
    pallas_call x1, Pallas kernels, body(): call(lambda *refs: stats_kernel(groups, tiles, *refs), (jax.ShapeDtypeStr...  2.66 us
    pallas_call x1, Pallas kernels, body(): call(lambda *refs: pack_kernel(wide, base, *refs), jax.ShapeDtypeStruct((...  1.72 us
  transfers between devices with their start and end apart: 5, of which 4 were waited for; matrix products, arithmetic and copies ran while one was open for 0% of the time, Pallas kernels for 38%

profile of v1, /device:TPU:0, one launch (start us, length us, event | category | flops | bytes accessed | tf_op | source)
XLA Modules:
  0.0 76.3 jit_solution(8754863576316453086)
XLA Ops:
  0.6 1.3 %copy-done.2 = bf16[2,1,8,40960]{3,2,1,0:T(8,128)(2,1)S(1)} copy-done((bf16[2,1,8,40960]{3,2,1,0:T(8,128)(2,1)S(1)}, bf16[2,1,8,40960]{3,2,1,0:T(8,128)(2,1)}, u32[]{:S(2)}) %copy-start.2) | copy-done | bytes 1310744
  1.9 0.7 copy-done.8
  2.6 1.7 %pack.1 = bf16[16,16,2688]{2,1,0:T(8,128)(2,1)} custom-call(bf16[16,40960]{1,0:T(8,128)(2,1)S(1)} %bitcast.8, f32[8]{0:T(128)S(1)} %copy-done.8), custom_call_target="tpu_custom_call" | custom-call | bytes 2621440 | tf_op jit(solution)/shard_map/pack/pallas_call | solution.py:578
  4.3 7.5 %all-to-all-start = ((bf16[16,16,2688]{2,1,0:T(8,128)(2,1)}), bf16[16,16,2688]{2,1,0:T(8,128)(2,1)S(1)}, u32[]{:S(2)}, u32[]{:S(2)}) async-start(bf16[16,16,2688]{2,1,0:T(8,128)(2,1)} %pack.1), calls=%async_computation | async-start | bytes 2752512 | tf_op jit(solution)/shard_map/all_to_all | solution.py:587
  11.9 0.0 copy-done.7
  11.9 0.0 copy-done.9
  11.9 0.0 copy-start.3
  11.9 0.0 copy-start.5
  11.9 0.0 copy-start.6
  12.0 28.9 %predict.1.refs_1_ = f32[6144,128]{1,0:T(8,128)S(1)} custom-call(s32[256]{0:T(256)S(1)} %copy-done.7, f32[2,256]{1,0:T(2,128)S(1)} %bitcast.18, f32[2,512]{1,0:T(2,128)S(1)} %copy-done.9, f32[1,512]{1,0:T(1,128)S(1)} %bitcast.19), custom_call_target="tpu_custom_call" | custom-call | flops 6442450944 | bytes 3145728 | tf_op jit(solution)/shard_map/predict/pallas_call | solution.py:597
  40.8 1.6 %copy-done = f32[6144,128]{1,0:T(8,128)} copy-done((f32[6144,128]{1,0:T(8,128)}, f32[6144,128]{1,0:T(8,128)S(1)}, u32[]{:S(2)}) %copy-start) | copy-done | bytes 3145752
  42.5 0.0 all-to-all-done.refs_0_.refs_1_
  42.5 1.9 %copy-done.1 = f32[6144,128]{1,0:T(8,128)S(1)} copy-done((f32[6144,128]{1,0:T(8,128)S(1)}, f32[6144,128]{1,0:T(8,128)}, u32[]{:S(2)}) %copy-start.1) | copy-done | bytes 3145752
  44.4 2.7 %stats.1 = (bf16[160,128]{1,0:T(8,128)(2,1)S(1)}, bf16[5120,128]{1,0:T(8,128)(2,1)S(1)}, f32[640,128]{1,0:T(8,128)S(1)}, f32[640,128]{1,0:T(8,128)S(1)}) custom-call(bf16[16,16,2688]{2,1,0:T(8,128)(2,1)S(1)} %all-to-all-done.refs_0_.refs_1_, f32[6144,128]{1,0:T(8,128)S(1)} %copy-done.1, s32[320,128]{1,0:T(8,128)S(1)} %bitcast.9, s32[20,128]{1,0:T(8,128)S(1)} %bitcast.15, ...), custom_call_target="tpu_custom_call" | custom-call | bytes 5242880 | tf_op jit(solution)/shard_map/stats/pallas_call | solution.py:610
  47.0 0.0 copy-start.4
  47.1 4.5 %collective-permute-start = (bf16[1,160,128]{2,1,0:T(8,128)(2,1)S(1)}, bf16[1,160,128]{2,1,0:T(8,128)(2,1)S(1)}, u32[]{:S(2)}, u32[]{:S(2)}) collective-permute-start(bf16[1,160,128]{2,1,0:T(8,128)(2,1)S(1)} %bitcast.11), channel_id=1, source_target_pairs={{0,8},{1,9},{2,10},{3,11},{4,12},{5,13},{6,14},{7,15},{8,0},{9,1},... | collective-permute-start | bytes 122888 | tf_op jit(solution)/shard_map/ppermute | solution.py:548
  51.6 2.8 %collective-permute-done = bf16[1,160,128]{2,1,0:T(8,128)(2,1)S(1)} collective-permute-done((bf16[1,160,128]{2,1,0:T(8,128)(2,1)S(1)}, bf16[1,160,128]{2,1,0:T(8,128)(2,1)S(1)}, u32[]{:S(2)}, u32[]{:S(2)}) %collective-permute-start) | collective-permute-done | bytes 40992 | tf_op jit(solution)/shard_map/ppermute | solution.py:548
  54.4 0.3 collective-permute-start.1
  54.6 4.2 %collective-permute-done.1 = bf16[2,160,128]{2,1,0:T(8,128)(2,1)S(1)} collective-permute-done((bf16[2,160,128]{2,1,0:T(8,128)(2,1)S(1)}, bf16[2,160,128]{2,1,0:T(8,128)(2,1)S(1)}, u32[]{:S(2)}, u32[]{:S(2)}) %collective-permute-start.1) | collective-permute-done | bytes 81952 | tf_op jit(solution)/shard_map/ppermute | solution.py:548
  58.9 0.3 collective-permute-start.2
  59.2 5.0 %collective-permute-done.2 = bf16[4,160,128]{2,1,0:T(8,128)(2,1)S(1)} collective-permute-done((bf16[4,160,128]{2,1,0:T(8,128)(2,1)S(1)}, bf16[4,160,128]{2,1,0:T(8,128)(2,1)S(1)}, u32[]{:S(2)}, u32[]{:S(2)}) %collective-permute-start.2) | collective-permute-done | bytes 163872 | tf_op jit(solution)/shard_map/ppermute | solution.py:548
  64.3 0.1 collective-permute-start.3
  64.5 1.5 %collective-permute-done.3 = bf16[8,160,128]{2,1,0:T(8,128)(2,1)S(1)} collective-permute-done((bf16[8,160,128]{2,1,0:T(8,128)(2,1)S(1)}, bf16[8,160,128]{2,1,0:T(8,128)(2,1)S(1)}, u32[]{:S(2)}, u32[]{:S(2)}) %collective-permute-start.3) | collective-permute-done | bytes 327712 | tf_op jit(solution)/shard_map/ppermute | solution.py:548
  66.1 10.3 %solve.1 = (f32[2,256]{1,0:T(2,128)}, bf16[2,1,128,2560]{3,2,1,0:T(8,128)(2,1)}) custom-call(bf16[16,160,128]{2,1,0:T(8,128)(2,1)S(1)} %constant_dynamic-update-slice_fusion.refs_0_, bf16[16,16,2688]{2,1,0:T(8,128)(2,1)S(1)} %all-to-all-done.refs_0_.refs_1_, bf16[5120,128]{1,0:T(8,128)(2,1)S(1)} %get-tuple-element.7.refs_2_, ...), custom_call_target="tpu_custom_call" | custom-call | bytes 3932160 | tf_op jit(solution)/shard_map/solve/pallas_call | solution.py:625
  (22 shorter events, 0.2 us)
Async XLA Ops:
  0.6 1.3 %copy-start.2 = (bf16[2,1,8,40960]{3,2,1,0:T(8,128)(2,1)S(1)}, bf16[2,1,8,40960]{3,2,1,0:T(8,128)(2,1)}, u32[]{:S(2)}) copy-start(bf16[2,1,8,40960]{3,2,1,0:T(8,128)(2,1)} %param.10) | copy-start | bytes 3932164
  1.9 0.7 copy-start.8
  4.3 7.5 %copy-start.7 = (s32[256]{0:T(256)S(1)}, s32[256]{0:T(256)}, u32[]{:S(2)}) copy-start(s32[256]{0:T(256)} %refs_0_.1) | copy-start | bytes 3076
  4.3 7.6 %copy-start.9 = (f32[2,512]{1,0:T(2,128)S(1)}, f32[2,512]{1,0:T(2,128)}, u32[]{:S(2)}) copy-start(f32[2,512]{1,0:T(2,128)} %refs_2_.1) | copy-start | bytes 12292
  4.3 7.6 %copy-start.10 = (f32[1,2,256]{2,1,0:T(2,128)S(1)}, f32[1,2,256]{2,1,0:T(2,128)}, u32[]{:S(2)}) copy-start(f32[1,2,256]{2,1,0:T(2,128)} %param.14) | copy-start | bytes 6148
  4.3 7.6 %copy-start.11 = (f32[512]{0:T(512)S(1)}, f32[512]{0:T(512)}, u32[]{:S(2)}) copy-start(f32[512]{0:T(512)} %param.16) | copy-start | bytes 6148
  4.3 38.1 %all-to-all-start = ((bf16[16,16,2688]{2,1,0:T(8,128)(2,1)}), bf16[16,16,2688]{2,1,0:T(8,128)(2,1)S(1)}, u32[]{:S(2)}, u32[]{:S(2)}) async-start(bf16[16,16,2688]{2,1,0:T(8,128)(2,1)} %pack.1), calls=%async_computation | async-start | bytes 2752512 | tf_op jit(solution)/shard_map/all_to_all | solution.py:587
  11.9 30.6 %copy-start.3 = (s32[40960]{0:T(1024)S(1)}, s32[40960]{0:T(1024)}, u32[]{:S(2)}) copy-start(s32[40960]{0:T(1024)} %param.11) | copy-start | bytes 491524
  11.9 30.5 %copy-start.5 = (s32[2560]{0:T(1024)S(1)}, s32[2560]{0:T(1024)}, u32[]{:S(2)}) copy-start(s32[2560]{0:T(1024)} %param.12) | copy-start | bytes 30724
  11.9 30.5 %copy-start.6 = (bf16[64,256]{1,0:T(8,128)(2,1)S(1)}, bf16[64,256]{1,0:T(8,128)(2,1)}, u32[]{:S(2)}) copy-start(bf16[64,256]{1,0:T(8,128)(2,1)} %constant.4.clone.refs_4_) | copy-start | bytes 98308
  40.8 1.6 %copy-start = (f32[6144,128]{1,0:T(8,128)}, f32[6144,128]{1,0:T(8,128)S(1)}, u32[]{:S(2)}) copy-start(f32[6144,128]{1,0:T(8,128)S(1)} %predict.1.refs_1_) | copy-start | bytes 9437188
  42.5 1.9 %copy-start.1 = (f32[6144,128]{1,0:T(8,128)S(1)}, f32[6144,128]{1,0:T(8,128)}, u32[]{:S(2)}) copy-start(f32[6144,128]{1,0:T(8,128)} %copy-done) | copy-start | bytes 9437188
  47.0 19.0 %copy-start.4 = (bf16[256,96]{1,0:T(8,128)(2,1)S(1)}, bf16[256,96]{1,0:T(8,128)(2,1)}, u32[]{:S(2)}) copy-start(bf16[256,96]{1,0:T(8,128)(2,1)} %constant.5.clone.refs_8_) | copy-start | bytes 147460
  47.1 7.3 %collective-permute-start = (bf16[1,160,128]{2,1,0:T(8,128)(2,1)S(1)}, bf16[1,160,128]{2,1,0:T(8,128)(2,1)S(1)}, u32[]{:S(2)}, u32[]{:S(2)}) collective-permute-start(bf16[1,160,128]{2,1,0:T(8,128)(2,1)S(1)} %bitcast.11), channel_id=1, source_target_pairs={{0,8},{1,9},{2,10},{3,11},{4,12},{5,13},{6,14},{7,15},{8,0},{9,1},... | collective-permute-start | bytes 122888 | tf_op jit(solution)/shard_map/ppermute | solution.py:548
  54.4 4.5 %collective-permute-start.1 = (bf16[2,160,128]{2,1,0:T(8,128)(2,1)S(1)}, bf16[2,160,128]{2,1,0:T(8,128)(2,1)S(1)}, u32[]{:S(2)}, u32[]{:S(2)}) collective-permute-start(bf16[2,160,128]{2,1,0:T(8,128)(2,1)S(1)} %pad_maximum_fusion.2), channel_id=1, source_target_pairs={{0,4},{1,5},{2,6},{3,7},{4,0},{5,1},{6,2},{7,3},{8,12},{9,13},{10,... | collective-permute-start | bytes 245768 | tf_op jit(solution)/shard_map/ppermute | solution.py:548
  58.9 5.4 %collective-permute-start.2 = (bf16[4,160,128]{2,1,0:T(8,128)(2,1)S(1)}, bf16[4,160,128]{2,1,0:T(8,128)(2,1)S(1)}, u32[]{:S(2)}, u32[]{:S(2)}) collective-permute-start(bf16[4,160,128]{2,1,0:T(8,128)(2,1)S(1)} %pad_maximum_fusion.1), channel_id=1, source_target_pairs={{0,2},{1,3},{2,0},{3,1},{4,6},{5,7},{6,4},{7,5},{8,10},{9,11},{10,... | collective-permute-start | bytes 491528 | tf_op jit(solution)/shard_map/ppermute | solution.py:548
  64.3 1.7 %collective-permute-start.3 = (bf16[8,160,128]{2,1,0:T(8,128)(2,1)S(1)}, bf16[8,160,128]{2,1,0:T(8,128)(2,1)S(1)}, u32[]{:S(2)}, u32[]{:S(2)}) collective-permute-start(bf16[8,160,128]{2,1,0:T(8,128)(2,1)S(1)} %pad_maximum_fusion), channel_id=1, source_target_pairs={{0,1},{1,0},{2,3},{3,2},{4,5},{5,4},{6,7},{7,6},{8,9},{9,8},{10,11... | collective-permute-start | bytes 983048 | tf_op jit(solution)/shard_map/ppermute | solution.py:548

commit v2 on v1

--- a/solution.py
+++ b/solution.py
@@ -84,21 +84,44 @@
     return cos_out, sin_out
 
 
-def pack_kernel(wide, base, source, centre, target):
+def pack_kernel(wide, base, source, centre, target, held, tail, flux, in_sems, out_sems, flux_sem):
     chan = centre.shape[0]
+    bring = [
+        pltpu.make_async_copy(
+            source.at[:, pl.ds(peer * base, base)], held.at[peer], in_sems.at[peer]
+        )
+        for peer in range(wide)
+    ]
+    send = [
+        pltpu.make_async_copy(held.at[peer], target.at[peer, :, pl.ds(0, base)], out_sems.at[peer])
+        for peer in range(wide)
+    ]
+    send_tail = [
+        pltpu.make_async_copy(tail, target.at[peer, :, pl.ds(base, LANES)], out_sems.at[wide + peer])
+        for peer in range(wide)
+    ]
+    fetch = pltpu.make_async_copy(centre, flux, flux_sem)
+    fetch.start()
+    for copy in bring:
+        copy.start()
+    fetch.wait()
     row = lax.broadcasted_iota(jnp.int32, (2 * chan, LANES), 0)
     lane = lax.broadcasted_iota(jnp.int32, (2 * chan, LANES), 1)
     value = jnp.zeros(row.shape, F32)
     for c in range(chan):
-        value = jnp.where(row == c, centre[c], value)
+        value = jnp.where(row == c, flux[c], value)
     high = value.astype(BF16).astype(F32)
     middle = (value - high).astype(BF16).astype(F32)
     low = value - high - middle
-    tail = jnp.where(lane == 0, high, jnp.where(lane == 1, middle, jnp.where(lane == 2, low, 0.0)))
-    tail = tail.astype(BF16)
-    for peer in range(wide):
-        target[peer, :, 0:base] = source[:, peer * base : (peer + 1) * base]
-        target[peer, :, base : base + LANES] = tail
+    parts = jnp.where(lane == 0, high, jnp.where(lane == 1, middle, jnp.where(lane == 2, low, 0.0)))
+    tail[...] = parts.astype(BF16)
+    for copy in send_tail:
+        copy.start()
+    for came, copy in zip(bring, send):
+        came.wait()
+        copy.start()
+    for copy in send + send_tail:
+        copy.wait()
 
 
 def predict_kernel(
@@ -109,7 +132,10 @@
     xy,
     lm,
     flux,
-    model,
+    real_out,
+    imag_out,
+    real,
+    imag,
     pos_x,
     pos_y,
     row_c,
@@ -171,59 +197,69 @@
         col_c[lane, :], col_s[lane, :] = turn_trig(turns)
         col_dc[lane, :], col_ds[lane, :] = turn_trig(turns * step)
 
-    def fill(left, right):
-        for k in range(0, comps, 16):
-            part = slice(k, k + 16)
-            c, s, dc, ds = col_c[part, :], col_s[part, :], col_dc[part, :], col_ds[part, :]
-            for u in range(UNROLL):
-                right[u, part, :] = c.astype(BF16)
-                right[u, comps + k : comps + k + 16, :] = s.astype(BF16)
-                c, s = c * dc - s * ds, s * dc + c * ds
-            col_c[part, :], col_s[part, :] = c, s
-        for r in range(0, rows, 16):
-            part = slice(r, r + 16)
-            low = slice(rows + r, rows + r + 16)
-            for k in range(0, comps, LANES):
-                lane = slice(k, k + LANES)
-                high = slice(comps + k, comps + k + LANES)
-                c, s, dc, ds = row_c[part, lane], row_s[part, lane], row_dc[part, lane], row_ds[part, lane]
-                for u in range(UNROLL):
-                    c16, s16 = c.astype(BF16), s.astype(BF16)
-                    left[u, part, lane] = c16
-                    left[u, part, high] = s16
-                    left[u, low, lane] = s16
-                    left[u, low, high] = -c16
-                    c, s = c * dc - s * ds, s * dc + c * ds
-                row_c[part, lane], row_s[part, lane] = c, s
-
-    lane_id = lax.broadcasted_iota(jnp.int32, (padded, LANES), 1)
-    first_half = lane_id < GROUP
+    def fill_col(right, k):
+        part = slice(k, k + 16)
+        c, s, dc, ds = col_c[part, :], col_s[part, :], col_dc[part, :], col_ds[part, :]
+        for u in range(UNROLL):
+            right[u, part, :] = c.astype(BF16)
+            right[u, comps + k : comps + k + 16, :] = s.astype(BF16)
+            c, s = c * dc - s * ds, s * dc + c * ds
+        col_c[part, :], col_s[part, :] = c, s
+
+    def fill_row(left, r, k):
+        part, low = slice(r, r + 16), slice(rows + r, rows + r + 16)
+        lane, high = slice(k, k + LANES), slice(comps + k, comps + k + LANES)
+        c, s, dc, ds = row_c[part, lane], row_s[part, lane], row_dc[part, lane], row_ds[part, lane]
+        for u in range(UNROLL):
+            c16, s16 = c.astype(BF16), s.astype(BF16)
+            left[u, part, lane] = c16
+            left[u, part, high] = s16
+            left[u, low, lane] = s16
+            left[u, low, high] = -c16
+            c, s = c * dc - s * ds, s * dc + c * ds
+        row_c[part, lane], row_s[part, lane] = c, s
+
+    def fill_steps(left, right):
+        steps = [lambda k=k: fill_col(right, k) for k in range(0, comps, 16)]
+        return steps + [
+            lambda r=r, k=k: fill_row(left, r, k)
+            for r in range(0, rows, 16)
+            for k in range(0, comps, LANES)
+        ]
+
+    first_half = lax.broadcasted_iota(jnp.int32, (padded, LANES), 1) < GROUP
     in_a = lax.broadcasted_iota(jnp.int32, (padded, LANES), 0) < edge
 
-    def multiply(left, right, group):
+    def multiply(left, right, group, u):
+        product = jnp.dot(left[u], right[u], preferred_element_type=F32)
+        channel = group * UNROLL + u
+        for side, out in ((0, real), (1, imag)):
+            even = product[side * rows : side * rows + padded]
+            odd = product[side * rows + padded : side * rows + 2 * padded]
+            even = jnp.where(in_a, even, pltpu.roll(even, GROUP, 1))
+            odd = jnp.where(in_a, pltpu.roll(odd, GROUP, 1), odd)
+            out[pl.ds(channel, padded, stride=FREQ_CHANNELS), :] = jnp.where(first_half, even, odd)
+
+    for step in fill_steps(left_a, right_a):
+        step()
+
+    def group_pass(now, later, group):
+        steps = fill_steps(*later)
+        share = -(-len(steps) // UNROLL)
         for u in range(UNROLL):
-            product = jnp.dot(left[u], right[u], preferred_element_type=F32)
-            channel = group * UNROLL + u
-            base = (channel >> 3) * 16 + (channel & 7)
-            for side in range(2):
-                even = product[side * rows : side * rows + padded]
-                odd = product[side * rows + padded : side * rows + 2 * padded]
-                even = jnp.where(in_a, even, pltpu.roll(even, GROUP, 1))
-                odd = jnp.where(in_a, pltpu.roll(odd, GROUP, 1), odd)
-                model[pl.ds(base + 8 * side, padded, stride=256), :] = jnp.where(
-                    first_half, even, odd
-                )
-
-    fill(left_a, right_a)
+            multiply(*now, group, u)
+            for step in steps[u * share : (u + 1) * share]:
+                step()
 
     def two_groups(pair, carry):
-        fill(left_b, right_b)
-        multiply(left_a, right_a, 2 * pair)
-        fill(left_a, right_a)
-        multiply(left_b, right_b, 2 * pair + 1)
+        group_pass((left_a, right_a), (left_b, right_b), 2 * pair)
+        group_pass((left_b, right_b), (left_a, right_a), 2 * pair + 1)
         return carry
 
     lax.fori_loop(0, FREQ_CHANNELS // (2 * UNROLL), two_groups, 0)
+    size = tiles * FREQ_CHANNELS
+    real_out[...] = real[0:size, :]
+    imag_out[...] = imag[0:size, :].astype(BF16)
 
 
 def coefficients(fit, block):
@@ -242,18 +278,22 @@
 
 
 def stats_kernel(
-    groups, tiles, observed, predicted, kept, counts, fit, stats, model, model_modes, data_modes, shift
+    groups, tiles, observed, real, imag, kept, counts, fit, stats, model, model_modes, data_modes, shift
 ):
     rank = lax.axis_index("wide")
     first_row = rank * (2 * tiles)
     mode = lax.broadcasted_iota(jnp.int32, (MODES, LANES), 0)
     tail = observed[:, :, tiles * LANES : (tiles + 1) * LANES].reshape(256, LANES).astype(F32)
-    shift[...] = jnp.broadcast_to(jnp.sum(tail, axis=1, keepdims=True), (256, LANES))
+    tail = tail.reshape(FREQ_CHANNELS // 8, 2, 8, LANES)[:, 0].reshape(FREQ_CHANNELS, LANES)
+    shift[...] = jnp.broadcast_to(jnp.sum(tail, axis=1, keepdims=True), tail.shape)
 
     def one(t):
         data = observed[:, :, pl.ds(pl.multiple_of(t * LANES, LANES), LANES)].reshape(256, LANES)
         part = pl.ds(pl.multiple_of(t * 256, 256), 256)
-        block = (predicted[part, :] + shift[...]).astype(BF16)
+        half = pl.ds(pl.multiple_of(t * FREQ_CHANNELS, FREQ_CHANNELS), FREQ_CHANNELS)
+        sides = [real[half, :] + shift[...], imag[half, :].astype(F32)]
+        sides = [side.reshape(FREQ_CHANNELS // 8, 1, 8, LANES) for side in sides]
+        block = jnp.concatenate(sides, axis=1).reshape(256, LANES).astype(BF16)
         model[part, :] = block
         data_parts = data.astype(F32).reshape(FREQ_CHANNELS // 8, 2, 8, LANES)
         mod_parts = block.astype(F32).reshape(FREQ_CHANNELS // 8, 2, 8, LANES)
@@ -288,7 +328,7 @@
         ).astype(BF16)
         return carry
 
-    lax.fori_loop(0, tiles // 2, two, 0)
+    lax.fori_loop(0, tiles // 2, two, 0, unroll=5)
 
 
 def split_rows(values):
@@ -330,12 +370,7 @@
     rank = lax.axis_index("wide")
     first_row = rank * (2 * tiles)
     chunk = 8 * tiles
-    for k in range(wide):
-        flip = 0
-        bit, distance = 1, wide // 2
-        while distance:
-            flip += distance if k & bit else 0
-            bit, distance = bit * 2, distance // 2
+    for k, flip in enumerate(gather_order(wide)):
         owner = rank ^ flip
         flat[pl.ds(pl.multiple_of(owner * chunk, 16), chunk), :] = gathered[k].astype(F32)
     halves = stations // LANES
@@ -375,10 +410,7 @@
                     full[stat, rows_b, rows_a] = turned
 
     def put_weights(part, chunk_rows, value):
-        high = value.astype(BF16)
-        low = (value - high.astype(F32)).astype(BF16)
-        weights[chunk_rows, (2 * part) * stations : (2 * part + 1) * stations] = high
-        weights[chunk_rows, (2 * part + 1) * stations : (2 * part + 2) * stations] = low
+        weights[chunk_rows, part * stations : (part + 1) * stations] = value.astype(BF16)
 
     gain_re = jnp.ones((1, stations), F32)
     gain_im = jnp.zeros((1, stations), F32)
@@ -419,16 +451,14 @@
             put_weights(2, rows, power)
             return carry
 
-        lax.fori_loop(0, stations // 16, build, 0)
+        lax.fori_loop(0, stations // 16, build, 0, unroll=4)
         for iteration in range(CAL_ITERS):
             left = split_rows([gain_re, gain_im, gain_re * gain_re + gain_im * gain_im])
             raw = jnp.dot(left, weights[...], preferred_element_type=F32)
 
             def product(vector, part):
-                at = 2 * part * stations
-                high = raw[2 * vector : 2 * vector + 1, at : at + stations]
-                low = raw[2 * vector + 1 : 2 * vector + 2, at : at + stations]
-                return high + low + raw[2 * vector : 2 * vector + 1, at + stations : at + 2 * stations]
+                at = slice(part * stations, (part + 1) * stations)
+                return raw[2 * vector : 2 * vector + 1, at] + raw[2 * vector + 1 : 2 * vector + 2, at]
 
             below = product(2, 2)
             next_re = (product(0, 0) + product(1, 1)) / below
@@ -525,7 +555,7 @@
         residual[1, 0, :, lanes] = left_im.reshape(FREQ_CHANNELS, LANES).astype(BF16)
         return carry
 
-    lax.fori_loop(0, tiles, tile, 0)
+    lax.fori_loop(0, tiles, tile, 0, unroll=5)
 
 
 def call(kernel, out_shape, scratch, name, in_spaces, mib, flops=0, moved=0):
@@ -541,12 +571,24 @@
     )
 
 
+def exchange(block, distance, wide):
+    return lax.ppermute(block, "wide", [(i, i ^ distance) for i in range(wide)])
+
+
+def gather_order(wide):
+    order = [0, wide // 2, 3 * wide // 4, wide // 4]
+    distance = wide // 8
+    while distance:
+        order += [place ^ distance for place in order]
+        distance //= 2
+    return order
+
+
 def gather_stats(stats, wide):
-    held = stats[None]
-    distance = wide // 2
+    held = jnp.stack([stats] + [exchange(stats, flip, wide) for flip in gather_order(wide)[1:4]])
+    distance = wide // 8
     while distance:
-        other = lax.ppermute(held, "wide", [(i, i ^ distance) for i in range(wide)])
-        held = jnp.concatenate([held, other])
+        held = jnp.concatenate([held, exchange(held, distance, wide)])
         distance //= 2
     return held
 
@@ -575,14 +617,21 @@
     kept = kept_baseline_mask.reshape(total // LANES, LANES)
     counts = fitted_mode_count.reshape(tiles, LANES)
 
-    packed = call(
+    packed = pl.pallas_call(
         lambda *refs: pack_kernel(wide, base, *refs),
-        jax.ShapeDtypeStruct((wide, 2 * local_chan, base + LANES), BF16),
-        [],
-        "pack",
-        [VMEM, SMEM],
-        16,
-        moved=8 * local_chan * total,
+        out_shape=jax.ShapeDtypeStruct((wide, 2 * local_chan, base + LANES), BF16),
+        in_specs=[pl.BlockSpec(memory_space=pltpu.MemorySpace.HBM)] * 2,
+        out_specs=pl.BlockSpec(memory_space=pltpu.MemorySpace.HBM),
+        scratch_shapes=[
+            pltpu.VMEM((wide, 2 * local_chan, base), BF16),
+            pltpu.VMEM((2 * local_chan, LANES), BF16),
+            pltpu.SMEM((local_chan,), F32),
+            pltpu.SemaphoreType.DMA((wide,)),
+            pltpu.SemaphoreType.DMA((2 * wide,)),
+            pltpu.SemaphoreType.DMA,
+        ],
+        compiler_params=pltpu.CompilerParams(vmem_limit_bytes=60 << 20),
+        name="pack",
     )(visibilities.reshape(2 * local_chan, total), centre_flux)
     observed = lax.all_to_all(packed, "wide", 0, 0, tiled=True)
     if local_chan != 8:
@@ -594,16 +643,20 @@
     state_col = pltpu.VMEM((comps, LANES), F32)
     left = pltpu.VMEM((UNROLL, 2 * rows, 2 * comps), BF16)
     right = pltpu.VMEM((UNROLL, 2 * comps, LANES), BF16)
-    predicted = call(
+    real, imag = call(
         lambda *refs: predict_kernel(groups, tiles, padded, *refs),
-        jax.ShapeDtypeStruct((padded * 256, LANES), F32),
-        [pltpu.VMEM((rows + LANES, LANES), F32)] * 2
+        (
+            jax.ShapeDtypeStruct((tiles * FREQ_CHANNELS, LANES), F32),
+            jax.ShapeDtypeStruct((tiles * FREQ_CHANNELS, LANES), BF16),
+        ),
+        [pltpu.VMEM((padded * FREQ_CHANNELS, LANES), F32)] * 2
+        + [pltpu.VMEM((rows + LANES, LANES), F32)] * 2
         + [state_row] * 4
         + [state_col] * 4
         + [left, right, left, right],
         "predict",
         [SMEM, SMEM, VMEM, VMEM],
-        24,
+        20,
         FREQ_CHANNELS * 2 * 2 * rows * 2 * comps * 256,
         padded * 256 * LANES * 4,
     )(station_order, station_xy.reshape(2, stations), comp_lm, comp_flux.reshape(1, comps))
@@ -615,12 +668,12 @@
             jax.ShapeDtypeStruct((tiles * 32, LANES), F32),
             jax.ShapeDtypeStruct((tiles * 32, LANES), F32),
         ),
-        [pltpu.VMEM((256, LANES), F32)],
+        [pltpu.VMEM((FREQ_CHANNELS, LANES), F32)],
         "stats",
-        [VMEM] * 5,
-        16,
+        [VMEM] * 6,
+        12,
         moved=tiles * 256 * LANES * 8,
-    )(observed, predicted, kept, counts, fit)
+    )(observed, real, imag, kept, counts, fit)
     gathered = gather_stats(stats, wide)
     gains, residual = call(
         lambda *refs: solve_kernel(groups, tiles, wide, *refs),
@@ -633,7 +686,7 @@
             pltpu.VMEM((stations // LANES, stations, LANES), F32),
             pltpu.VMEM((STATS, stations, stations), F32),
             pltpu.VMEM((4, stations, stations), F32),
-            pltpu.VMEM((stations, 6 * stations), BF16),
+            pltpu.VMEM((stations, 3 * stations), BF16),
             pltpu.VMEM((groups, 8, LANES), F32),
             pltpu.VMEM((groups, 8, LANES), F32),
             pltpu.VMEM((stations, 8, LANES), F32),
@@ -641,7 +694,7 @@
         ],
         "solve",
         [VMEM] * 9,
-        32,
+        16,
         moved=tiles * 256 * LANES * 6,
     )(
         gathered,

time: 76.6 us -> 67.7 us (0.88)
  local copies, waits for them, and re-layouts: 5.63 us -> 2.23 us
  Pallas kernels: 43.5 us -> 40.2 us
  waiting for transfers between devices: 13.6 us -> 11.2 us
    unnamed x28 -> x20, local copies, waits for them, and re-layouts: 5.58 us -> 2.12 us
    pallas_call x1, Pallas kernels: 10.3 us -> 7.04 us  [body(): call(lambda *refs: solve_kernel(groups, tiles, wide, *refs), (jax.ShapeDt...]
    ppermute x4 -> x5, waiting for transfers between devices: 13.6 us -> 11.2 us  [exchange(): return lax.ppermute(block, 'wide', [(i, i ^ distance) for i in range(wide)])]
    pallas_call x1, Pallas kernels: 2.66 us -> 1.6 us  [body(): call(lambda *refs: stats_kernel(groups, tiles, *refs), (jax.ShapeDtypeStr...]
    pallas_call x2, Pallas kernels: 30.6 us -> 31.6 us  [the longest x1 29 us: body(): call(lambda *refs: predict_kernel(groups, tiles, padded, *refs), (jax.Sha...]
    ppermute x4 -> x5, starting transfers between devices: 5.18 us -> 5.56 us  [exchange(): return lax.ppermute(block, 'wide', [(i, i ^ distance) for i in range(wide)])]
  transfers between devices with their start and end apart: 5 -> 6, of which waited for: 4 -> 4; matrix products, arithmetic and copies ran while one was open for 0% -> 0% of each run, Pallas kernels for 38% -> 43%
where the time goes in v2:
time: 67.7 us; the launch traced here: 67.4 us
  Pallas kernels  40.2 us (59%)
  starting transfers between devices  13 us (19%)
  waiting for transfers between devices  11.2 us (17%)
  local copies, waits for them, and re-layouts  2.23 us (3%)
  between operations  0.77 us (1%)
    pallas_call x1, Pallas kernels, body(): call(lambda *refs: predict_kernel(groups, tiles, padded, *refs), (jax.Sha...  29 us
    ppermute x5, waiting for transfers between devices, exchange(): return lax.ppermute(block, 'wide', [(i, i ^ distance) for i in range(wide)])  11.2 us
    all_to_all x1, starting transfers between devices, body(): observed = lax.all_to_all(packed, 'wide', 0, 0, tiled=True)  7.4 us
    pallas_call x1, Pallas kernels, body(): call(lambda *refs: solve_kernel(groups, tiles, wide, *refs), (jax.ShapeDt...  7.04 us
    ppermute x5, starting transfers between devices, exchange(): return lax.ppermute(block, 'wide', [(i, i ^ distance) for i in range(wide)])  5.56 us
    pallas_call x1, Pallas kernels, body(): pl.pallas_call(lambda *refs: pack_kernel(wide, base, *refs), out_shape=ja...  2.53 us
    unnamed x20, local copies, waits for them, and re-layouts  2.12 us
    pallas_call x1, Pallas kernels, body(): call(lambda *refs: stats_kernel(groups, tiles, *refs), (jax.ShapeDtypeStr...  1.6 us
  transfers between devices with their start and end apart: 6, of which 4 were waited for; matrix products, arithmetic and copies ran while one was open for 0% of the time, Pallas kernels for 43%

profile of v2, /device:TPU:0, one launch (start us, length us, event | category | flops | bytes accessed | tf_op | source)
XLA Modules:
  0.0 67.4 jit_solution(3796650370116827771)
XLA Ops:
  0.6 2.5 %pack.1 = bf16[16,16,2688]{2,1,0:T(8,128)(2,1)} custom-call(bf16[16,40960]{1,0:T(8,128)(2,1)} %bitcast.26, f32[8]{0:T(128)} %refs_1_.1), custom_call_target="tpu_custom_call" | custom-call | tf_op jit(solution)/shard_map/pack/pallas_call | solution.py:620
  3.2 0.0 copy-start.4
  3.2 7.4 %all-to-all-start = ((bf16[16,16,2688]{2,1,0:T(8,128)(2,1)}), bf16[16,16,2688]{2,1,0:T(8,128)(2,1)S(1)}, u32[]{:S(2)}, u32[]{:S(2)}) async-start(bf16[16,16,2688]{2,1,0:T(8,128)(2,1)} %pack.1), calls=%async_computation | async-start | bytes 2752512 | tf_op jit(solution)/shard_map/all_to_all | solution.py:636
  10.6 0.0 copy-start.5
  10.6 0.7 %copy-done.5 = f32[2,512]{1,0:T(2,128)S(1)} copy-done((f32[2,512]{1,0:T(2,128)S(1)}, f32[2,512]{1,0:T(2,128)}, u32[]{:S(2)}) %copy-start.5) | copy-done | bytes 4120
  11.3 0.7 %copy-done.6 = f32[1,2,256]{2,1,0:T(2,128)S(1)} copy-done((f32[1,2,256]{2,1,0:T(2,128)S(1)}, f32[1,2,256]{2,1,0:T(2,128)}, u32[]{:S(2)}) %copy-start.6) | copy-done | bytes 2072
  12.0 0.7 %copy-done.7 = f32[512]{0:T(512)S(1)} copy-done((f32[512]{0:T(512)S(1)}, f32[512]{0:T(512)}, u32[]{:S(2)}) %copy-start.7) | copy-done | bytes 2072
  12.7 29.0 %predict.1 = (f32[2560,128]{1,0:T(8,128)S(1)}, bf16[2560,128]{1,0:T(8,128)(2,1)S(1)}) custom-call(s32[256]{0:T(256)S(1)} %copy-done.4, f32[2,256]{1,0:T(2,128)S(1)} %bitcast.24, f32[2,512]{1,0:T(2,128)S(1)} %copy-done.5, f32[1,512]{1,0:T(1,128)S(1)} %bitcast.25), custom_call_target="tpu_custom_call" | custom-call | flops 6442450944 | bytes 3145728 | tf_op jit(solution)/shard_map/predict/pallas_call | solution.py:646
  41.7 0.0 all-to-all-done.refs_0_.refs_1_
  41.7 0.0 copy-done
  41.7 1.6 %stats.1 = (bf16[160,128]{1,0:T(8,128)(2,1)S(1)}, bf16[5120,128]{1,0:T(8,128)(2,1)S(1)}, f32[640,128]{1,0:T(8,128)S(1)}, f32[640,128]{1,0:T(8,128)S(1)}) custom-call(bf16[16,16,2688]{2,1,0:T(8,128)(2,1)S(1)} %all-to-all-done.refs_0_.refs_1_, f32[2560,128]{1,0:T(8,128)S(1)} %get-tuple-element.8.refs_1_, bf16[2560,128]{1,0:T(8,128)(2,1)S(1)} %get-tuple-element.9.refs_2_, ...), custom_call_target="tpu_custom_call" | custom-call | bytes 5242880 | tf_op jit(solution)/shard_map/stats/pallas_call | solution.py:663
  43.4 0.0 copy-start.1
  43.4 3.9 %collective-permute-start = (bf16[160,128]{1,0:T(8,128)(2,1)S(1)}, bf16[160,128]{1,0:T(8,128)(2,1)S(1)}, u32[]{:S(2)}, u32[]{:S(2)}) collective-permute-start(bf16[160,128]{1,0:T(8,128)(2,1)S(1)} %get-tuple-element.10), channel_id=1, source_target_pairs={{0,8},{1,9},{2,10},{3,11},{4,12},{5,13},{6,14},{7,15},{8,0},{9,1},... | collective-permute-start | bytes 122888 | tf_op jit(solution)/shard_map/ppermute | solution.py:575
  47.3 0.4 collective-permute-start.1
  47.7 0.2 collective-permute-start.2
  48.0 2.5 %collective-permute-done = bf16[160,128]{1,0:T(8,128)(2,1)S(1)} collective-permute-done((bf16[160,128]{1,0:T(8,128)(2,1)S(1)}, bf16[160,128]{1,0:T(8,128)(2,1)S(1)}, u32[]{:S(2)}, u32[]{:S(2)}) %collective-permute-start) | collective-permute-done | bytes 40992 | tf_op jit(solution)/shard_map/ppermute | solution.py:575
  50.5 2.6 %collective-permute-done.1 = bf16[160,128]{1,0:T(8,128)(2,1)S(1)} collective-permute-done((bf16[160,128]{1,0:T(8,128)(2,1)S(1)}, bf16[160,128]{1,0:T(8,128)(2,1)S(1)}, u32[]{:S(2)}, u32[]{:S(2)}) %collective-permute-start.1) | collective-permute-done | bytes 40992 | tf_op jit(solution)/shard_map/ppermute | solution.py:575
  53.1 0.0 collective-permute-done.2
  53.1 0.9 %collective-permute-start.3 = (bf16[4,160,128]{2,1,0:T(8,128)(2,1)S(1)}, bf16[4,160,128]{2,1,0:T(8,128)(2,1)S(1)}, u32[]{:S(2)}, u32[]{:S(2)}) collective-permute-start(bf16[4,160,128]{2,1,0:T(8,128)(2,1)S(1)} %pad_maximum_fusion), channel_id=1, source_target_pairs={{0,2},{1,3},{2,0},{3,1},{4,6},{5,7},{6,4},{7,5},{8,10},{9,11},{10,... | collective-permute-start | bytes 491528 | tf_op jit(solution)/shard_map/ppermute | solution.py:575
  54.1 4.4 %collective-permute-done.3 = bf16[4,160,128]{2,1,0:T(8,128)(2,1)S(1)} collective-permute-done((bf16[4,160,128]{2,1,0:T(8,128)(2,1)S(1)}, bf16[4,160,128]{2,1,0:T(8,128)(2,1)S(1)}, u32[]{:S(2)}, u32[]{:S(2)}) %collective-permute-start.3) | collective-permute-done | bytes 163872 | tf_op jit(solution)/shard_map/ppermute | solution.py:575
  58.5 0.1 constant_dynamic-update-slice_fusion
  58.6 0.1 collective-permute-start.4
  58.7 1.6 %collective-permute-done.4 = bf16[8,160,128]{2,1,0:T(8,128)(2,1)S(1)} collective-permute-done((bf16[8,160,128]{2,1,0:T(8,128)(2,1)S(1)}, bf16[8,160,128]{2,1,0:T(8,128)(2,1)S(1)}, u32[]{:S(2)}, u32[]{:S(2)}) %collective-permute-start.4) | collective-permute-done | bytes 327712 | tf_op jit(solution)/shard_map/ppermute | solution.py:575
  60.3 7.0 %solve.1 = (f32[2,256]{1,0:T(2,128)}, bf16[2,1,128,2560]{3,2,1,0:T(8,128)(2,1)}) custom-call(bf16[16,160,128]{2,1,0:T(8,128)(2,1)S(1)} %constant_dynamic-update-slice_fusion.5.refs_0_, bf16[16,16,2688]{2,1,0:T(8,128)(2,1)S(1)} %all-to-all-done.refs_0_.refs_1_, bf16[5120,128]{1,0:T(8,128)(2,1)S(1)} %get-tuple-element.11.refs_2_, ...), custom_call_target="tpu_custom_call" | custom-call | bytes 3932160 | tf_op jit(solution)/shard_map/solve/pallas_call | solution.py:678
  (15 shorter events, 0.1 us)
Async XLA Ops:
  3.2 7.4 %copy-start.4 = (s32[256]{0:T(256)S(1)}, s32[256]{0:T(256)}, u32[]{:S(2)}) copy-start(s32[256]{0:T(256)} %refs_0_.1) | copy-start | bytes 3076
  3.2 38.5 %all-to-all-start = ((bf16[16,16,2688]{2,1,0:T(8,128)(2,1)}), bf16[16,16,2688]{2,1,0:T(8,128)(2,1)S(1)}, u32[]{:S(2)}, u32[]{:S(2)}) async-start(bf16[16,16,2688]{2,1,0:T(8,128)(2,1)} %pack.1), calls=%async_computation | async-start | bytes 2752512 | tf_op jit(solution)/shard_map/all_to_all | solution.py:636
  10.6 0.7 %copy-start.5 = (f32[2,512]{1,0:T(2,128)S(1)}, f32[2,512]{1,0:T(2,128)}, u32[]{:S(2)}) copy-start(f32[2,512]{1,0:T(2,128)} %refs_2_.1) | copy-start | bytes 12292
  11.3 0.7 %copy-start.6 = (f32[1,2,256]{2,1,0:T(2,128)S(1)}, f32[1,2,256]{2,1,0:T(2,128)}, u32[]{:S(2)}) copy-start(f32[1,2,256]{2,1,0:T(2,128)} %param.14) | copy-start | bytes 6148
  12.0 0.7 %copy-start.7 = (f32[512]{0:T(512)S(1)}, f32[512]{0:T(512)}, u32[]{:S(2)}) copy-start(f32[512]{0:T(512)} %param.16) | copy-start | bytes 6148
  12.6 29.1 %copy-start = (s32[40960]{0:T(1024)S(1)}, s32[40960]{0:T(1024)}, u32[]{:S(2)}) copy-start(s32[40960]{0:T(1024)} %param.11) | copy-start | bytes 491524
  12.7 29.1 %copy-start.2 = (s32[2560]{0:T(1024)S(1)}, s32[2560]{0:T(1024)}, u32[]{:S(2)}) copy-start(s32[2560]{0:T(1024)} %param.12) | copy-start | bytes 30724
  12.7 29.1 %copy-start.3 = (bf16[64,256]{1,0:T(8,128)(2,1)S(1)}, bf16[64,256]{1,0:T(8,128)(2,1)}, u32[]{:S(2)}) copy-start(bf16[64,256]{1,0:T(8,128)(2,1)} %constant.4.clone.refs_5_) | copy-start | bytes 98308
  43.4 17.0 %copy-start.1 = (bf16[256,96]{1,0:T(8,128)(2,1)S(1)}, bf16[256,96]{1,0:T(8,128)(2,1)}, u32[]{:S(2)}) copy-start(bf16[256,96]{1,0:T(8,128)(2,1)} %constant.5.clone.refs_8_) | copy-start | bytes 147460
  43.4 7.1 %collective-permute-start = (bf16[160,128]{1,0:T(8,128)(2,1)S(1)}, bf16[160,128]{1,0:T(8,128)(2,1)S(1)}, u32[]{:S(2)}, u32[]{:S(2)}) collective-permute-start(bf16[160,128]{1,0:T(8,128)(2,1)S(1)} %get-tuple-element.10), channel_id=1, source_target_pairs={{0,8},{1,9},{2,10},{3,11},{4,12},{5,13},{6,14},{7,15},{8,0},{9,1},... | collective-permute-start | bytes 122888 | tf_op jit(solution)/shard_map/ppermute | solution.py:575
  47.3 5.8 %collective-permute-start.1 = (bf16[160,128]{1,0:T(8,128)(2,1)S(1)}, bf16[160,128]{1,0:T(8,128)(2,1)S(1)}, u32[]{:S(2)}, u32[]{:S(2)}) collective-permute-start(bf16[160,128]{1,0:T(8,128)(2,1)S(1)} %get-tuple-element.10), channel_id=1, source_target_pairs={{0,12},{1,13},{2,14},{3,15},{4,8},{5,9},{6,10},{7,11},{8,4},{9,5},... | collective-permute-start | bytes 122888 | tf_op jit(solution)/shard_map/ppermute | solution.py:575
  47.7 5.4 %collective-permute-start.2 = (bf16[160,128]{1,0:T(8,128)(2,1)S(1)}, bf16[160,128]{1,0:T(8,128)(2,1)S(1)}, u32[]{:S(2)}, u32[]{:S(2)}) collective-permute-start(bf16[160,128]{1,0:T(8,128)(2,1)S(1)} %get-tuple-element.10), channel_id=1, source_target_pairs={{0,4},{1,5},{2,6},{3,7},{4,0},{5,1},{6,2},{7,3},{8,12},{9,13},{10,... | collective-permute-start | bytes 122888 | tf_op jit(solution)/shard_map/ppermute | solution.py:575
  53.1 5.4 %collective-permute-start.3 = (bf16[4,160,128]{2,1,0:T(8,128)(2,1)S(1)}, bf16[4,160,128]{2,1,0:T(8,128)(2,1)S(1)}, u32[]{:S(2)}, u32[]{:S(2)}) collective-permute-start(bf16[4,160,128]{2,1,0:T(8,128)(2,1)S(1)} %pad_maximum_fusion), channel_id=1, source_target_pairs={{0,2},{1,3},{2,0},{3,1},{4,6},{5,7},{6,4},{7,5},{8,10},{9,11},{10,... | collective-permute-start | bytes 491528 | tf_op jit(solution)/shard_map/ppermute | solution.py:575
  58.6 1.7 %collective-permute-start.4 = (bf16[8,160,128]{2,1,0:T(8,128)(2,1)S(1)}, bf16[8,160,128]{2,1,0:T(8,128)(2,1)S(1)}, u32[]{:S(2)}, u32[]{:S(2)}) collective-permute-start(bf16[8,160,128]{2,1,0:T(8,128)(2,1)S(1)} %get-tuple-element.14), channel_id=1, source_target_pairs={{0,1},{1,0},{2,3},{3,2},{4,5},{5,4},{6,7},{7,6},{8,9},{9,8},{10,11... | collective-permute-start | bytes 983048 | tf_op jit(solution)/shard_map/ppermute | solution.py:575

commit v3 on v2

v3 whole, which is shorter than its diff:
```python
import math

import jax
import jax.numpy as jnp
import numpy as np
from jax import lax
from jax.experimental import pallas as pl
from jax.experimental.pallas import tpu as pltpu
from jax.sharding import PartitionSpec as P

GROUP = 64
FREQ_CHANNELS = 128
MODES = 16
CAL_ITERS = 3
ROUNDS = 3
STATS = 7
LANES = 128
UNROLL = 4
PACK_PARTS = 4
VMEM = pltpu.MemorySpace.VMEM
SMEM = pltpu.MemorySpace.SMEM
F32 = jnp.float32
BF16 = jnp.bfloat16


def row_groups_of(row, groups):
    block = row >> 6
    first = jnp.zeros_like(block)
    start = jnp.zeros_like(block)
    edge = 0
    for group in range(1, groups):
        edge += groups - group + 1
        past = (block >= edge).astype(jnp.int32)
        first = first + past
        start = start + past * (groups - group + 1)
    return first, block - start + first


def basis_tables():
    mid = np.arange(FREQ_CHANNELS)[:, None] + 0.5
    order = np.arange(MODES)[None, :]
    scale = np.where(order == 0, math.sqrt(1.0 / FREQ_CHANNELS), math.sqrt(2.0 / FREQ_CHANNELS))
    basis = (scale * np.cos(math.pi / FREQ_CHANNELS * mid * order)).astype(np.float32)
    high = basis.astype(BF16)
    low = (basis - high.astype(np.float32)).astype(BF16)
    return np.concatenate([high, low], axis=1).T, np.concatenate([high, high, low], axis=1)


def output_parts(tiles):
    return 4 if tiles % 4 == 0 else 2


def stat_groups(tiles):
    return -(-tiles * STATS // 8)


def turn_trig(turns):
    quarter = jnp.floor(turns * 4.0 + 0.5)
    angle = (turns - 0.25 * quarter) * (2.0 * math.pi)
    square = angle * angle
    sine = angle * (
        1.0
        + square
        * (-1.0 / 6 + square * (1.0 / 120 + square * (-1.0 / 5040 + square * (1.0 / 362880))))
    )
    cosine = 1.0 + square * (
        -0.5
        + square
        * (1.0 / 24 + square * (-1.0 / 720 + square * (1.0 / 40320 + square * (-1.0 / 3628800))))
    )
    phase = quarter - 4.0 * jnp.floor(quarter * 0.25)
    odd = (phase == 1.0) | (phase == 3.0)
    cos_out = jnp.where(odd, sine, cosine)
    sin_out = jnp.where(odd, cosine, sine)
    cos_out = jnp.where((phase == 1.0) | (phase == 2.0), -cos_out, cos_out)
    sin_out = jnp.where(phase >= 2.0, -sin_out, sin_out)
    return cos_out, sin_out


def pack_kernel(wide, base, source, centre, target, held, flux, in_sems, out_sems, flux_sem):
    chan = centre.shape[0]
    share = wide // PACK_PARTS
    peers = [pl.ds(part * share, share) for part in range(PACK_PARTS)]
    bring = [
        [
            pltpu.make_async_copy(
                source.at[side, peers[part]],
                held.at[peers[part], :, pl.ds(side * base, base)],
                in_sems.at[part, side],
            )
            for side in range(2)
        ]
        for part in range(PACK_PARTS)
    ]
    send = [
        pltpu.make_async_copy(held.at[peers[part]], target.at[peers[part]], out_sems.at[part])
        for part in range(PACK_PARTS)
    ]
    fetch = pltpu.make_async_copy(centre, flux, flux_sem)
    fetch.start()
    for pair in bring:
        for copy in pair:
            copy.start()
    fetch.wait()
    row = lax.broadcasted_iota(jnp.int32, (chan, LANES), 0)
    lane = lax.broadcasted_iota(jnp.int32, (chan, LANES), 1)
    value = jnp.zeros(row.shape, F32)
    for c in range(chan):
        value = jnp.where(row == c, flux[c], value)
    high = value.astype(BF16).astype(F32)
    middle = (value - high).astype(BF16).astype(F32)
    low = value - high - middle
    parts = jnp.where(lane == 0, high, jnp.where(lane == 1, middle, jnp.where(lane == 2, low, 0.0)))
    held[:, :, 2 * base : 2 * base + LANES] = jnp.broadcast_to(
        parts.astype(BF16)[None], (wide, chan, LANES)
    )
    for pair, copy in zip(bring, send):
        for came in pair:
            came.wait()
        copy.start()
    for copy in send:
        copy.wait()


def predict_kernel(
    groups,
    tiles,
    padded,
    order,
    xy,
    lm,
    flux,
    real_out,
    imag_out,
    real,
    imag,
    pos_x,
    pos_y,
    row_c,
    row_s,
    row_dc,
    row_ds,
    col_c,
    col_s,
    col_dc,
    col_ds,
    left_a,
    right_a,
    left_b,
    right_b,
):
    comps = lm.shape[1]
    rank = lax.axis_index("wide")
    first_row = rank * (2 * tiles)
    last_row = first_row + (2 * tiles - 1)
    col_a = row_groups_of(first_row, groups)[1] * GROUP
    col_b = row_groups_of(last_row, groups)[1] * GROUP
    edge = jnp.minimum((((first_row >> 6) + 1) * GROUP - first_row) >> 1, tiles)
    pos_x[...] = jnp.zeros_like(pos_x)
    pos_y[...] = jnp.zeros_like(pos_y)

    def place(slot, position):
        station = order[position]
        pos_x[pl.ds(slot, 1), :] = jnp.full((1, LANES), xy[0, station], F32)
        pos_y[pl.ds(slot, 1), :] = jnp.full((1, LANES), xy[1, station], F32)

    def place_row(t, carry):
        for half in range(2):
            row = first_row + 2 * t + half
            place(half * padded + t, row_groups_of(row, groups)[0] * GROUP + (row & 63))
        return carry

    def place_col(j, carry):
        place(2 * padded + j, col_a + j)
        place(2 * padded + GROUP + j, col_b + j)
        return carry

    lax.fori_loop(0, tiles, place_row, 0, unroll=2)
    lax.fori_loop(0, GROUP, place_col, 0, unroll=4)
    step = 0.25 / FREQ_CHANNELS
    rows = 2 * padded
    weight = flux[...] * (1.0 / math.sqrt(comps))
    for k in range(0, comps, LANES):
        lane = slice(k, k + LANES)
        axis_l = lm[0:1, lane]
        axis_m = lm[1:2, lane]
        turns = pos_x[0:rows, :] * axis_l + pos_y[0:rows, :] * axis_m
        cosine, sine = turn_trig(turns)
        row_c[:, lane] = cosine * weight[:, lane]
        row_s[:, lane] = sine * weight[:, lane]
        row_dc[:, lane], row_ds[:, lane] = turn_trig(turns * step)
        turns = (
            pos_x[rows : rows + LANES, :] * axis_l + pos_y[rows : rows + LANES, :] * axis_m
        ).T
        col_c[lane, :], col_s[lane, :] = turn_trig(turns)
        col_dc[lane, :], col_ds[lane, :] = turn_trig(turns * step)

    def fill_col(right, k):
        part = slice(k, k + 16)
        c, s, dc, ds = col_c[part, :], col_s[part, :], col_dc[part, :], col_ds[part, :]
        for u in range(UNROLL):
            right[u, part, 0:LANES] = c.astype(BF16)
            right[u, part, LANES : 2 * LANES] = s.astype(BF16)
            c, s = c * dc - s * ds, s * dc + c * ds
        col_c[part, :], col_s[part, :] = c, s

    def fill_row(left, r, k):
        part, low = slice(r, r + 16), slice(rows + r, rows + r + 16)
        lane = slice(k, k + LANES)
        c, s, dc, ds = row_c[part, lane], row_s[part, lane], row_dc[part, lane], row_ds[part, lane]
        for u in range(UNROLL):
            left[u, part, lane] = c.astype(BF16)
            left[u, low, lane] = s.astype(BF16)
            c, s = c * dc - s * ds, s * dc + c * ds
        row_c[part, lane], row_s[part, lane] = c, s

    def fill_steps(left, right):
        steps = [lambda k=k: fill_col(right, k) for k in range(0, comps, 16)]
        return steps + [
            lambda r=r, k=k: fill_row(left, r, k)
            for r in range(0, rows, 16)
            for k in range(0, comps, LANES)
        ]

    first_half = lax.broadcasted_iota(jnp.int32, (padded, LANES), 1) < GROUP
    in_a = lax.broadcasted_iota(jnp.int32, (padded, LANES), 0) < edge

    def multiply(left, right, group, u):
        product = jnp.dot(left[u], right[u], preferred_element_type=F32)
        channel = group * UNROLL + u
        with_cos, with_sin = product[:, 0:LANES], product[:, LANES : 2 * LANES]
        sums = (
            (with_cos[0:rows] + with_sin[rows : 2 * rows], real),
            (with_cos[rows : 2 * rows] - with_sin[0:rows], imag),
        )
        for side, out in sums:
            even, odd = side[0:padded], side[padded : 2 * padded]
            even = jnp.where(in_a, even, pltpu.roll(even, GROUP, 1))
            odd = jnp.where(in_a, pltpu.roll(odd, GROUP, 1), odd)
            out[pl.ds(channel, padded, stride=FREQ_CHANNELS), :] = jnp.where(first_half, even, odd)

    for step in fill_steps(left_a, right_a):
        step()

    def group_pass(now, later, group):
        steps = fill_steps(*later)
        share = -(-len(steps) // UNROLL)
        for u in range(UNROLL):
            multiply(*now, group, u)
            for step in steps[u * share : (u + 1) * share]:
                step()

    def two_groups(pair, carry):
        group_pass((left_a, right_a), (left_b, right_b), 2 * pair)
        group_pass((left_b, right_b), (left_a, right_a), 2 * pair + 1)
        return carry

    lax.fori_loop(0, FREQ_CHANNELS // (2 * UNROLL), two_groups, 0)
    size = tiles * FREQ_CHANNELS
    real_out[...] = real[0:size, :]
    imag_out[...] = imag[0:size, :].astype(BF16)


def tile_weights(groups, tiles, first_row, t, kept):
    lane = lax.broadcasted_iota(jnp.int32, (1, LANES), 1)
    row = first_row + 2 * t
    first, second = row_groups_of(row, groups)
    inside = (row & 63) + (lane >> 6)
    usable = (first != second) | (inside < (lane & 63))
    mask = kept[pl.ds((first_row >> 1) + t, 1), :].astype(F32)
    return jnp.where(usable, mask, 0.0)


def tile_lanes(t, size=LANES, offset=0):
    return pl.ds(pl.multiple_of(offset + t * size, size), size)


def data_sides(observed, tiles, t):
    return [
        observed[:, :, tile_lanes(t, LANES, side * tiles * LANES)]
        .astype(F32)
        .reshape(FREQ_CHANNELS, LANES)
        for side in range(2)
    ]


def stats_kernel(
    groups, tiles, observed, real, imag, kept, counts, fit, stats, model, modes, shift, rows
):
    rank = lax.axis_index("wide")
    first_row = rank * (2 * tiles)
    mode = lax.broadcasted_iota(jnp.int32, (MODES, LANES), 0)
    tail = observed[:, :, 2 * tiles * LANES : (2 * tiles + 1) * LANES].astype(F32)
    tail = tail.reshape(FREQ_CHANNELS, LANES)
    shift[...] = jnp.broadcast_to(jnp.sum(tail, axis=1, keepdims=True), tail.shape)

    def one(t, carry):
        obs_re, obs_im = data_sides(observed, tiles, t)
        half = tile_lanes(t, FREQ_CHANNELS)
        mod_re16, mod_im16 = (real[half, :] + shift[...]).astype(BF16), imag[half, :]
        both = pl.multiple_of(2 * t * FREQ_CHANNELS, FREQ_CHANNELS)
        model[pl.ds(both, FREQ_CHANNELS), :] = mod_re16
        model[pl.ds(both + FREQ_CHANNELS, FREQ_CHANNELS), :] = mod_im16
        mod_re, mod_im = mod_re16.astype(F32), mod_im16.astype(F32)

        def total(terms):
            return jnp.sum(terms, axis=0, keepdims=True)

        cross_re = total(obs_re * mod_re + obs_im * mod_im)
        cross_im = total(obs_im * mod_re - obs_re * mod_im)
        power = total(mod_re * mod_re + mod_im * mod_im)
        sides = [obs_re.astype(BF16), obs_im.astype(BF16), mod_re16, mod_im16]
        raw = jnp.dot(fit[...], jnp.concatenate(sides, axis=1), preferred_element_type=F32)
        raw = raw[0:MODES] + raw[MODES : 2 * MODES]
        modes[tile_lanes(t, MODES), :] = raw
        v_re, v_im, m_re, m_im = (raw[:, LANES * i : LANES * (i + 1)] for i in range(4))
        inside = (mode < counts[pl.ds(t, 1), :]).astype(F32)
        vv = total(inside * (v_re * v_re + v_im * v_im))
        vm_re = total(inside * (v_re * m_re + v_im * m_im))
        vm_im = total(inside * (v_im * m_re - v_re * m_im))
        mm = total(inside * (m_re * m_re + m_im * m_im))
        weight = tile_weights(groups, tiles, first_row, t, kept)
        parts = [cross_re, cross_im, vv, vm_re, vm_im, power, mm, jnp.zeros((1, LANES), F32)]
        rows[tile_lanes(t, 8), :] = jnp.concatenate(parts) * weight
        return carry

    lax.fori_loop(0, tiles, one, 0, unroll=10)
    held = stat_groups(tiles)
    for extra in range(tiles - held):
        late = 8 * (held + extra)
        rows[pl.ds(7 + 8 * STATS * extra, STATS, stride=8), :] = rows[late : late + STATS, :]
    stats[...] = rows[0 : 8 * held, :].astype(BF16)


def solve_kernel(
    groups,
    tiles,
    wide,
    gathered,
    observed,
    model,
    modes,
    kept,
    counts,
    order,
    expand,
    gains,
    residual,
    flat,
    upper,
    full,
    weights,
    row_gain_re,
    row_gain_im,
    col_gain_re,
    col_gain_im,
    left_out,
    out_sems,
):
    stations = groups * GROUP
    rank = lax.axis_index("wide")
    first_row = rank * (2 * tiles)
    chunk = 8 * tiles
    held = stat_groups(tiles)
    for k, flip in enumerate(gather_order(wide)):
        start = pl.multiple_of((rank ^ flip) * chunk, 16)
        flat[pl.ds(start, 8 * held), :] = gathered[k].astype(F32)
        for extra in range(tiles - held):
            late = flat[pl.ds(start + (7 + 8 * STATS * extra), STATS, stride=8), :]
            flat[pl.ds(pl.multiple_of(start + 8 * (held + extra), 8), STATS), :] = late
    halves = stations // LANES
    lane32 = lax.broadcasted_iota(jnp.int32, (32, LANES), 1) < GROUP
    block_id = {}
    for first in range(groups):
        for second in range(first, groups):
            block_id[first, second] = len(block_id)
    for stat in range(STATS):
        for first in range(groups):
            for half in range(halves):
                pair = []
                for side in range(2):
                    index = block_id.get((first, 2 * half + side))
                    pair.append(
                        jnp.zeros((32, LANES), F32)
                        if index is None
                        else flat[pl.ds(256 * index + stat, 32, stride=8), :]
                    )
                if block_id.get((first, 2 * half + 1)) is None:
                    continue
                even = jnp.where(lane32, pair[0], pltpu.roll(pair[1], GROUP, 1))
                odd = jnp.where(lane32, pltpu.roll(pair[0], GROUP, 1), pair[1])
                upper[half, pl.ds(GROUP * first, 32, stride=2), :] = even
                upper[half, pl.ds(GROUP * first + 1, 32, stride=2), :] = odd
        sign = -1.0 if stat in (1, 4) else 1.0
        for a in range(halves):
            rows_a = slice(LANES * a, LANES * (a + 1))
            for b in range(a, halves):
                rows_b = slice(LANES * b, LANES * (b + 1))
                block = upper[b, rows_a, :]
                turned = block.T * sign
                if a == b:
                    full[stat, rows_a, rows_a] = block + turned
                else:
                    full[stat, rows_a, rows_b] = block
                    full[stat, rows_b, rows_a] = turned

    gain_re = jnp.ones((1, stations), F32)
    gain_im = jnp.zeros((1, stations), F32)
    for round_id in range(ROUNDS):

        def build(step, carry):
            rows = pl.ds(pl.multiple_of(step * 16, 16), 16)
            vm_re, vm_im, mm = full[3, rows, :], full[4, rows, :], full[6, rows, :]
            if round_id == 0:
                cross_re, cross_im, power = full[0, rows, :], full[1, rows, :], full[5, rows, :]
                full[0, rows, :] = cross_re - vm_re
                full[1, rows, :] = cross_im - vm_im
                full[5, rows, :] = power - mm
            else:
                vv = full[2, rows, :]
                col_re = jnp.concatenate([col_gain_re[round_id - 1, rows, :]] * halves, axis=1)
                col_im = jnp.concatenate([col_gain_im[round_id - 1, rows, :]] * halves, axis=1)
                rest_re = 1.0 - (col_re * gain_re + col_im * gain_im)
                rest_im = col_re * gain_im - col_im * gain_re
                turn_re = rest_re * vm_re + rest_im * vm_im
                turn_im = rest_re * vm_im - rest_im * vm_re
                mm = vv + (rest_re * rest_re + rest_im * rest_im) * mm + (turn_re + turn_re)
                vm_re, vm_im = vv + turn_re, turn_im
                if round_id + 1 < ROUNDS:
                    full[3, rows, :], full[4, rows, :], full[6, rows, :] = vm_re, vm_im, mm
                cross_re, cross_im = full[0, rows, :] + vm_re, full[1, rows, :] + vm_im
                power = full[5, rows, :] + mm
            for part, value in enumerate((cross_re, cross_im, power)):
                weights[rows, part * stations : (part + 1) * stations] = value.astype(BF16)
            return carry

        lax.fori_loop(0, stations // 16, build, 0, unroll=4)
        row8 = lax.broadcasted_iota(jnp.int32, (8, stations), 0)
        for iteration in range(CAL_ITERS):
            norm = gain_re * gain_re + gain_im * gain_im
            left = jnp.where(row8 == 0, gain_re, jnp.where(row8 == 1, gain_im, norm))
            high = left.astype(BF16).astype(F32)
            left = jnp.concatenate([high, left - high]).astype(BF16)
            raw = jnp.dot(left, weights[...], preferred_element_type=F32)
            raw = raw[0:8] + raw[8:16]
            with_re, with_im = raw[:, 0:stations], raw[:, stations : 2 * stations]
            below = raw[2:3, 2 * stations : 3 * stations]
            next_re = (with_re[0:1] + with_im[1:2]) / below
            next_im = (with_re[1:2] - with_im[0:1]) / below
            if iteration % 2 == 1:
                next_re = 0.5 * (next_re + gain_re)
                next_im = 0.5 * (next_im + gain_im)
            gain_re, gain_im = next_re, next_im
        lane1 = lax.broadcasted_iota(jnp.int32, (1, LANES), 1) < GROUP
        for value, row_gain, col_gain in (
            (gain_re, row_gain_re, col_gain_re),
            (gain_im, row_gain_im, col_gain_im),
        ):
            for half in range(halves):
                part = value[:, LANES * half : LANES * (half + 1)]
                turned = pltpu.roll(jnp.broadcast_to(part, (8, LANES)), GROUP, 1)[0:1]
                row_gain[2 * half, round_id : round_id + 1, :] = jnp.where(lane1, part, turned)
                row_gain[2 * half + 1, round_id : round_id + 1, :] = jnp.where(lane1, turned, part)
                col_gain[round_id, LANES * half : LANES * (half + 1), :] = jnp.broadcast_to(
                    part, (LANES, LANES)
                ).T

    hot = (
        lax.broadcasted_iota(jnp.int32, (stations, stations), 0) == order[...]
    ).astype(BF16)
    pieces = []
    for value in (gain_re, gain_im):
        high = value.astype(BF16).astype(F32)
        middle = (value - high).astype(BF16).astype(F32)
        pieces += [high, middle, value - high - middle]
    row16 = lax.broadcasted_iota(jnp.int32, (16, stations), 0)
    left = jnp.zeros((16, stations), F32)
    for at, piece in enumerate(pieces):
        left = jnp.where(row16 == at, piece, left)
    spread = lax.dot_general(
        left.astype(BF16), hot, (((1,), (1,)), ((), ())), preferred_element_type=F32
    )
    gains[0:1, :] = spread[0:1] + spread[1:2] + spread[2:3]
    gains[1:2, :] = spread[3:4] + spread[4:5] + spread[5:6]

    mode = lax.broadcasted_iota(jnp.int32, (MODES, LANES), 0)
    lane_half = lax.broadcasted_iota(jnp.int32, (1, LANES), 1) < GROUP

    def tile(t, carry):
        row = first_row + 2 * t
        first, second = row_groups_of(row, groups)
        station = first * GROUP + (row & 63)

        def row_side(table, round_id):
            low, high = table[round_id, pl.ds(station, 1), :], table[round_id, pl.ds(station + 1, 1), :]
            return jnp.where(lane_half, low, high)

        q_res, q_ims = row_gain_re[second], row_gain_im[second]
        a_re, a_im = jnp.zeros((1, LANES), F32), jnp.zeros((1, LANES), F32)
        b_re, b_im = jnp.ones((1, LANES), F32), jnp.zeros((1, LANES), F32)
        for round_id in range(ROUNDS):
            p_re, p_im = row_side(col_gain_re, round_id), row_side(col_gain_im, round_id)
            q_re, q_im = q_res[round_id : round_id + 1], q_ims[round_id : round_id + 1]
            prod_re = p_re * q_re + p_im * q_im
            prod_im = p_im * q_re - p_re * q_im
            if round_id + 1 == ROUNDS:
                break
            rest_re, rest_im = 1.0 - prod_re, -prod_im
            a_re, a_im = 1.0 + rest_re * a_re - rest_im * a_im, rest_re * a_im + rest_im * a_re
            b_re, b_im = rest_re * b_re - rest_im * b_im, rest_re * b_im + rest_im * b_re
        b_re = b_re - 1.0
        inside = (mode < counts[pl.ds(t, 1), :]).astype(F32)
        raw = modes[tile_lanes(t, MODES), :]
        v_re, v_im, m_re, m_im = (raw[:, LANES * i : LANES * (i + 1)] for i in range(4))
        f_re = inside * (a_re * v_re - a_im * v_im + b_re * m_re - b_im * m_im)
        f_im = inside * (a_re * v_im + a_im * v_re + b_re * m_im + b_im * m_re)
        both = jnp.concatenate([f_re, f_im], axis=1)
        high = both.astype(BF16)
        low = (both - high.astype(F32)).astype(BF16)
        fitted = jnp.dot(
            expand[...], jnp.concatenate([high, low, high]), preferred_element_type=F32
        )
        start = pl.multiple_of(2 * t * FREQ_CHANNELS, FREQ_CHANNELS)
        mod_re = model[pl.ds(start, FREQ_CHANNELS), :].astype(F32) + fitted[:, 0:LANES]
        mod_im = model[pl.ds(start + FREQ_CHANNELS, FREQ_CHANNELS), :].astype(F32)
        mod_im = mod_im + fitted[:, LANES : 2 * LANES]
        obs_re, obs_im = data_sides(observed, tiles, t)
        weight = tile_weights(groups, tiles, first_row, t, kept)
        left_re = weight * (obs_re - (prod_re * mod_re - prod_im * mod_im))
        left_im = weight * (obs_im - (prod_re * mod_im + prod_im * mod_re))
        left_out[0, 0, :, tile_lanes(t)] = left_re.astype(BF16)
        left_out[1, 0, :, tile_lanes(t)] = left_im.astype(BF16)
        return carry

    parts = output_parts(tiles)
    size = tiles // parts
    copies = []
    for part in range(parts):
        lax.fori_loop(part * size, (part + 1) * size, tile, 0, unroll=size)
        lanes = pl.ds(part * size * LANES, size * LANES)
        copies.append(
            pltpu.make_async_copy(
                left_out.at[:, :, :, lanes], residual.at[:, :, :, lanes], out_sems.at[part]
            )
        )
        copies[-1].start()
    for copy in copies:
        copy.wait()


def call(kernel, out_shape, scratch, name, in_spaces, mib, flops=0, moved=0, out_specs=None):
    return pl.pallas_call(
        kernel,
        out_shape=out_shape,
        in_specs=[pl.BlockSpec(memory_space=space) for space in in_spaces],
        out_specs=out_specs or jax.tree.map(lambda _: pl.BlockSpec(memory_space=VMEM), out_shape),
        scratch_shapes=scratch,
        compiler_params=pltpu.CompilerParams(vmem_limit_bytes=mib << 20),
        cost_estimate=pl.CostEstimate(flops=flops, bytes_accessed=moved, transcendentals=0),
        name=name,
    )


def exchange(block, distance, wide):
    return lax.ppermute(block, "wide", [(i, i ^ distance) for i in range(wide)])


def gather_order(wide):
    order = [0, wide // 2, 3 * wide // 4, wide // 4]
    distance = wide // 8
    while distance:
        order += [place ^ distance for place in order]
        distance //= 2
    return order


def gather_stats(stats, wide):
    held = jnp.stack([stats] + [exchange(stats, flip, wide) for flip in gather_order(wide)[1:4]])
    distance = wide // 8
    while distance:
        held = jnp.concatenate([held, exchange(held, distance, wide)])
        distance //= 2
    return held


def body(
    visibilities,
    kept_baseline_mask,
    fitted_mode_count,
    station_order,
    station_xy,
    comp_lm,
    comp_flux,
    centre_flux,
):
    wide = lax.axis_size("wide")
    local_chan = visibilities.shape[2]
    total = visibilities.shape[3]
    base = total // wide
    tiles = base // LANES
    padded = -(-tiles // 8) * 8
    stations = station_order.shape[0]
    groups = stations // GROUP
    comps = comp_lm.shape[1]
    rows = 2 * padded
    fit, expand = (jnp.asarray(table) for table in basis_tables())
    kept = kept_baseline_mask.reshape(total // LANES, LANES)
    counts = fitted_mode_count.reshape(tiles, LANES)

    packed = pl.pallas_call(
        lambda *refs: pack_kernel(wide, base, *refs),
        out_shape=jax.ShapeDtypeStruct((wide, local_chan, 2 * base + LANES), BF16),
        in_specs=[pl.BlockSpec(memory_space=pltpu.MemorySpace.HBM)] * 2,
        out_specs=pl.BlockSpec(memory_space=pltpu.MemorySpace.HBM),
        scratch_shapes=[
            pltpu.VMEM((wide, local_chan, 2 * base + LANES), BF16),
            pltpu.SMEM((local_chan,), F32),
            pltpu.SemaphoreType.DMA((PACK_PARTS, 2)),
            pltpu.SemaphoreType.DMA((PACK_PARTS,)),
            pltpu.SemaphoreType.DMA,
        ],
        compiler_params=pltpu.CompilerParams(vmem_limit_bytes=60 << 20),
        name="pack",
    )(visibilities.reshape(2, local_chan, wide, base).transpose(0, 2, 1, 3), centre_flux)
    observed = lax.all_to_all(packed, "wide", 0, 0, tiled=True)
    observed = observed.reshape(FREQ_CHANNELS // 8, 8, 2 * base + LANES)

    state_row = pltpu.VMEM((rows, comps), F32)
    state_col = pltpu.VMEM((comps, LANES), F32)
    left = pltpu.VMEM((UNROLL, 2 * rows, comps), BF16)
    right = pltpu.VMEM((UNROLL, comps, 2 * LANES), BF16)
    real, imag = call(
        lambda *refs: predict_kernel(groups, tiles, padded, *refs),
        (
            jax.ShapeDtypeStruct((tiles * FREQ_CHANNELS, LANES), F32),
            jax.ShapeDtypeStruct((tiles * FREQ_CHANNELS, LANES), BF16),
        ),
        [pltpu.VMEM((padded * FREQ_CHANNELS, LANES), F32)] * 2
        + [pltpu.VMEM((rows + LANES, LANES), F32)] * 2
        + [state_row] * 4
        + [state_col] * 4
        + [left, right, left, right],
        "predict",
        [SMEM, SMEM, VMEM, VMEM],
        20,
        FREQ_CHANNELS * 2 * 2 * rows * 2 * comps * 256,
        padded * 256 * LANES * 4,
    )(station_order, station_xy.reshape(2, stations), comp_lm, comp_flux.reshape(1, comps))
    stats, model, modes = call(
        lambda *refs: stats_kernel(groups, tiles, *refs),
        (
            jax.ShapeDtypeStruct((stat_groups(tiles) * 8, LANES), BF16),
            jax.ShapeDtypeStruct((tiles * 2 * FREQ_CHANNELS, LANES), BF16),
            jax.ShapeDtypeStruct((tiles * MODES, 4 * LANES), F32),
        ),
        [pltpu.VMEM((FREQ_CHANNELS, LANES), F32), pltpu.VMEM((tiles * 8, LANES), F32)],
        "stats",
        [VMEM] * 6,
        12,
        moved=tiles * 256 * LANES * 8,
    )(observed, real, imag, kept, counts, fit)
    gathered = gather_stats(stats, wide)
    gains, residual = call(
        lambda *refs: solve_kernel(groups, tiles, wide, *refs),
        (
            jax.ShapeDtypeStruct((2, stations), F32),
            jax.ShapeDtypeStruct((2, 1, FREQ_CHANNELS, base), BF16),
        ),
        [
            pltpu.VMEM((wide * tiles * 8, LANES), F32),
            pltpu.VMEM((stations // LANES, stations, LANES), F32),
            pltpu.VMEM((STATS, stations, stations), F32),
            pltpu.VMEM((stations, 3 * stations), BF16),
            pltpu.VMEM((groups, 8, LANES), F32),
            pltpu.VMEM((groups, 8, LANES), F32),
            pltpu.VMEM((ROUNDS, stations, LANES), F32),
            pltpu.VMEM((ROUNDS, stations, LANES), F32),
            pltpu.VMEM((2, 1, FREQ_CHANNELS, base), BF16),
            pltpu.SemaphoreType.DMA((output_parts(tiles),)),
        ],
        "solve",
        [VMEM] * 8,
        16,
        moved=tiles * 256 * LANES * 6,
        out_specs=(
            pl.BlockSpec(memory_space=VMEM),
            pl.BlockSpec(memory_space=pltpu.MemorySpace.HBM),
        ),
    )(
        gathered,
        observed,
        model,
        modes,
        kept,
        counts,
        station_order.reshape(1, stations),
        expand,
    )
    return gains, residual


def solution(mesh):
    placed = (
        P(None, None, ("band", "wide"), None),
        P("band"),
        P("wide"),
        P(),
        P(),
        P(),
        P(),
        P(("band", "wide")),
    )
    return jax.shard_map(
        body,
        mesh=mesh,
        in_specs=placed,
        out_specs=(P(None, "band"), P(None, None, "band", "wide")),
        check_vma=False,
    )
```

time: 67.7 us -> 65.6 us (0.969)
  Pallas kernels: 40.2 us -> 33.3 us
  waiting for transfers between devices: 11.2 us -> 15.5 us
  starting transfers between devices: 13 us -> 15.5 us
  local copies, waits for them, and re-layouts: 2.23 us -> 0.2 us
    pallas_call x1, Pallas kernels: 29 us -> 23.4 us  [body(): call(lambda *refs: predict_kernel(groups, tiles, padded, *refs), (jax.Sha...]
    all_to_all x1, waiting for transfers between devices: 0.01 us -> 4.49 us  [body(): observed = lax.all_to_all(packed, 'wide', 0, 0, tiled=True)]
    ppermute x5, starting transfers between devices: 5.56 us -> 7.93 us  [exchange(): return lax.ppermute(block, 'wide', [(i, i ^ distance) for i in range(wide)])]
    unnamed x20, local copies, waits for them, and re-layouts: 2.12 us -> 0.1 us
    pallas_call x1, Pallas kernels: 7.04 us -> 6.24 us  [body(): call(lambda *refs: solve_kernel(groups, tiles, wide, *refs), (jax.ShapeDt...]
  transfers between devices with their start and end apart: 6 -> 6, of which waited for: 4 -> 5; matrix products, arithmetic and copies ran while one was open for 0% -> 0% of each run, Pallas kernels for 43% -> 36%
where the time goes in v3:
time: 65.6 us; the launch traced here: 65.3 us
  Pallas kernels  33.3 us (51%)
  starting transfers between devices  15.5 us (24%)
  waiting for transfers between devices  15.5 us (24%)
  between operations  0.8 us (1%)
    pallas_call x1, Pallas kernels, body(): call(lambda *refs: predict_kernel(groups, tiles, padded, *refs), (jax.Sha...  23.4 us
    ppermute x5, waiting for transfers between devices, exchange(): return lax.ppermute(block, 'wide', [(i, i ^ distance) for i in range(wide)])  11 us
    ppermute x5, starting transfers between devices, exchange(): return lax.ppermute(block, 'wide', [(i, i ^ distance) for i in range(wide)])  7.93 us
    all_to_all x1, starting transfers between devices, body(): observed = lax.all_to_all(packed, 'wide', 0, 0, tiled=True)  7.53 us
    pallas_call x1, Pallas kernels, body(): call(lambda *refs: solve_kernel(groups, tiles, wide, *refs), (jax.ShapeDt...  6.24 us
    all_to_all x1, waiting for transfers between devices, body(): observed = lax.all_to_all(packed, 'wide', 0, 0, tiled=True)  4.49 us
    pallas_call x1, Pallas kernels, body(): pl.pallas_call(lambda *refs: pack_kernel(wide, base, *refs), out_shape=ja...  2.26 us
    pallas_call x1, Pallas kernels, body(): call(lambda *refs: stats_kernel(groups, tiles, *refs), (jax.ShapeDtypeStr...  1.42 us
  transfers between devices with their start and end apart: 6, of which 5 were waited for; matrix products, arithmetic and copies ran while one was open for 0% of the time, Pallas kernels for 36%

profile of v3, /device:TPU:0, one launch (start us, length us, event | category | flops | bytes accessed | tf_op | source)
XLA Modules:
  0.0 65.3 jit_solution(17286249079304779284)
XLA Ops:
  0.6 2.3 %pack.1 = bf16[16,8,5248]{2,1,0:T(8,128)(2,1)} custom-call(bf16[2,16,8,2560]{3,2,1,0:T(8,128)(2,1)} %bitcast.28, f32[8]{0:T(128)} %refs_1_.1), custom_call_target="tpu_custom_call" | custom-call | tf_op jit(solution)/shard_map/pack/pallas_call | solution.py:610
  2.9 0.0 copy-start.4
  2.9 0.0 copy-start.5
  2.9 0.0 copy-start.6
  2.9 0.0 copy-start.7
  2.9 7.5 %all-to-all-start = ((bf16[16,8,5248]{2,1,0:T(8,128)(2,1)}), bf16[16,8,5248]{2,1,0:T(8,128)(2,1)S(1)}, u32[]{:S(2)}, u32[]{:S(2)}) async-start(bf16[16,8,5248]{2,1,0:T(8,128)(2,1)} %pack.1), calls=%async_computation | async-start | bytes 2686976 | tf_op jit(solution)/shard_map/all_to_all | solution.py:625
  10.5 0.0 copy-start
  10.5 0.0 copy-start.1
  10.5 0.0 copy-start.3
  10.6 23.4 %predict.1 = (f32[2560,128]{1,0:T(8,128)S(1)}, bf16[2560,128]{1,0:T(8,128)(2,1)S(1)}) custom-call(s32[256]{0:T(256)S(1)} %copy-done.4, f32[2,256]{1,0:T(2,128)S(1)} %bitcast.26, f32[2,512]{1,0:T(2,128)S(1)} %copy-done.5, f32[1,512]{1,0:T(1,128)S(1)} %bitcast.27), custom_call_target="tpu_custom_call" | custom-call | flops 6442450944 | bytes 3145728 | tf_op jit(solution)/shard_map/predict/pallas_call | solution.py:632
  34.0 4.5 %all-to-all-done.refs_0_.refs_1_ = bf16[16,8,5248]{2,1,0:T(8,128)(2,1)S(1)} async-done(((bf16[16,8,5248]{2,1,0:T(8,128)(2,1)}), bf16[16,8,5248]{2,1,0:T(8,128)(2,1)S(1)}, u32[]{:S(2)}, u32[]{:S(2)}) %all-to-all-start) | async-done | bytes 1343520 | tf_op jit(solution)/shard_map/all_to_all | solution.py:625
  38.5 1.4 %stats.1 = (bf16[144,128]{1,0:T(8,128)(2,1)S(1)}, bf16[5120,128]{1,0:T(8,128)(2,1)S(1)}, f32[320,512]{1,0:T(8,128)S(1)}) custom-call(bf16[16,8,5248]{2,1,0:T(8,128)(2,1)S(1)} %all-to-all-done.refs_0_.refs_1_, f32[2560,128]{1,0:T(8,128)S(1)} %get-tuple-element.7.refs_1_, bf16[2560,128]{1,0:T(8,128)(2,1)S(1)} %get-tuple-element.8.refs_2_, ...), custom_call_target="tpu_custom_call" | custom-call | bytes 5242880 | tf_op jit(solution)/shard_map/stats/pallas_call | solution.py:649
  39.9 0.0 copy-start.2
  39.9 6.4 %collective-permute-start = (bf16[144,128]{1,0:T(8,128)(2,1)S(1)}, bf16[144,128]{1,0:T(8,128)(2,1)S(1)}, u32[]{:S(2)}, u32[]{:S(2)}) collective-permute-start(bf16[144,128]{1,0:T(8,128)(2,1)S(1)} %get-tuple-element.9), channel_id=1, source_target_pairs={{0,8},{1,9},{2,10},{3,11},{4,12},{5,13},{6,14},{7,15},{8,0},{9,1},... | collective-permute-start | bytes 110600 | tf_op jit(solution)/shard_map/ppermute | solution.py:565
  46.3 0.2 collective-permute-start.1
  46.5 0.5 collective-permute-start.2
  47.0 2.1 %collective-permute-done = bf16[144,128]{1,0:T(8,128)(2,1)S(1)} collective-permute-done((bf16[144,128]{1,0:T(8,128)(2,1)S(1)}, bf16[144,128]{1,0:T(8,128)(2,1)S(1)}, u32[]{:S(2)}, u32[]{:S(2)}) %collective-permute-start) | collective-permute-done | bytes 36896 | tf_op jit(solution)/shard_map/ppermute | solution.py:565
  49.0 3.0 %collective-permute-done.1 = bf16[144,128]{1,0:T(8,128)(2,1)S(1)} collective-permute-done((bf16[144,128]{1,0:T(8,128)(2,1)S(1)}, bf16[144,128]{1,0:T(8,128)(2,1)S(1)}, u32[]{:S(2)}, u32[]{:S(2)}) %collective-permute-start.1) | collective-permute-done | bytes 36896 | tf_op jit(solution)/shard_map/ppermute | solution.py:565
  52.1 0.8 %collective-permute-start.3 = (bf16[4,144,128]{2,1,0:T(8,128)(2,1)S(1)}, bf16[4,144,128]{2,1,0:T(8,128)(2,1)S(1)}, u32[]{:S(2)}, u32[]{:S(2)}) collective-permute-start(bf16[4,144,128]{2,1,0:T(8,128)(2,1)S(1)} %pad_maximum_fusion), channel_id=1, source_target_pairs={{0,2},{1,3},{2,0},{3,1},{4,6},{5,7},{6,4},{7,5},{8,10},{9,11},{10,... | collective-permute-start | bytes 442376 | tf_op jit(solution)/shard_map/ppermute | solution.py:565
  53.0 4.3 %collective-permute-done.3 = bf16[4,144,128]{2,1,0:T(8,128)(2,1)S(1)} collective-permute-done((bf16[4,144,128]{2,1,0:T(8,128)(2,1)S(1)}, bf16[4,144,128]{2,1,0:T(8,128)(2,1)S(1)}, u32[]{:S(2)}, u32[]{:S(2)}) %collective-permute-start.3) | collective-permute-done | bytes 147488 | tf_op jit(solution)/shard_map/ppermute | solution.py:565
  57.3 0.1 constant_dynamic-update-slice_fusion
  57.4 0.1 collective-permute-start.4
  57.4 1.6 %collective-permute-done.4 = bf16[8,144,128]{2,1,0:T(8,128)(2,1)S(1)} collective-permute-done((bf16[8,144,128]{2,1,0:T(8,128)(2,1)S(1)}, bf16[8,144,128]{2,1,0:T(8,128)(2,1)S(1)}, u32[]{:S(2)}, u32[]{:S(2)}) %collective-permute-start.4) | collective-permute-done | bytes 294944 | tf_op jit(solution)/shard_map/ppermute | solution.py:565
  59.1 6.2 %solve.1 = (f32[2,256]{1,0:T(2,128)}, bf16[2,1,128,2560]{3,2,1,0:T(8,128)(2,1)}) custom-call(bf16[16,144,128]{2,1,0:T(8,128)(2,1)S(1)} %constant_dynamic-update-slice_fusion.5.refs_0_, bf16[16,8,5248]{2,1,0:T(8,128)(2,1)S(1)} %all-to-all-done.refs_0_.refs_1_, bf16[5120,128]{1,0:T(8,128)(2,1)S(1)} %get-tuple-element.10.refs_2_, ...), custom_call_target="tpu_custom_call" | custom-call | bytes 3932160 | tf_op jit(solution)/shard_map/solve/pallas_call | solution.py:663
  (15 shorter events, 0.1 us)
Async XLA Ops:
  2.9 7.6 %copy-start.4 = (s32[256]{0:T(256)S(1)}, s32[256]{0:T(256)}, u32[]{:S(2)}) copy-start(s32[256]{0:T(256)} %refs_0_.1) | copy-start | bytes 3076
  2.9 7.6 %copy-start.5 = (f32[2,512]{1,0:T(2,128)S(1)}, f32[2,512]{1,0:T(2,128)}, u32[]{:S(2)}) copy-start(f32[2,512]{1,0:T(2,128)} %refs_2_.1) | copy-start | bytes 12292
  2.9 7.6 %copy-start.6 = (f32[1,2,256]{2,1,0:T(2,128)S(1)}, f32[1,2,256]{2,1,0:T(2,128)}, u32[]{:S(2)}) copy-start(f32[1,2,256]{2,1,0:T(2,128)} %param.14) | copy-start | bytes 6148
  2.9 7.6 %copy-start.7 = (f32[512]{0:T(512)S(1)}, f32[512]{0:T(512)}, u32[]{:S(2)}) copy-start(f32[512]{0:T(512)} %param.16) | copy-start | bytes 6148
  2.9 35.5 %all-to-all-start = ((bf16[16,8,5248]{2,1,0:T(8,128)(2,1)}), bf16[16,8,5248]{2,1,0:T(8,128)(2,1)S(1)}, u32[]{:S(2)}, u32[]{:S(2)}) async-start(bf16[16,8,5248]{2,1,0:T(8,128)(2,1)} %pack.1), calls=%async_computation | async-start | bytes 2686976 | tf_op jit(solution)/shard_map/all_to_all | solution.py:625
  10.5 27.9 %copy-start = (s32[40960]{0:T(1024)S(1)}, s32[40960]{0:T(1024)}, u32[]{:S(2)}) copy-start(s32[40960]{0:T(1024)} %param.11) | copy-start | bytes 491524
  10.5 27.9 %copy-start.1 = (s32[2560]{0:T(1024)S(1)}, s32[2560]{0:T(1024)}, u32[]{:S(2)}) copy-start(s32[2560]{0:T(1024)} %param.12) | copy-start | bytes 30724
  10.5 27.9 %copy-start.3 = (bf16[32,128]{1,0:T(8,128)(2,1)S(1)}, bf16[32,128]{1,0:T(8,128)(2,1)}, u32[]{:S(2)}) copy-start(bf16[32,128]{1,0:T(8,128)(2,1)} %constant.4.clone.refs_5_) | copy-start | bytes 24580
  39.9 19.2 %copy-start.2 = (bf16[128,48]{1,0:T(8,128)(2,1)S(1)}, bf16[128,48]{1,0:T(8,128)(2,1)}, u32[]{:S(2)}) copy-start(bf16[128,48]{1,0:T(8,128)(2,1)} %constant.5.clone.refs_7_) | copy-start | bytes 36868
  39.9 9.1 %collective-permute-start = (bf16[144,128]{1,0:T(8,128)(2,1)S(1)}, bf16[144,128]{1,0:T(8,128)(2,1)S(1)}, u32[]{:S(2)}, u32[]{:S(2)}) collective-permute-start(bf16[144,128]{1,0:T(8,128)(2,1)S(1)} %get-tuple-element.9), channel_id=1, source_target_pairs={{0,8},{1,9},{2,10},{3,11},{4,12},{5,13},{6,14},{7,15},{8,0},{9,1},... | collective-permute-start | bytes 110600 | tf_op jit(solution)/shard_map/ppermute | solution.py:565
  46.3 5.8 %collective-permute-start.1 = (bf16[144,128]{1,0:T(8,128)(2,1)S(1)}, bf16[144,128]{1,0:T(8,128)(2,1)S(1)}, u32[]{:S(2)}, u32[]{:S(2)}) collective-permute-start(bf16[144,128]{1,0:T(8,128)(2,1)S(1)} %get-tuple-element.9), channel_id=1, source_target_pairs={{0,12},{1,13},{2,14},{3,15},{4,8},{5,9},{6,10},{7,11},{8,4},{9,5},... | collective-permute-start | bytes 110600 | tf_op jit(solution)/shard_map/ppermute | solution.py:565
  46.5 5.6 %collective-permute-start.2 = (bf16[144,128]{1,0:T(8,128)(2,1)S(1)}, bf16[144,128]{1,0:T(8,128)(2,1)S(1)}, u32[]{:S(2)}, u32[]{:S(2)}) collective-permute-start(bf16[144,128]{1,0:T(8,128)(2,1)S(1)} %get-tuple-element.9), channel_id=1, source_target_pairs={{0,4},{1,5},{2,6},{3,7},{4,0},{5,1},{6,2},{7,3},{8,12},{9,13},{10,... | collective-permute-start | bytes 110600 | tf_op jit(solution)/shard_map/ppermute | solution.py:565
  52.1 5.2 %collective-permute-start.3 = (bf16[4,144,128]{2,1,0:T(8,128)(2,1)S(1)}, bf16[4,144,128]{2,1,0:T(8,128)(2,1)S(1)}, u32[]{:S(2)}, u32[]{:S(2)}) collective-permute-start(bf16[4,144,128]{2,1,0:T(8,128)(2,1)S(1)} %pad_maximum_fusion), channel_id=1, source_target_pairs={{0,2},{1,3},{2,0},{3,1},{4,6},{5,7},{6,4},{7,5},{8,10},{9,11},{10,... | collective-permute-start | bytes 442376 | tf_op jit(solution)/shard_map/ppermute | solution.py:565
  57.4 1.6 %collective-permute-start.4 = (bf16[8,144,128]{2,1,0:T(8,128)(2,1)S(1)}, bf16[8,144,128]{2,1,0:T(8,128)(2,1)S(1)}, u32[]{:S(2)}, u32[]{:S(2)}) collective-permute-start(bf16[8,144,128]{2,1,0:T(8,128)(2,1)S(1)} %get-tuple-element.12), channel_id=1, source_target_pairs={{0,1},{1,0},{2,3},{3,2},{4,5},{5,4},{6,7},{7,6},{8,9},{9,8},{10,11... | collective-permute-start | bytes 884744 | tf_op jit(solution)/shard_map/ppermute | solution.py:565

commit v4 on v3

--- a/solution.py
+++ b/solution.py
@@ -14,9 +14,11 @@
 CAL_ITERS = 3
 ROUNDS = 3
 STATS = 7
+PAIRS = 4
 LANES = 128
-UNROLL = 4
+UNROLL = 8
 PACK_PARTS = 4
+PLACES_FLOPS = 4 * 10**9
 VMEM = pltpu.MemorySpace.VMEM
 SMEM = pltpu.MemorySpace.SMEM
 F32 = jnp.float32
@@ -47,11 +49,12 @@
 
 
 def output_parts(tiles):
-    return 4 if tiles % 4 == 0 else 2
-
-
-def stat_groups(tiles):
-    return -(-tiles * STATS // 8)
+    sizes = []
+    for left in (tiles - early_tiles(tiles), early_tiles(tiles)):
+        while left:
+            sizes.append(-(-left // 2))
+            left -= sizes[-1]
+    return sizes
 
 
 def turn_trig(turns):
@@ -77,15 +80,66 @@
     return cos_out, sin_out
 
 
-def pack_kernel(wide, base, source, centre, target, held, flux, in_sems, out_sems, flux_sem):
+def early_tiles(tiles):
+    return tiles * 3 // 10
+
+
+def pack_early_kernel(wide, base, source, centre, *rest):
+    targets, (held, flux, in_sems, out_sems, flux_sem) = rest[:4], rest[4:]
     chan = centre.shape[0]
+    rank = lax.axis_index("wide")
+    quarter = wide // 4
+    late = base - early_tiles(base // LANES) * LANES
+    size = base - late
+    bring = [
+        pltpu.make_async_copy(
+            source.at[side, :, :, pl.ds(late, size)],
+            held.at[:, :, pl.ds(side * size, size)],
+            in_sems.at[side],
+        )
+        for side in range(2)
+    ]
+    fetch = pltpu.make_async_copy(centre, flux, flux_sem)
+    fetch.start()
+    for copy in bring:
+        copy.start()
+    fetch.wait()
+    row = lax.broadcasted_iota(jnp.int32, (chan, LANES), 0)
+    lane = lax.broadcasted_iota(jnp.int32, (chan, LANES), 1)
+    value = jnp.zeros(row.shape, F32)
+    for c in range(chan):
+        value = jnp.where(row == c, flux[c], value)
+    high = value.astype(BF16).astype(F32)
+    middle = (value - high).astype(BF16).astype(F32)
+    low = value - high - middle
+    parts = jnp.where(lane == 0, high, jnp.where(lane == 1, middle, jnp.where(lane == 2, low, 0.0)))
+    held[:, :, 2 * size : 2 * size + LANES] = jnp.broadcast_to(
+        parts.astype(BF16)[None], (wide, chan, LANES)
+    )
+    for copy in bring:
+        copy.wait()
+    send = [
+        pltpu.make_async_copy(
+            held.at[rank ^ flip], targets[flip // quarter].at[flip % quarter], out_sems.at[flip]
+        )
+        for flip in range(wide)
+    ]
+    for copy in send:
+        copy.start()
+    for copy in send:
+        copy.wait()
+
+
+def pack_kernel(wide, base, source, after, target, held, in_sems, out_sems):
+    del after
+    size = base - early_tiles(base // LANES) * LANES
     share = wide // PACK_PARTS
     peers = [pl.ds(part * share, share) for part in range(PACK_PARTS)]
     bring = [
         [
             pltpu.make_async_copy(
-                source.at[side, peers[part]],
-                held.at[peers[part], :, pl.ds(side * base, base)],
+                source.at[side, peers[part], :, pl.ds(0, size)],
+                held.at[peers[part], :, pl.ds(side * size, size)],
                 in_sems.at[part, side],
             )
             for side in range(2)
@@ -96,24 +150,9 @@
         pltpu.make_async_copy(held.at[peers[part]], target.at[peers[part]], out_sems.at[part])
         for part in range(PACK_PARTS)
     ]
-    fetch = pltpu.make_async_copy(centre, flux, flux_sem)
-    fetch.start()
     for pair in bring:
         for copy in pair:
             copy.start()
-    fetch.wait()
-    row = lax.broadcasted_iota(jnp.int32, (chan, LANES), 0)
-    lane = lax.broadcasted_iota(jnp.int32, (chan, LANES), 1)
-    value = jnp.zeros(row.shape, F32)
-    for c in range(chan):
-        value = jnp.where(row == c, flux[c], value)
-    high = value.astype(BF16).astype(F32)
-    middle = (value - high).astype(BF16).astype(F32)
-    low = value - high - middle
-    parts = jnp.where(lane == 0, high, jnp.where(lane == 1, middle, jnp.where(lane == 2, low, 0.0)))
-    held[:, :, 2 * base : 2 * base + LANES] = jnp.broadcast_to(
-        parts.astype(BF16)[None], (wide, chan, LANES)
-    )
     for pair, copy in zip(bring, send):
         for came in pair:
             came.wait()
@@ -122,61 +161,70 @@
         copy.wait()
 
 
+def column_groups(groups, tiles, first_row):
+    last_row = first_row + (2 * tiles - 1)
+    return [row_groups_of(row, groups)[1] * GROUP for row in (first_row, last_row)]
+
+
+def places_kernel(groups, tiles, padded, order, xy, after, pos_x, pos_y):
+    del after
+    first_row = lax.axis_index("wide") * (2 * tiles)
+    col_a, col_b = column_groups(groups, tiles, first_row)
+    pos_x[...] = jnp.zeros_like(pos_x)
+    pos_y[...] = jnp.zeros_like(pos_y)
+
+    def place(slot, position):
+        station = order[position]
+        pos_x[pl.ds(slot, 1), :] = jnp.full((1, LANES), xy[0, station], F32)
+        pos_y[pl.ds(slot, 1), :] = jnp.full((1, LANES), xy[1, station], F32)
+
+    def place_row(t, carry):
+        for half in range(2):
+            row = first_row + 2 * t + half
+            place(half * padded + t, row_groups_of(row, groups)[0] * GROUP + (row & 63))
+        return carry
+
+    def place_col(j, carry):
+        place(2 * padded + j, col_a + j)
+        place(2 * padded + GROUP + j, col_b + j)
+        return carry
+
+    lax.fori_loop(0, tiles, place_row, 0, unroll=10)
+    lax.fori_loop(0, GROUP, place_col, 0, unroll=16)
+
+
 def predict_kernel(
     groups,
     tiles,
     padded,
-    order,
-    xy,
+    pos_x,
+    pos_y,
     lm,
     flux,
     real_out,
     imag_out,
     real,
     imag,
-    pos_x,
-    pos_y,
     row_c,
     row_s,
     row_dc,
     row_ds,
+    row_lc,
+    row_ls,
     col_c,
     col_s,
     col_dc,
     col_ds,
+    col_lc,
+    col_ls,
     left_a,
     right_a,
     left_b,
     right_b,
 ):
     comps = lm.shape[1]
-    rank = lax.axis_index("wide")
-    first_row = rank * (2 * tiles)
-    last_row = first_row + (2 * tiles - 1)
-    col_a = row_groups_of(first_row, groups)[1] * GROUP
-    col_b = row_groups_of(last_row, groups)[1] * GROUP
+    first_row = lax.axis_index("wide") * (2 * tiles)
     edge = jnp.minimum((((first_row >> 6) + 1) * GROUP - first_row) >> 1, tiles)
-    pos_x[...] = jnp.zeros_like(pos_x)
-    pos_y[...] = jnp.zeros_like(pos_y)
-
-    def place(slot, position):
-        station = order[position]
-        pos_x[pl.ds(slot, 1), :] = jnp.full((1, LANES), xy[0, station], F32)
-        pos_y[pl.ds(slot, 1), :] = jnp.full((1, LANES), xy[1, station], F32)
-
-    def place_row(t, carry):
-        for half in range(2):
-            row = first_row + 2 * t + half
-            place(half * padded + t, row_groups_of(row, groups)[0] * GROUP + (row & 63))
-        return carry
-
-    def place_col(j, carry):
-        place(2 * padded + j, col_a + j)
-        place(2 * padded + GROUP + j, col_b + j)
-        return carry
-
-    lax.fori_loop(0, tiles, place_row, 0, unroll=2)
-    lax.fori_loop(0, GROUP, place_col, 0, unroll=4)
     step = 0.25 / FREQ_CHANNELS
     rows = 2 * padded
     weight = flux[...] * (1.0 / math.sqrt(comps))
@@ -189,30 +237,37 @@
         row_c[:, lane] = cosine * weight[:, lane]
         row_s[:, lane] = sine * weight[:, lane]
         row_dc[:, lane], row_ds[:, lane] = turn_trig(turns * step)
+        row_lc[:, lane], row_ls[:, lane] = turn_trig(turns * (UNROLL * step))
         turns = (
             pos_x[rows : rows + LANES, :] * axis_l + pos_y[rows : rows + LANES, :] * axis_m
         ).T
         col_c[lane, :], col_s[lane, :] = turn_trig(turns)
         col_dc[lane, :], col_ds[lane, :] = turn_trig(turns * step)
+        col_lc[lane, :], col_ls[lane, :] = turn_trig(turns * (UNROLL * step))
+
+    def channels(c, s, dc, ds, leap_c, leap_s):
+        twice = dc + dc
+        out = [(c, s), (c * dc - s * ds, s * dc + c * ds)]
+        while len(out) < UNROLL:
+            out.append(tuple(twice * now - before for now, before in zip(out[-1], out[-2])))
+        return out, (c * leap_c - s * leap_s, s * leap_c + c * leap_s)
 
     def fill_col(right, k):
         part = slice(k, k + 16)
-        c, s, dc, ds = col_c[part, :], col_s[part, :], col_dc[part, :], col_ds[part, :]
-        for u in range(UNROLL):
+        state = [table[part, :] for table in (col_c, col_s, col_dc, col_ds, col_lc, col_ls)]
+        values, (col_c[part, :], col_s[part, :]) = channels(*state)
+        for u, (c, s) in enumerate(values):
             right[u, part, 0:LANES] = c.astype(BF16)
             right[u, part, LANES : 2 * LANES] = s.astype(BF16)
-            c, s = c * dc - s * ds, s * dc + c * ds
-        col_c[part, :], col_s[part, :] = c, s
 
     def fill_row(left, r, k):
         part, low = slice(r, r + 16), slice(rows + r, rows + r + 16)
         lane = slice(k, k + LANES)
-        c, s, dc, ds = row_c[part, lane], row_s[part, lane], row_dc[part, lane], row_ds[part, lane]
-        for u in range(UNROLL):
+        state = [table[part, lane] for table in (row_c, row_s, row_dc, row_ds, row_lc, row_ls)]
+        values, (row_c[part, lane], row_s[part, lane]) = channels(*state)
+        for u, (c, s) in enumerate(values):
             left[u, part, lane] = c.astype(BF16)
             left[u, low, lane] = s.astype(BF16)
-            c, s = c * dc - s * ds, s * dc + c * ds
-        row_c[part, lane], row_s[part, lane] = c, s
 
     def fill_steps(left, right):
         steps = [lambda k=k: fill_col(right, k) for k in range(0, comps, 16)]
@@ -275,7 +330,7 @@
     return pl.ds(pl.multiple_of(offset + t * size, size), size)
 
 
-def data_sides(observed, tiles, t):
+def late_sides(observed, tiles, t):
     return [
         observed[:, :, tile_lanes(t, LANES, side * tiles * LANES)]
         .astype(F32)
@@ -284,18 +339,29 @@
     ]
 
 
+def early_lanes(early, key, lanes):
+    blocks = [early[key ^ at, :, lanes].astype(F32) for at in range(early.shape[0])]
+    return jnp.concatenate(blocks)
+
+
+def early_sides(early, key, tiles, t):
+    return [early_lanes(early, key, tile_lanes(t, LANES, side * tiles * LANES)) for side in range(2)]
+
+
 def stats_kernel(
-    groups, tiles, observed, real, imag, kept, counts, fit, stats, model, modes, shift, rows
+    groups, tiles, by_flip, observed, early, real, imag, kept, counts, fit, stats, model, modes, shift, rows, paired
 ):
     rank = lax.axis_index("wide")
     first_row = rank * (2 * tiles)
     mode = lax.broadcasted_iota(jnp.int32, (MODES, LANES), 0)
-    tail = observed[:, :, 2 * tiles * LANES : (2 * tiles + 1) * LANES].astype(F32)
-    tail = tail.reshape(FREQ_CHANNELS, LANES)
+    key = rank if by_flip else 0
+    ahead = early_tiles(tiles)
+    rest = tiles - ahead
+    tail = early_lanes(early, key, pl.ds(2 * ahead * LANES, LANES))
     shift[...] = jnp.broadcast_to(jnp.sum(tail, axis=1, keepdims=True), tail.shape)
 
-    def one(t, carry):
-        obs_re, obs_im = data_sides(observed, tiles, t)
+    def one(t, sides):
+        obs_re, obs_im = sides
         half = tile_lanes(t, FREQ_CHANNELS)
         mod_re16, mod_im16 = (real[half, :] + shift[...]).astype(BF16), imag[half, :]
         both = pl.multiple_of(2 * t * FREQ_CHANNELS, FREQ_CHANNELS)
@@ -322,22 +388,36 @@
         weight = tile_weights(groups, tiles, first_row, t, kept)
         parts = [cross_re, cross_im, vv, vm_re, vm_im, power, mm, jnp.zeros((1, LANES), F32)]
         rows[tile_lanes(t, 8), :] = jnp.concatenate(parts) * weight
+
+    def one_late(t, carry):
+        one(t, late_sides(observed, rest, t))
         return carry
 
-    lax.fori_loop(0, tiles, one, 0, unroll=10)
-    held = stat_groups(tiles)
-    for extra in range(tiles - held):
-        late = 8 * (held + extra)
-        rows[pl.ds(7 + 8 * STATS * extra, STATS, stride=8), :] = rows[late : late + STATS, :]
-    stats[...] = rows[0 : 8 * held, :].astype(BF16)
+    def one_early(t, carry):
+        one(rest + t, early_sides(early, key, ahead, t))
+        return carry
+
+    lax.fori_loop(0, rest, one_late, 0, unroll=rest // 2 if rest % 2 == 0 else rest)
+    lax.fori_loop(0, ahead, one_early, 0, unroll=ahead)
+    first_half = lax.broadcasted_iota(jnp.int32, (tiles, LANES), 1) < GROUP
+    for pair in range(PAIRS):
+        one_stat = rows[pl.ds(2 * pair, tiles, stride=8), :]
+        other = rows[pl.ds(2 * pair + 1, tiles, stride=8), :]
+        even = jnp.where(first_half, one_stat, pltpu.roll(other, GROUP, 1))
+        odd = jnp.where(first_half, pltpu.roll(one_stat, GROUP, 1), other)
+        paired[pl.ds(2 * tiles * pair, tiles, stride=2), :] = even
+        paired[pl.ds(2 * tiles * pair + 1, tiles, stride=2), :] = odd
+    stats[...] = paired[...].astype(BF16)
 
 
 def solve_kernel(
     groups,
     tiles,
+    by_flip,
     wide,
     gathered,
     observed,
+    early,
     model,
     modes,
     kept,
@@ -347,7 +427,6 @@
     gains,
     residual,
     flat,
-    upper,
     full,
     weights,
     row_gain_re,
@@ -360,43 +439,38 @@
     stations = groups * GROUP
     rank = lax.axis_index("wide")
     first_row = rank * (2 * tiles)
-    chunk = 8 * tiles
-    held = stat_groups(tiles)
+    halves = stations // LANES
+    count = 2 * tiles
     for k, flip in enumerate(gather_order(wide)):
-        start = pl.multiple_of((rank ^ flip) * chunk, 16)
-        flat[pl.ds(start, 8 * held), :] = gathered[k].astype(F32)
-        for extra in range(tiles - held):
-            late = flat[pl.ds(start + (7 + 8 * STATS * extra), STATS, stride=8), :]
-            flat[pl.ds(pl.multiple_of(start + 8 * (held + extra), 8), STATS), :] = late
-    halves = stations // LANES
-    lane32 = lax.broadcasted_iota(jnp.int32, (32, LANES), 1) < GROUP
+        start = pl.multiple_of((rank ^ flip) * count, count & -count)
+        values = gathered[k].astype(F32)
+        for pair in range(PAIRS):
+            flat[pair, pl.ds(start, count), :] = values[pair * count : (pair + 1) * count]
     block_id = {}
     for first in range(groups):
         for second in range(first, groups):
             block_id[first, second] = len(block_id)
+    lane64 = lax.broadcasted_iota(jnp.int32, (GROUP, LANES), 1) < GROUP
+
+    def placed_block(stat, first, half):
+        pair, side = stat // 2, stat % 2
+        sides = []
+        for at in range(2):
+            index = block_id.get((first, 2 * half + at))
+            if index is None:
+                sides.append(jnp.zeros((GROUP, LANES), F32))
+                continue
+            block = flat[pair, GROUP * index : GROUP * (index + 1), :]
+            sides.append(block if at == side else pltpu.roll(block, GROUP, 1))
+        return jnp.where(lane64, sides[0], sides[1])
+
     for stat in range(STATS):
-        for first in range(groups):
-            for half in range(halves):
-                pair = []
-                for side in range(2):
-                    index = block_id.get((first, 2 * half + side))
-                    pair.append(
-                        jnp.zeros((32, LANES), F32)
-                        if index is None
-                        else flat[pl.ds(256 * index + stat, 32, stride=8), :]
-                    )
-                if block_id.get((first, 2 * half + 1)) is None:
-                    continue
-                even = jnp.where(lane32, pair[0], pltpu.roll(pair[1], GROUP, 1))
-                odd = jnp.where(lane32, pltpu.roll(pair[0], GROUP, 1), pair[1])
-                upper[half, pl.ds(GROUP * first, 32, stride=2), :] = even
-                upper[half, pl.ds(GROUP * first + 1, 32, stride=2), :] = odd
         sign = -1.0 if stat in (1, 4) else 1.0
         for a in range(halves):
             rows_a = slice(LANES * a, LANES * (a + 1))
             for b in range(a, halves):
                 rows_b = slice(LANES * b, LANES * (b + 1))
-                block = upper[b, rows_a, :]
+                block = jnp.concatenate([placed_block(stat, 2 * a + i, b) for i in range(2)])
                 turned = block.T * sign
                 if a == b:
                     full[stat, rows_a, rows_a] = block + turned
@@ -465,28 +539,14 @@
                     part, (LANES, LANES)
                 ).T
 
-    hot = (
-        lax.broadcasted_iota(jnp.int32, (stations, stations), 0) == order[...]
-    ).astype(BF16)
-    pieces = []
-    for value in (gain_re, gain_im):
-        high = value.astype(BF16).astype(F32)
-        middle = (value - high).astype(BF16).astype(F32)
-        pieces += [high, middle, value - high - middle]
-    row16 = lax.broadcasted_iota(jnp.int32, (16, stations), 0)
-    left = jnp.zeros((16, stations), F32)
-    for at, piece in enumerate(pieces):
-        left = jnp.where(row16 == at, piece, left)
-    spread = lax.dot_general(
-        left.astype(BF16), hot, (((1,), (1,)), ((), ())), preferred_element_type=F32
-    )
-    gains[0:1, :] = spread[0:1] + spread[1:2] + spread[2:3]
-    gains[1:2, :] = spread[3:4] + spread[4:5] + spread[5:6]
-
     mode = lax.broadcasted_iota(jnp.int32, (MODES, LANES), 0)
     lane_half = lax.broadcasted_iota(jnp.int32, (1, LANES), 1) < GROUP
 
-    def tile(t, carry):
+    key = rank if by_flip else 0
+    ahead = early_tiles(tiles)
+    rest = tiles - ahead
+
+    def tile(t, get_sides):
         row = first_row + 2 * t
         first, second = row_groups_of(row, groups)
         station = first * GROUP + (row & 63)
@@ -524,26 +584,50 @@
         mod_re = model[pl.ds(start, FREQ_CHANNELS), :].astype(F32) + fitted[:, 0:LANES]
         mod_im = model[pl.ds(start + FREQ_CHANNELS, FREQ_CHANNELS), :].astype(F32)
         mod_im = mod_im + fitted[:, LANES : 2 * LANES]
-        obs_re, obs_im = data_sides(observed, tiles, t)
+        obs_re, obs_im = get_sides()
         weight = tile_weights(groups, tiles, first_row, t, kept)
         left_re = weight * (obs_re - (prod_re * mod_re - prod_im * mod_im))
         left_im = weight * (obs_im - (prod_re * mod_im + prod_im * mod_re))
         left_out[0, 0, :, tile_lanes(t)] = left_re.astype(BF16)
         left_out[1, 0, :, tile_lanes(t)] = left_im.astype(BF16)
+
+    def tile_late(t, carry):
+        tile(t, lambda: late_sides(observed, rest, t))
         return carry
 
-    parts = output_parts(tiles)
-    size = tiles // parts
+    def tile_early(t, carry):
+        tile(t, lambda: early_sides(early, key, ahead, t - rest))
+        return carry
+
     copies = []
-    for part in range(parts):
-        lax.fori_loop(part * size, (part + 1) * size, tile, 0, unroll=size)
-        lanes = pl.ds(part * size * LANES, size * LANES)
+    done = 0
+    for part, size in enumerate(output_parts(tiles)):
+        lax.fori_loop(done, done + size, tile_late if done < rest else tile_early, 0, unroll=size)
+        lanes = pl.ds(done * LANES, size * LANES)
         copies.append(
             pltpu.make_async_copy(
                 left_out.at[:, :, :, lanes], residual.at[:, :, :, lanes], out_sems.at[part]
             )
         )
         copies[-1].start()
+        done += size
+    hot = (
+        lax.broadcasted_iota(jnp.int32, (stations, stations), 0) == order[...]
+    ).astype(BF16)
+    pieces = []
+    for value in (gain_re, gain_im):
+        high = value.astype(BF16).astype(F32)
+        middle = (value - high).astype(BF16).astype(F32)
+        pieces += [high, middle, value - high - middle]
+    row16 = lax.broadcasted_iota(jnp.int32, (16, stations), 0)
+    left = jnp.zeros((16, stations), F32)
+    for at, piece in enumerate(pieces):
+        left = jnp.where(row16 == at, piece, left)
+    spread = lax.dot_general(
+        left.astype(BF16), hot, (((1,), (1,)), ((), ())), preferred_element_type=F32
+    )
+    gains[0:1, :] = spread[0:1] + spread[1:2] + spread[2:3]
+    gains[1:2, :] = spread[3:4] + spread[4:5] + spread[5:6]
     for copy in copies:
         copy.wait()
 
@@ -572,6 +656,25 @@
         order += [place ^ distance for place in order]
         distance //= 2
     return order
+
+
+def send_quarters(blocks, wide):
+    quarter = wide // 4
+    return [blocks[0]] + [exchange(blocks[at], at * quarter, wide) for at in (1, 2, 3)]
+
+
+def exchange_early(held, wide, places, predicted):
+    distance = wide // 8
+    held, _ = lax.optimization_barrier((held, places))
+    held = jnp.stack(held)
+    while distance:
+        split = held.reshape(held.shape[0], 2, distance, *held.shape[2:])
+        other = exchange(split[:, 1], distance, wide)
+        other, predicted = lax.optimization_barrier((other, predicted))
+        held = jnp.stack([split[:, 0], other], axis=1)
+        held = held.reshape(-1, distance, *held.shape[3:])
+        distance //= 2
+    return held[:, 0]
 
 
 def gather_stats(stats, wide):
@@ -607,23 +710,53 @@
     kept = kept_baseline_mask.reshape(total // LANES, LANES)
     counts = fitted_mode_count.reshape(tiles, LANES)
 
-    packed = pl.pallas_call(
-        lambda *refs: pack_kernel(wide, base, *refs),
-        out_shape=jax.ShapeDtypeStruct((wide, local_chan, 2 * base + LANES), BF16),
-        in_specs=[pl.BlockSpec(memory_space=pltpu.MemorySpace.HBM)] * 2,
-        out_specs=pl.BlockSpec(memory_space=pltpu.MemorySpace.HBM),
+    ahead = early_tiles(tiles)
+    blocks = visibilities.reshape(2, local_chan, wide, base).transpose(0, 2, 1, 3)
+    hbm = pl.BlockSpec(memory_space=pltpu.MemorySpace.HBM)
+    early_width = 2 * ahead * LANES + LANES
+    early = pl.pallas_call(
+        lambda *refs: pack_early_kernel(wide, base, *refs),
+        out_shape=(jax.ShapeDtypeStruct((wide // 4, local_chan, early_width), BF16),) * 4,
+        in_specs=[hbm] * 2,
+        out_specs=(hbm,) * 4,
         scratch_shapes=[
-            pltpu.VMEM((wide, local_chan, 2 * base + LANES), BF16),
+            pltpu.VMEM((wide, local_chan, early_width), BF16),
             pltpu.SMEM((local_chan,), F32),
-            pltpu.SemaphoreType.DMA((PACK_PARTS, 2)),
-            pltpu.SemaphoreType.DMA((PACK_PARTS,)),
+            pltpu.SemaphoreType.DMA((2,)),
+            pltpu.SemaphoreType.DMA((wide,)),
             pltpu.SemaphoreType.DMA,
         ],
         compiler_params=pltpu.CompilerParams(vmem_limit_bytes=60 << 20),
+        name="pack_early",
+    )(blocks, centre_flux)
+    late_width = 2 * (tiles - ahead) * LANES
+    packed = pl.pallas_call(
+        lambda *refs: pack_kernel(wide, base, *refs),
+        out_shape=jax.ShapeDtypeStruct((wide, local_chan, late_width), BF16),
+        in_specs=[hbm] * 2,
+        out_specs=hbm,
+        scratch_shapes=[
+            pltpu.VMEM((wide, local_chan, late_width), BF16),
+            pltpu.SemaphoreType.DMA((PACK_PARTS, 2)),
+            pltpu.SemaphoreType.DMA((PACK_PARTS,)),
+        ],
+        compiler_params=pltpu.CompilerParams(vmem_limit_bytes=60 << 20),
         name="pack",
-    )(visibilities.reshape(2, local_chan, wide, base).transpose(0, 2, 1, 3), centre_flux)
+    )(blocks, early[0])
+    early = send_quarters(early, wide)
+    packed, early[1] = lax.optimization_barrier((packed, early[1]))
     observed = lax.all_to_all(packed, "wide", 0, 0, tiled=True)
-    observed = observed.reshape(FREQ_CHANNELS // 8, 8, 2 * base + LANES)
+    observed = observed.reshape(FREQ_CHANNELS // 8, 8, late_width)
+    places = call(
+        lambda *refs: places_kernel(groups, tiles, padded, *refs),
+        (jax.ShapeDtypeStruct((rows + LANES, LANES), F32),) * 2,
+        [],
+        "places",
+        [SMEM, SMEM, pltpu.MemorySpace.HBM],
+        12,
+        PLACES_FLOPS,
+        (rows + LANES) * LANES * 8,
+    )(station_order, station_xy.reshape(2, stations), packed)
 
     state_row = pltpu.VMEM((rows, comps), F32)
     state_col = pltpu.VMEM((comps, LANES), F32)
@@ -636,39 +769,46 @@
             jax.ShapeDtypeStruct((tiles * FREQ_CHANNELS, LANES), BF16),
         ),
         [pltpu.VMEM((padded * FREQ_CHANNELS, LANES), F32)] * 2
-        + [pltpu.VMEM((rows + LANES, LANES), F32)] * 2
-        + [state_row] * 4
-        + [state_col] * 4
+        + [state_row] * 6
+        + [state_col] * 6
         + [left, right, left, right],
         "predict",
-        [SMEM, SMEM, VMEM, VMEM],
+        [VMEM] * 4,
         20,
         FREQ_CHANNELS * 2 * 2 * rows * 2 * comps * 256,
         padded * 256 * LANES * 4,
-    )(station_order, station_xy.reshape(2, stations), comp_lm, comp_flux.reshape(1, comps))
+    )(*places, comp_lm, comp_flux.reshape(1, comps))
+    early = exchange_early(early, wide, places[0], real)
+    by_flip = local_chan == 8
+    if not by_flip:
+        early = early[lax.axis_index("wide") ^ jnp.arange(wide)]
+        early = early.reshape(FREQ_CHANNELS // 8, 8, early_width)
     stats, model, modes = call(
-        lambda *refs: stats_kernel(groups, tiles, *refs),
+        lambda *refs: stats_kernel(groups, tiles, by_flip, *refs),
         (
-            jax.ShapeDtypeStruct((stat_groups(tiles) * 8, LANES), BF16),
+            jax.ShapeDtypeStruct((PAIRS * 2 * tiles, LANES), BF16),
             jax.ShapeDtypeStruct((tiles * 2 * FREQ_CHANNELS, LANES), BF16),
             jax.ShapeDtypeStruct((tiles * MODES, 4 * LANES), F32),
         ),
-        [pltpu.VMEM((FREQ_CHANNELS, LANES), F32), pltpu.VMEM((tiles * 8, LANES), F32)],
+        [
+            pltpu.VMEM((FREQ_CHANNELS, LANES), F32),
+            pltpu.VMEM((tiles * 8, LANES), F32),
+            pltpu.VMEM((PAIRS * 2 * tiles, LANES), F32),
+        ],
         "stats",
-        [VMEM] * 6,
+        [VMEM] * 7,
         12,
         moved=tiles * 256 * LANES * 8,
-    )(observed, real, imag, kept, counts, fit)
+    )(observed, early, real, imag, kept, counts, fit)
     gathered = gather_stats(stats, wide)
     gains, residual = call(
-        lambda *refs: solve_kernel(groups, tiles, wide, *refs),
+        lambda *refs: solve_kernel(groups, tiles, by_flip, wide, *refs),
         (
             jax.ShapeDtypeStruct((2, stations), F32),
             jax.ShapeDtypeStruct((2, 1, FREQ_CHANNELS, base), BF16),
         ),
         [
-            pltpu.VMEM((wide * tiles * 8, LANES), F32),
-            pltpu.VMEM((stations // LANES, stations, LANES), F32),
+            pltpu.VMEM((PAIRS, wide * 2 * tiles, LANES), F32),
             pltpu.VMEM((STATS, stations, stations), F32),
             pltpu.VMEM((stations, 3 * stations), BF16),
             pltpu.VMEM((groups, 8, LANES), F32),
@@ -676,10 +816,10 @@
             pltpu.VMEM((ROUNDS, stations, LANES), F32),
             pltpu.VMEM((ROUNDS, stations, LANES), F32),
             pltpu.VMEM((2, 1, FREQ_CHANNELS, base), BF16),
-            pltpu.SemaphoreType.DMA((output_parts(tiles),)),
+            pltpu.SemaphoreType.DMA((len(output_parts(tiles)),)),
         ],
         "solve",
-        [VMEM] * 8,
+        [VMEM] * 9,
         16,
         moved=tiles * 256 * LANES * 6,
         out_specs=(
@@ -689,6 +829,7 @@
     )(
         gathered,
         observed,
+        early,
         model,
         modes,
         kept,

time: 65.6 us -> 63.8 us (0.973)
  waiting for transfers between devices: 15.5 us -> 12.2 us
  starting transfers between devices: 15.5 us -> 18.6 us
  Pallas kernels: 33.3 us -> 31.2 us
    pallas_call x1, Pallas kernels: 23.4 us -> 18.3 us  [body(): call(lambda *refs: predict_kernel(groups, tiles, padded, *refs), (jax.Sha...]
    all_to_all x1, waiting for transfers between devices: 4.49 us -> 0.01 us  [body(): observed = lax.all_to_all(packed, 'wide', 0, 0, tiled=True)]
    ppermute x5 -> x10, starting transfers between devices: 7.93 us -> 12.3 us  [exchange(): return lax.ppermute(block, 'wide', [(i, i ^ distance) for i in range(wide)])]
    pallas_call x2 -> x4, Pallas kernels: 7.66 us -> 10.9 us  [the longest x1 6.07 us: body(): call(lambda *refs: solve_kernel(groups, tiles, by_flip, wide, *refs), (ja...]
    all_to_all x1, starting transfers between devices: 7.53 us -> 6.3 us  [body(): observed = lax.all_to_all(packed, 'wide', 0, 0, tiled=True)]
    ppermute x5 -> x10, waiting for transfers between devices: 11 us -> 12.2 us  [exchange(): return lax.ppermute(block, 'wide', [(i, i ^ distance) for i in range(wide)])]
  transfers between devices with their start and end apart: 6 -> 11, of which waited for: 5 -> 5; matrix products, arithmetic and copies ran while one was open for 0% -> 0% of each run, Pallas kernels for 36% -> 34%
where the time goes in v4:
time: 63.8 us; the launch traced here: 63.5 us
  Pallas kernels  31.2 us (49%)
  starting transfers between devices  18.6 us (29%)
  waiting for transfers between devices  12.2 us (19%)
  between operations  0.95 us (1%)
    pallas_call x1, Pallas kernels, body(): call(lambda *refs: predict_kernel(groups, tiles, padded, *refs), (jax.Sha...  18.3 us
    ppermute x10, starting transfers between devices, exchange(): return lax.ppermute(block, 'wide', [(i, i ^ distance) for i in range(wide)])  12.3 us
    ppermute x10, waiting for transfers between devices, exchange(): return lax.ppermute(block, 'wide', [(i, i ^ distance) for i in range(wide)])  12.2 us
    all_to_all x1, starting transfers between devices, body(): observed = lax.all_to_all(packed, 'wide', 0, 0, tiled=True)  6.3 us
    pallas_call x1, Pallas kernels, body(): call(lambda *refs: solve_kernel(groups, tiles, by_flip, wide, *refs), (ja...  6.07 us
    pallas_call x1, Pallas kernels, body(): pl.pallas_call(lambda *refs: pack_kernel(wide, base, *refs), out_shape=ja...  2.05 us
    pallas_call x1, Pallas kernels, body(): pl.pallas_call(lambda *refs: pack_early_kernel(wide, base, *refs), out_sh...  1.97 us
    pallas_call x1, Pallas kernels, body(): call(lambda *refs: stats_kernel(groups, tiles, by_flip, *refs), (jax.Shap...  1.58 us
  transfers between devices with their start and end apart: 11, of which 5 were waited for; matrix products, arithmetic and copies ran while one was open for 0% of the time, Pallas kernels for 34%

profile of v4, /device:TPU:0, one launch (start us, length us, event | category | flops | bytes accessed | tf_op | source)
XLA Modules:
  0.0 63.5 jit_solution(2759190012924847778)
XLA Ops:
  0.6 2.0 %pack_early.1 = (bf16[4,8,1664]{2,1,0:T(8,128)(2,1)}, bf16[4,8,1664]{2,1,0:T(8,128)(2,1)}, bf16[4,8,1664]{2,1,0:T(8,128)(2,1)}, bf16[4,8,1664]{2,1,0:T(8,128)(2,1)}) custom-call(bf16[2,16,8,2560]{3,2,1,0:T(8,128)(2,1)} %bitcast.46, f32[8]{0:T(128)} %refs_1_.1), custom_call_target="tpu_custom_call" | custom-call | tf_op jit(solution)/shard_map/pack_early/pallas_call | solution.py:717
  2.6 3.1 %collective-permute-start = (bf16[4,8,1664]{2,1,0:T(8,128)(2,1)}, bf16[4,8,1664]{2,1,0:T(8,128)(2,1)S(1)}, u32[]{:S(2)}, u32[]{:S(2)}) collective-permute-start(bf16[4,8,1664]{2,1,0:T(8,128)(2,1)} %get-tuple-element.21), channel_id=1, source_target_pairs={{0,4},{1,5},{2,6},{3,7},{4,0},{5,1},{6,2},{7,3},{8,12},{9,13},{10,... | collective-permute-start | bytes 319496 | tf_op jit(solution)/shard_map/ppermute | solution.py:649
  5.7 2.6 %collective-permute-start.1 = (bf16[4,8,1664]{2,1,0:T(8,128)(2,1)}, bf16[4,8,1664]{2,1,0:T(8,128)(2,1)S(1)}, u32[]{:S(2)}, u32[]{:S(2)}) collective-permute-start(bf16[4,8,1664]{2,1,0:T(8,128)(2,1)} %get-tuple-element.24), channel_id=1, source_target_pairs={{0,8},{1,9},{2,10},{3,11},{4,12},{5,13},{6,14},{7,15},{8,0},{9,1},... | collective-permute-start | bytes 319496 | tf_op jit(solution)/shard_map/ppermute | solution.py:649
  8.3 2.0 %pack.1.refs_2_ = bf16[16,8,3584]{2,1,0:T(8,128)(2,1)} custom-call(bf16[2,16,8,2560]{3,2,1,0:T(8,128)(2,1)} %bitcast.47, bf16[4,8,1664]{2,1,0:T(8,128)(2,1)} %get-tuple-element.27.refs_1_), custom_call_target="tpu_custom_call" | custom-call | tf_op jit(solution)/shard_map/pack/pallas_call | solution.py:733
  10.4 6.3 %all-to-all-start = ((bf16[16,8,3584]{2,1,0:T(8,128)(2,1)}), bf16[16,8,3584]{2,1,0:T(8,128)(2,1)S(1)}, u32[]{:S(2)}, u32[]{:S(2)}) async-start(bf16[16,8,3584]{2,1,0:T(8,128)(2,1)} %pack.1.refs_2_), calls=%async_computation | async-start | bytes 1835008 | tf_op jit(solution)/shard_map/all_to_all | solution.py:748
  16.7 1.3 %places.1 = (f32[176,128]{1,0:T(8,128)S(1)}, f32[176,128]{1,0:T(8,128)S(1)}) custom-call(s32[256]{0:T(256)S(1)} %copy-done.5, f32[2,256]{1,0:T(2,128)S(1)} %bitcast.44, bf16[16,8,3584]{2,1,0:T(8,128)(2,1)S(1)} %copy-done), custom_call_target="tpu_custom_call" | custom-call | flops 4000000000 | bytes 180224 | tf_op jit(solution)/shard_map/places/pallas_call | solution.py:750
  18.1 0.1 pad_maximum_fusion
  18.2 2.0 %collective-permute-start.3 = (bf16[4,2,8,1664]{3,2,1,0:T(8,128)(2,1)S(1)}, bf16[4,2,8,1664]{3,2,1,0:T(8,128)(2,1)S(1)}, u32[]{:S(2)}, u32[]{:S(2)}) collective-permute-start(bf16[4,2,8,1664]{3,2,1,0:T(8,128)(2,1)S(1)} %get-tuple-element.41), channel_id=1, source_target_pairs={{0,2},{1,3},{2,0},{3,1},{4,6},{5,7},{6,4},{7,5},{8,10},{9,11},{10,... | collective-permute-start | bytes 638984 | tf_op jit(solution)/shard_map/ppermute | solution.py:649
  20.2 18.3 %predict.1 = (f32[2560,128]{1,0:T(8,128)S(1)}, bf16[2560,128]{1,0:T(8,128)(2,1)S(1)}) custom-call(f32[176,128]{1,0:T(8,128)S(1)} %get-tuple-element.26.refs_0_, f32[176,128]{1,0:T(8,128)S(1)} %get-tuple-element.31.refs_1_, f32[2,512]{1,0:T(2,128)S(1)} %copy-done.6, f32[1,512]{1,0:T(1,128)S(1)} %bitcast.45), custom_call_target="tpu_custom_call" | custom-call | flops 6442450944 | bytes 3145728 | tf_op jit(solution)/shard_map/predict/pallas_call | solution.py:765
  38.6 0.0 copy-start.4
  38.7 0.1 collective-permute-start.4
  38.8 1.5 %collective-permute-done.4 = bf16[8,1,8,1664]{3,2,0,1:T(8,128)(2,1)S(1)} collective-permute-done((bf16[8,1,8,1664]{3,2,0,1:T(8,128)(2,1)S(1)}, bf16[8,1,8,1664]{3,2,0,1:T(8,128)(2,1)S(1)}, u32[]{:S(2)}, u32[]{:S(2)}) %collective-permute-start.4) | collective-permute-done | bytes 213024 | tf_op jit(solution)/shard_map/ppermute | solution.py:649
  40.3 1.6 %stats.1 = (bf16[160,128]{1,0:T(8,128)(2,1)S(1)}, bf16[5120,128]{1,0:T(8,128)(2,1)S(1)}, f32[320,512]{1,0:T(8,128)S(1)}) custom-call(bf16[16,8,3584]{2,1,0:T(8,128)(2,1)S(1)} %all-to-all-done.refs_0_.refs_1_, bf16[16,8,1664]{2,1,0:T(8,128)(2,1)S(1)} %bitcast.36, f32[2560,128]{1,0:T(8,128)S(1)} %get-tuple-element.32.refs_2_, ...), custom_call_target="tpu_custom_call" | custom-call | bytes 5242880 | tf_op jit(solution)/shard_map/stats/pallas_call | solution.py:786
  41.9 2.4 %collective-permute-start.5 = (bf16[160,128]{1,0:T(8,128)(2,1)S(1)}, bf16[160,128]{1,0:T(8,128)(2,1)S(1)}, u32[]{:S(2)}, u32[]{:S(2)}) collective-permute-start(bf16[160,128]{1,0:T(8,128)(2,1)S(1)} %get-tuple-element.35), channel_id=1, source_target_pairs={{0,8},{1,9},{2,10},{3,11},{4,12},{5,13},{6,14},{7,15},{8,0},{9,1},... | collective-permute-start | bytes 122888 | tf_op jit(solution)/shard_map/ppermute | solution.py:649
  44.3 1.5 %collective-permute-start.6 = (bf16[160,128]{1,0:T(8,128)(2,1)S(1)}, bf16[160,128]{1,0:T(8,128)(2,1)S(1)}, u32[]{:S(2)}, u32[]{:S(2)}) collective-permute-start(bf16[160,128]{1,0:T(8,128)(2,1)S(1)} %get-tuple-element.35), channel_id=1, source_target_pairs={{0,12},{1,13},{2,14},{3,15},{4,8},{5,9},{6,10},{7,11},{8,4},{9,5},... | collective-permute-start | bytes 122888 | tf_op jit(solution)/shard_map/ppermute | solution.py:649
  45.8 0.0 collective-permute-start.7
  45.8 1.5 %collective-permute-done.5 = bf16[160,128]{1,0:T(8,128)(2,1)S(1)} collective-permute-done((bf16[160,128]{1,0:T(8,128)(2,1)S(1)}, bf16[160,128]{1,0:T(8,128)(2,1)S(1)}, u32[]{:S(2)}, u32[]{:S(2)}) %collective-permute-start.5) | collective-permute-done | bytes 40992 | tf_op jit(solution)/shard_map/ppermute | solution.py:649
  47.3 2.9 %collective-permute-done.6 = bf16[160,128]{1,0:T(8,128)(2,1)S(1)} collective-permute-done((bf16[160,128]{1,0:T(8,128)(2,1)S(1)}, bf16[160,128]{1,0:T(8,128)(2,1)S(1)}, u32[]{:S(2)}, u32[]{:S(2)}) %collective-permute-start.6) | collective-permute-done | bytes 40992 | tf_op jit(solution)/shard_map/ppermute | solution.py:649
  50.3 0.6 collective-permute-start.8
  51.0 4.7 %collective-permute-done.8 = bf16[4,160,128]{2,1,0:T(8,128)(2,1)S(1)} collective-permute-done((bf16[4,160,128]{2,1,0:T(8,128)(2,1)S(1)}, bf16[4,160,128]{2,1,0:T(8,128)(2,1)S(1)}, u32[]{:S(2)}, u32[]{:S(2)}) %collective-permute-start.8) | collective-permute-done | bytes 163872 | tf_op jit(solution)/shard_map/ppermute | solution.py:649
  55.7 0.1 constant_dynamic-update-slice_fusion
  55.7 0.1 collective-permute-start.9
  55.8 1.6 %collective-permute-done.9 = bf16[8,160,128]{2,1,0:T(8,128)(2,1)S(1)} collective-permute-done((bf16[8,160,128]{2,1,0:T(8,128)(2,1)S(1)}, bf16[8,160,128]{2,1,0:T(8,128)(2,1)S(1)}, u32[]{:S(2)}, u32[]{:S(2)}) %collective-permute-start.9) | collective-permute-done | bytes 327712 | tf_op jit(solution)/shard_map/ppermute | solution.py:649
  57.5 6.1 %solve.1 = (f32[2,256]{1,0:T(2,128)}, bf16[2,1,128,2560]{3,2,1,0:T(8,128)(2,1)}) custom-call(bf16[16,160,128]{2,1,0:T(8,128)(2,1)S(1)} %constant_dynamic-update-slice_fusion.5.refs_0_, bf16[16,8,3584]{2,1,0:T(8,128)(2,1)S(1)} %all-to-all-done.refs_0_.refs_1_, bf16[16,8,1664]{2,1,0:T(8,128)(2,1)S(1)} %bitcast.37, ...), custom_call_target="tpu_custom_call" | custom-call | bytes 3932160 | tf_op jit(solution)/shard_map/solve/pallas_call | solution.py:804
  (37 shorter events, 0.4 us)
Async XLA Ops:
  2.6 7.8 %collective-permute-start = (bf16[4,8,1664]{2,1,0:T(8,128)(2,1)}, bf16[4,8,1664]{2,1,0:T(8,128)(2,1)S(1)}, u32[]{:S(2)}, u32[]{:S(2)}) collective-permute-start(bf16[4,8,1664]{2,1,0:T(8,128)(2,1)} %get-tuple-element.21), channel_id=1, source_target_pairs={{0,4},{1,5},{2,6},{3,7},{4,0},{5,1},{6,2},{7,3},{8,12},{9,13},{10,... | collective-permute-start | bytes 319496 | tf_op jit(solution)/shard_map/ppermute | solution.py:649
  5.7 12.3 %collective-permute-start.1 = (bf16[4,8,1664]{2,1,0:T(8,128)(2,1)}, bf16[4,8,1664]{2,1,0:T(8,128)(2,1)S(1)}, u32[]{:S(2)}, u32[]{:S(2)}) collective-permute-start(bf16[4,8,1664]{2,1,0:T(8,128)(2,1)} %get-tuple-element.24), channel_id=1, source_target_pairs={{0,8},{1,9},{2,10},{3,11},{4,12},{5,13},{6,14},{7,15},{8,0},{9,1},... | collective-permute-start | bytes 319496 | tf_op jit(solution)/shard_map/ppermute | solution.py:649
  8.3 9.8 %collective-permute-start.2 = (bf16[4,8,1664]{2,1,0:T(8,128)(2,1)}, bf16[4,8,1664]{2,1,0:T(8,128)(2,1)S(1)}, u32[]{:S(2)}, u32[]{:S(2)}) collective-permute-start(bf16[4,8,1664]{2,1,0:T(8,128)(2,1)} %get-tuple-element.25), channel_id=1, source_target_pairs={{0,12},{1,13},{2,14},{3,15},{4,8},{5,9},{6,10},{7,11},{8,4},{9,5},... | collective-permute-start | bytes 319496 | tf_op jit(solution)/shard_map/ppermute | solution.py:649
  10.3 6.4 %copy-start = (bf16[16,8,3584]{2,1,0:T(8,128)(2,1)S(1)}, bf16[16,8,3584]{2,1,0:T(8,128)(2,1)}, u32[]{:S(2)}) copy-start(bf16[16,8,3584]{2,1,0:T(8,128)(2,1)} %pack.1.refs_2_) | copy-start | bytes 2752516
  10.4 6.4 %copy-start.5 = (s32[256]{0:T(256)S(1)}, s32[256]{0:T(256)}, u32[]{:S(2)}) copy-start(s32[256]{0:T(256)} %refs_0_.1) | copy-start | bytes 3076
  10.4 6.4 %copy-start.7 = (f32[1,2,256]{2,1,0:T(2,128)S(1)}, f32[1,2,256]{2,1,0:T(2,128)}, u32[]{:S(2)}) copy-start(f32[1,2,256]{2,1,0:T(2,128)} %param.14) | copy-start | bytes 6148
  10.4 29.9 %all-to-all-start = ((bf16[16,8,3584]{2,1,0:T(8,128)(2,1)}), bf16[16,8,3584]{2,1,0:T(8,128)(2,1)S(1)}, u32[]{:S(2)}, u32[]{:S(2)}) async-start(bf16[16,8,3584]{2,1,0:T(8,128)(2,1)} %pack.1.refs_2_), calls=%async_computation | async-start | bytes 1835008 | tf_op jit(solution)/shard_map/all_to_all | solution.py:748
  16.7 1.3 %copy-start.9 = (bf16[4,8,1664]{2,1,0:T(8,128)(2,1)S(1)}, bf16[4,8,1664]{2,1,0:T(8,128)(2,1)}, u32[]{:S(2)}) copy-start(bf16[4,8,1664]{2,1,0:T(8,128)(2,1)} %get-tuple-element.27.refs_1_) | copy-start | bytes 319492
  18.0 2.2 %copy-start.6 = (f32[2,512]{1,0:T(2,128)S(1)}, f32[2,512]{1,0:T(2,128)}, u32[]{:S(2)}) copy-start(f32[2,512]{1,0:T(2,128)} %refs_2_.1) | copy-start | bytes 12292
  18.0 2.2 %copy-start.8 = (f32[512]{0:T(512)S(1)}, f32[512]{0:T(512)}, u32[]{:S(2)}) copy-start(f32[512]{0:T(512)} %param.16) | copy-start | bytes 6148
  18.2 20.3 %collective-permute-start.3 = (bf16[4,2,8,1664]{3,2,1,0:T(8,128)(2,1)S(1)}, bf16[4,2,8,1664]{3,2,1,0:T(8,128)(2,1)S(1)}, u32[]{:S(2)}, u32[]{:S(2)}) collective-permute-start(bf16[4,2,8,1664]{3,2,1,0:T(8,128)(2,1)S(1)} %get-tuple-element.41), channel_id=1, source_target_pairs={{0,2},{1,3},{2,0},{3,1},{4,6},{5,7},{6,4},{7,5},{8,10},{9,11},{10,... | collective-permute-start | bytes 638984 | tf_op jit(solution)/shard_map/ppermute | solution.py:649
  38.6 1.7 %copy-start.1 = (s32[40960]{0:T(1024)S(1)}, s32[40960]{0:T(1024)}, u32[]{:S(2)}) copy-start(s32[40960]{0:T(1024)} %param.11) | copy-start | bytes 491524
  38.6 1.7 %copy-start.2 = (s32[2560]{0:T(1024)S(1)}, s32[2560]{0:T(1024)}, u32[]{:S(2)}) copy-start(s32[2560]{0:T(1024)} %param.12) | copy-start | bytes 30724
  38.6 1.7 %copy-start.4 = (bf16[32,128]{1,0:T(8,128)(2,1)S(1)}, bf16[32,128]{1,0:T(8,128)(2,1)}, u32[]{:S(2)}) copy-start(bf16[32,128]{1,0:T(8,128)(2,1)} %constant.4.clone.refs_6_) | copy-start | bytes 24580
  38.7 1.5 %collective-permute-start.4 = (bf16[8,1,8,1664]{3,2,0,1:T(8,128)(2,1)S(1)}, bf16[8,1,8,1664]{3,2,0,1:T(8,128)(2,1)S(1)}, u32[]{:S(2)}, u32[]{:S(2)}) collective-permute-start(bf16[8,1,8,1664]{3,2,0,1:T(8,128)(2,1)S(1)} %get-tuple-element.39), channel_id=1, source_target_pairs={{0,1},{1,0},{2,3},{3,2},{4,5},{5,4},{6,7},{7,6},{8,9},{9,8},{10,11... | collective-permute-start | bytes 638984 | tf_op jit(solution)/shard_map/ppermute | solution.py:649
  41.9 15.6 %copy-start.3 = (bf16[128,48]{1,0:T(8,128)(2,1)S(1)}, bf16[128,48]{1,0:T(8,128)(2,1)}, u32[]{:S(2)}) copy-start(bf16[128,48]{1,0:T(8,128)(2,1)} %constant.5.clone.refs_8_) | copy-start | bytes 36868
  41.9 5.4 %collective-permute-start.5 = (bf16[160,128]{1,0:T(8,128)(2,1)S(1)}, bf16[160,128]{1,0:T(8,128)(2,1)S(1)}, u32[]{:S(2)}, u32[]{:S(2)}) collective-permute-start(bf16[160,128]{1,0:T(8,128)(2,1)S(1)} %get-tuple-element.35), channel_id=1, source_target_pairs={{0,8},{1,9},{2,10},{3,11},{4,12},{5,13},{6,14},{7,15},{8,0},{9,1},... | collective-permute-start | bytes 122888 | tf_op jit(solution)/shard_map/ppermute | solution.py:649
  44.3 5.9 %collective-permute-start.6 = (bf16[160,128]{1,0:T(8,128)(2,1)S(1)}, bf16[160,128]{1,0:T(8,128)(2,1)S(1)}, u32[]{:S(2)}, u32[]{:S(2)}) collective-permute-start(bf16[160,128]{1,0:T(8,128)(2,1)S(1)} %get-tuple-element.35), channel_id=1, source_target_pairs={{0,12},{1,13},{2,14},{3,15},{4,8},{5,9},{6,10},{7,11},{8,4},{9,5},... | collective-permute-start | bytes 122888 | tf_op jit(solution)/shard_map/ppermute | solution.py:649
  45.8 4.4 %collective-permute-start.7 = (bf16[160,128]{1,0:T(8,128)(2,1)S(1)}, bf16[160,128]{1,0:T(8,128)(2,1)S(1)}, u32[]{:S(2)}, u32[]{:S(2)}) collective-permute-start(bf16[160,128]{1,0:T(8,128)(2,1)S(1)} %get-tuple-element.35), channel_id=1, source_target_pairs={{0,4},{1,5},{2,6},{3,7},{4,0},{5,1},{6,2},{7,3},{8,12},{9,13},{10,... | collective-permute-start | bytes 122888 | tf_op jit(solution)/shard_map/ppermute | solution.py:649
  50.3 5.4 %collective-permute-start.8 = (bf16[4,160,128]{2,1,0:T(8,128)(2,1)S(1)}, bf16[4,160,128]{2,1,0:T(8,128)(2,1)S(1)}, u32[]{:S(2)}, u32[]{:S(2)}) collective-permute-start(bf16[4,160,128]{2,1,0:T(8,128)(2,1)S(1)} %pad_maximum_fusion.3), channel_id=1, source_target_pairs={{0,2},{1,3},{2,0},{3,1},{4,6},{5,7},{6,4},{7,5},{8,10},{9,11},{10,... | collective-permute-start | bytes 491528 | tf_op jit(solution)/shard_map/ppermute | solution.py:649
  55.7 1.7 %collective-permute-start.9 = (bf16[8,160,128]{2,1,0:T(8,128)(2,1)S(1)}, bf16[8,160,128]{2,1,0:T(8,128)(2,1)S(1)}, u32[]{:S(2)}, u32[]{:S(2)}) collective-permute-start(bf16[8,160,128]{2,1,0:T(8,128)(2,1)S(1)} %get-tuple-element.42), channel_id=1, source_target_pairs={{0,1},{1,0},{2,3},{3,2},{4,5},{5,4},{6,7},{7,6},{8,9},{9,8},{10,11... | collective-permute-start | bytes 983048 | tf_op jit(solution)/shard_map/ppermute | solution.py:649

commit v5 on v4

--- a/solution.py
+++ b/solution.py
@@ -84,9 +84,8 @@
     return tiles * 3 // 10
 
 
-def pack_early_kernel(wide, base, source, centre, *rest):
-    targets, (held, flux, in_sems, out_sems, flux_sem) = rest[:4], rest[4:]
-    chan = centre.shape[0]
+def pack_early_kernel(wide, base, source, *rest):
+    targets, (held, in_sems, out_sems) = rest[:4], rest[4:]
     rank = lax.axis_index("wide")
     quarter = wide // 4
     late = base - early_tiles(base // LANES) * LANES
@@ -99,23 +98,8 @@
         )
         for side in range(2)
     ]
-    fetch = pltpu.make_async_copy(centre, flux, flux_sem)
-    fetch.start()
     for copy in bring:
         copy.start()
-    fetch.wait()
-    row = lax.broadcasted_iota(jnp.int32, (chan, LANES), 0)
-    lane = lax.broadcasted_iota(jnp.int32, (chan, LANES), 1)
-    value = jnp.zeros(row.shape, F32)
-    for c in range(chan):
-        value = jnp.where(row == c, flux[c], value)
-    high = value.astype(BF16).astype(F32)
-    middle = (value - high).astype(BF16).astype(F32)
-    low = value - high - middle
-    parts = jnp.where(lane == 0, high, jnp.where(lane == 1, middle, jnp.where(lane == 2, low, 0.0)))
-    held[:, :, 2 * size : 2 * size + LANES] = jnp.broadcast_to(
-        parts.astype(BF16)[None], (wide, chan, LANES)
-    )
     for copy in bring:
         copy.wait()
     send = [
@@ -130,8 +114,9 @@
         copy.wait()
 
 
-def pack_kernel(wide, base, source, after, target, held, in_sems, out_sems):
+def pack_kernel(wide, base, source, centre, after, target, held, flux, in_sems, out_sems, flux_sem):
     del after
+    chan = centre.shape[0]
     size = base - early_tiles(base // LANES) * LANES
     share = wide // PACK_PARTS
     peers = [pl.ds(part * share, share) for part in range(PACK_PARTS)]
@@ -150,9 +135,24 @@
         pltpu.make_async_copy(held.at[peers[part]], target.at[peers[part]], out_sems.at[part])
         for part in range(PACK_PARTS)
     ]
+    fetch = pltpu.make_async_copy(centre, flux, flux_sem)
+    fetch.start()
     for pair in bring:
         for copy in pair:
             copy.start()
+    fetch.wait()
+    row = lax.broadcasted_iota(jnp.int32, (chan, LANES), 0)
+    lane = lax.broadcasted_iota(jnp.int32, (chan, LANES), 1)
+    value = jnp.zeros(row.shape, F32)
+    for c in range(chan):
+        value = jnp.where(row == c, flux[c], value)
+    high = value.astype(BF16).astype(F32)
+    middle = (value - high).astype(BF16).astype(F32)
+    low = value - high - middle
+    parts = jnp.where(lane == 0, high, jnp.where(lane == 1, middle, jnp.where(lane == 2, low, 0.0)))
+    held[:, :, 2 * size : 2 * size + LANES] = jnp.broadcast_to(
+        parts.astype(BF16)[None], (wide, chan, LANES)
+    )
     for pair, copy in zip(bring, send):
         for came in pair:
             came.wait()
@@ -348,23 +348,16 @@
     return [early_lanes(early, key, tile_lanes(t, LANES, side * tiles * LANES)) for side in range(2)]
 
 
-def stats_kernel(
-    groups, tiles, by_flip, observed, early, real, imag, kept, counts, fit, stats, model, modes, shift, rows, paired
-):
-    rank = lax.axis_index("wide")
-    first_row = rank * (2 * tiles)
+def tile_stats(groups, tiles, begin, count, sides_of, shift, real, imag, kept, counts, fit, model, modes, rows):
+    first_row = lax.axis_index("wide") * (2 * tiles)
     mode = lax.broadcasted_iota(jnp.int32, (MODES, LANES), 0)
-    key = rank if by_flip else 0
-    ahead = early_tiles(tiles)
-    rest = tiles - ahead
-    tail = early_lanes(early, key, pl.ds(2 * ahead * LANES, LANES))
-    shift[...] = jnp.broadcast_to(jnp.sum(tail, axis=1, keepdims=True), tail.shape)
-
-    def one(t, sides):
-        obs_re, obs_im = sides
+
+    def one(at, carry):
+        t = begin + at
+        obs_re, obs_im = sides_of(at)
         half = tile_lanes(t, FREQ_CHANNELS)
         mod_re16, mod_im16 = (real[half, :] + shift[...]).astype(BF16), imag[half, :]
-        both = pl.multiple_of(2 * t * FREQ_CHANNELS, FREQ_CHANNELS)
+        both = pl.multiple_of(2 * at * FREQ_CHANNELS, FREQ_CHANNELS)
         model[pl.ds(both, FREQ_CHANNELS), :] = mod_re16
         model[pl.ds(both + FREQ_CHANNELS, FREQ_CHANNELS), :] = mod_im16
         mod_re, mod_im = mod_re16.astype(F32), mod_im16.astype(F32)
@@ -378,7 +371,7 @@
         sides = [obs_re.astype(BF16), obs_im.astype(BF16), mod_re16, mod_im16]
         raw = jnp.dot(fit[...], jnp.concatenate(sides, axis=1), preferred_element_type=F32)
         raw = raw[0:MODES] + raw[MODES : 2 * MODES]
-        modes[tile_lanes(t, MODES), :] = raw
+        modes[tile_lanes(at, MODES), :] = raw
         v_re, v_im, m_re, m_im = (raw[:, LANES * i : LANES * (i + 1)] for i in range(4))
         inside = (mode < counts[pl.ds(t, 1), :]).astype(F32)
         vv = total(inside * (v_re * v_re + v_im * v_im))
@@ -387,18 +380,54 @@
         mm = total(inside * (m_re * m_re + m_im * m_im))
         weight = tile_weights(groups, tiles, first_row, t, kept)
         parts = [cross_re, cross_im, vv, vm_re, vm_im, power, mm, jnp.zeros((1, LANES), F32)]
-        rows[tile_lanes(t, 8), :] = jnp.concatenate(parts) * weight
-
-    def one_late(t, carry):
-        one(t, late_sides(observed, rest, t))
+        rows[tile_lanes(at, 8), :] = jnp.concatenate(parts) * weight
         return carry
 
-    def one_early(t, carry):
-        one(rest + t, early_sides(early, key, ahead, t))
-        return carry
-
-    lax.fori_loop(0, rest, one_late, 0, unroll=rest // 2 if rest % 2 == 0 else rest)
-    lax.fori_loop(0, ahead, one_early, 0, unroll=ahead)
+    lax.fori_loop(0, count, one, 0, unroll=count)
+
+
+def late_stats_kernel(
+    groups, tiles, observed, real, imag, kept, counts, fit, rows, model, modes, shift
+):
+    rest = tiles - early_tiles(tiles)
+    tail = observed[:, :, 2 * rest * LANES : (2 * rest + 1) * LANES].astype(F32)
+    tail = tail.reshape(FREQ_CHANNELS, LANES)
+    shift[...] = jnp.broadcast_to(jnp.sum(tail, axis=1, keepdims=True), tail.shape)
+
+    def sides(at):
+        return late_sides(observed, rest, at)
+
+    tile_stats(groups, tiles, 0, rest, sides, shift, real, imag, kept, counts, fit, model, modes, rows)
+
+
+def early_stats_kernel(
+    groups,
+    tiles,
+    by_flip,
+    early,
+    late_rows,
+    shift,
+    real,
+    imag,
+    kept,
+    counts,
+    fit,
+    stats,
+    model,
+    modes,
+    rows,
+    paired,
+):
+    key = lax.axis_index("wide") if by_flip else 0
+    ahead = early_tiles(tiles)
+    rest = tiles - ahead
+    rows[0 : 8 * rest, :] = late_rows[...]
+
+    def sides(at):
+        return early_sides(early, key, ahead, at)
+
+    late = rows.at[8 * rest : 8 * tiles]
+    tile_stats(groups, tiles, rest, ahead, sides, shift, real, imag, kept, counts, fit, model, modes, late)
     first_half = lax.broadcasted_iota(jnp.int32, (tiles, LANES), 1) < GROUP
     for pair in range(PAIRS):
         one_stat = rows[pl.ds(2 * pair, tiles, stride=8), :]
@@ -418,8 +447,10 @@
     gathered,
     observed,
     early,
-    model,
-    modes,
+    late_model,
+    early_model,
+    late_modes,
+    early_modes,
     kept,
     counts,
     order,
@@ -546,7 +577,7 @@
     ahead = early_tiles(tiles)
     rest = tiles - ahead
 
-    def tile(t, get_sides):
+    def tile(t, at, get_sides, model, modes):
         row = first_row + 2 * t
         first, second = row_groups_of(row, groups)
         station = first * GROUP + (row & 63)
@@ -570,7 +601,7 @@
             b_re, b_im = rest_re * b_re - rest_im * b_im, rest_re * b_im + rest_im * b_re
         b_re = b_re - 1.0
         inside = (mode < counts[pl.ds(t, 1), :]).astype(F32)
-        raw = modes[tile_lanes(t, MODES), :]
+        raw = modes[tile_lanes(at, MODES), :]
         v_re, v_im, m_re, m_im = (raw[:, LANES * i : LANES * (i + 1)] for i in range(4))
         f_re = inside * (a_re * v_re - a_im * v_im + b_re * m_re - b_im * m_im)
         f_im = inside * (a_re * v_im + a_im * v_re + b_re * m_im + b_im * m_re)
@@ -580,7 +611,7 @@
         fitted = jnp.dot(
             expand[...], jnp.concatenate([high, low, high]), preferred_element_type=F32
         )
-        start = pl.multiple_of(2 * t * FREQ_CHANNELS, FREQ_CHANNELS)
+        start = pl.multiple_of(2 * at * FREQ_CHANNELS, FREQ_CHANNELS)
         mod_re = model[pl.ds(start, FREQ_CHANNELS), :].astype(F32) + fitted[:, 0:LANES]
         mod_im = model[pl.ds(start + FREQ_CHANNELS, FREQ_CHANNELS), :].astype(F32)
         mod_im = mod_im + fitted[:, LANES : 2 * LANES]
@@ -592,11 +623,12 @@
         left_out[1, 0, :, tile_lanes(t)] = left_im.astype(BF16)
 
     def tile_late(t, carry):
-        tile(t, lambda: late_sides(observed, rest, t))
+        tile(t, t, lambda: late_sides(observed, rest, t), late_model, late_modes)
         return carry
 
     def tile_early(t, carry):
-        tile(t, lambda: early_sides(early, key, ahead, t - rest))
+        at = t - rest
+        tile(t, at, lambda: early_sides(early, key, ahead, at), early_model, early_modes)
         return carry
 
     copies = []
@@ -713,36 +745,36 @@
     ahead = early_tiles(tiles)
     blocks = visibilities.reshape(2, local_chan, wide, base).transpose(0, 2, 1, 3)
     hbm = pl.BlockSpec(memory_space=pltpu.MemorySpace.HBM)
-    early_width = 2 * ahead * LANES + LANES
+    early_width = 2 * ahead * LANES
     early = pl.pallas_call(
         lambda *refs: pack_early_kernel(wide, base, *refs),
         out_shape=(jax.ShapeDtypeStruct((wide // 4, local_chan, early_width), BF16),) * 4,
-        in_specs=[hbm] * 2,
+        in_specs=[hbm],
         out_specs=(hbm,) * 4,
         scratch_shapes=[
             pltpu.VMEM((wide, local_chan, early_width), BF16),
-            pltpu.SMEM((local_chan,), F32),
             pltpu.SemaphoreType.DMA((2,)),
             pltpu.SemaphoreType.DMA((wide,)),
+        ],
+        compiler_params=pltpu.CompilerParams(vmem_limit_bytes=60 << 20),
+        name="pack_early",
+    )(blocks)
+    late_width = 2 * (tiles - ahead) * LANES + LANES
+    packed = pl.pallas_call(
+        lambda *refs: pack_kernel(wide, base, *refs),
+        out_shape=jax.ShapeDtypeStruct((wide, local_chan, late_width), BF16),
+        in_specs=[hbm] * 3,
+        out_specs=hbm,
+        scratch_shapes=[
+            pltpu.VMEM((wide, local_chan, late_width), BF16),
+            pltpu.SMEM((local_chan,), F32),
+            pltpu.SemaphoreType.DMA((PACK_PARTS, 2)),
+            pltpu.SemaphoreType.DMA((PACK_PARTS,)),
             pltpu.SemaphoreType.DMA,
         ],
         compiler_params=pltpu.CompilerParams(vmem_limit_bytes=60 << 20),
-        name="pack_early",
-    )(blocks, centre_flux)
-    late_width = 2 * (tiles - ahead) * LANES
-    packed = pl.pallas_call(
-        lambda *refs: pack_kernel(wide, base, *refs),
-        out_shape=jax.ShapeDtypeStruct((wide, local_chan, late_width), BF16),
-        in_specs=[hbm] * 2,
-        out_specs=hbm,
-        scratch_shapes=[
-            pltpu.VMEM((wide, local_chan, late_width), BF16),
-            pltpu.SemaphoreType.DMA((PACK_PARTS, 2)),
-            pltpu.SemaphoreType.DMA((PACK_PARTS,)),
-        ],
-        compiler_params=pltpu.CompilerParams(vmem_limit_bytes=60 << 20),
         name="pack",
-    )(blocks, early[0])
+    )(blocks, centre_flux, early[0])
     early = send_quarters(early, wide)
     packed, early[1] = lax.optimization_barrier((packed, early[1]))
     observed = lax.all_to_all(packed, "wide", 0, 0, tiled=True)
@@ -783,23 +815,36 @@
     if not by_flip:
         early = early[lax.axis_index("wide") ^ jnp.arange(wide)]
         early = early.reshape(FREQ_CHANNELS // 8, 8, early_width)
-    stats, model, modes = call(
-        lambda *refs: stats_kernel(groups, tiles, by_flip, *refs),
+
+    def tables(count):
+        return (
+            jax.ShapeDtypeStruct((count * 2 * FREQ_CHANNELS, LANES), BF16),
+            jax.ShapeDtypeStruct((count * MODES, 4 * LANES), F32),
+        )
+
+    rest = tiles - ahead
+    late_rows, late_model, late_modes, shift = call(
+        lambda *refs: late_stats_kernel(groups, tiles, *refs),
         (
-            jax.ShapeDtypeStruct((PAIRS * 2 * tiles, LANES), BF16),
-            jax.ShapeDtypeStruct((tiles * 2 * FREQ_CHANNELS, LANES), BF16),
-            jax.ShapeDtypeStruct((tiles * MODES, 4 * LANES), F32),
+            jax.ShapeDtypeStruct((rest * 8, LANES), F32),
+            *tables(rest),
+            jax.ShapeDtypeStruct((FREQ_CHANNELS, LANES), F32),
         ),
-        [
-            pltpu.VMEM((FREQ_CHANNELS, LANES), F32),
-            pltpu.VMEM((tiles * 8, LANES), F32),
-            pltpu.VMEM((PAIRS * 2 * tiles, LANES), F32),
-        ],
-        "stats",
-        [VMEM] * 7,
+        [],
+        "late_stats",
+        [VMEM] * 6,
         12,
-        moved=tiles * 256 * LANES * 8,
-    )(observed, early, real, imag, kept, counts, fit)
+        moved=rest * 256 * LANES * 8,
+    )(observed, real, imag, kept, counts, fit)
+    stats, early_model, early_modes = call(
+        lambda *refs: early_stats_kernel(groups, tiles, by_flip, *refs),
+        (jax.ShapeDtypeStruct((PAIRS * 2 * tiles, LANES), BF16), *tables(ahead)),
+        [pltpu.VMEM((tiles * 8, LANES), F32), pltpu.VMEM((PAIRS * 2 * tiles, LANES), F32)],
+        "early_stats",
+        [VMEM] * 8,
+        12,
+        moved=ahead * 256 * LANES * 8,
+    )(early, late_rows, shift, real, imag, kept, counts, fit)
     gathered = gather_stats(stats, wide)
     gains, residual = call(
         lambda *refs: solve_kernel(groups, tiles, by_flip, wide, *refs),
@@ -819,7 +864,7 @@
             pltpu.SemaphoreType.DMA((len(output_parts(tiles)),)),
         ],
         "solve",
-        [VMEM] * 9,
+        [VMEM] * 11,
         16,
         moved=tiles * 256 * LANES * 6,
         out_specs=(
@@ -830,8 +875,10 @@
         gathered,
         observed,
         early,
-        model,
-        modes,
+        late_model,
+        early_model,
+        late_modes,
+        early_modes,
         kept,
         counts,
         station_order.reshape(1, stations),

time: 63.8 us -> 63.6 us (level)
    pallas_call x1 -> x2, Pallas kernels: 1.58 us -> 1.51 us  [the longest x1 1.01 us: body(): call(lambda *refs: late_stats_kernel(groups, tiles, *refs), (jax.ShapeDty...]
where the time goes in v5:
time: 63.6 us; the launch traced here: 63.4 us
  Pallas kernels  31.1 us (49%)
  starting transfers between devices  19 us (30%)
  waiting for transfers between devices  11.9 us (19%)
  between operations  0.95 us (1%)
    pallas_call x1, Pallas kernels, body(): call(lambda *refs: predict_kernel(groups, tiles, padded, *refs), (jax.Sha...  18.3 us
    ppermute x10, starting transfers between devices, exchange(): return lax.ppermute(block, 'wide', [(i, i ^ distance) for i in range(wide)])  12.7 us
    ppermute x10, waiting for transfers between devices, exchange(): return lax.ppermute(block, 'wide', [(i, i ^ distance) for i in range(wide)])  11.8 us
    all_to_all x1, starting transfers between devices, body(): observed = lax.all_to_all(packed, 'wide', 0, 0, tiled=True)  6.3 us
    pallas_call x1, Pallas kernels, body(): call(lambda *refs: solve_kernel(groups, tiles, by_flip, wide, *refs), (ja...  6.06 us
    pallas_call x1, Pallas kernels, body(): pl.pallas_call(lambda *refs: pack_kernel(wide, base, *refs), out_shape=ja...  2.06 us
    pallas_call x1, Pallas kernels, body(): pl.pallas_call(lambda *refs: pack_early_kernel(wide, base, *refs), out_sh...  1.93 us
  transfers between devices with their start and end apart: 11, of which 5 were waited for; matrix products, arithmetic and copies ran while one was open for 0% of the time, Pallas kernels for 34%

profile of v5, /device:TPU:0, one launch (start us, length us, event | category | flops | bytes accessed | tf_op | source)
XLA Modules:
  0.0 63.4 jit_solution(11472264315537510581)
XLA Ops:
  0.6 1.9 %pack_early.1 = (bf16[4,8,1536]{2,1,0:T(8,128)(2,1)}, bf16[4,8,1536]{2,1,0:T(8,128)(2,1)}, bf16[4,8,1536]{2,1,0:T(8,128)(2,1)}, bf16[4,8,1536]{2,1,0:T(8,128)(2,1)}) custom-call(bf16[2,16,8,2560]{3,2,1,0:T(8,128)(2,1)} %bitcast.48), custom_call_target="tpu_custom_call" | custom-call | tf_op jit(solution)/shard_map/pack_early/pallas_call | solution.py:749
  2.6 3.1 %collective-permute-start = (bf16[4,8,1536]{2,1,0:T(8,128)(2,1)}, bf16[4,8,1536]{2,1,0:T(8,128)(2,1)S(1)}, u32[]{:S(2)}, u32[]{:S(2)}) collective-permute-start(bf16[4,8,1536]{2,1,0:T(8,128)(2,1)} %get-tuple-element.25), channel_id=1, source_target_pairs={{0,4},{1,5},{2,6},{3,7},{4,0},{5,1},{6,2},{7,3},{8,12},{9,13},{10,... | collective-permute-start | bytes 294920 | tf_op jit(solution)/shard_map/ppermute | solution.py:681
  5.7 2.6 %collective-permute-start.1 = (bf16[4,8,1536]{2,1,0:T(8,128)(2,1)}, bf16[4,8,1536]{2,1,0:T(8,128)(2,1)S(1)}, u32[]{:S(2)}, u32[]{:S(2)}) collective-permute-start(bf16[4,8,1536]{2,1,0:T(8,128)(2,1)} %get-tuple-element.27), channel_id=1, source_target_pairs={{0,8},{1,9},{2,10},{3,11},{4,12},{5,13},{6,14},{7,15},{8,0},{9,1},... | collective-permute-start | bytes 294920 | tf_op jit(solution)/shard_map/ppermute | solution.py:681
  8.2 2.1 %pack.1.refs_2_ = bf16[16,8,3712]{2,1,0:T(8,128)(2,1)} custom-call(bf16[2,16,8,2560]{3,2,1,0:T(8,128)(2,1)} %bitcast.49, f32[8]{0:T(128)} %refs_1_.1, bf16[4,8,1536]{2,1,0:T(8,128)(2,1)} %get-tuple-element.31.refs_2_), custom_call_target="tpu_custom_call" | custom-call | tf_op jit(solution)/shard_map/pack/pallas_call | solution.py:763
  10.4 6.3 %all-to-all-start = ((bf16[16,8,3712]{2,1,0:T(8,128)(2,1)}), bf16[16,8,3712]{2,1,0:T(8,128)(2,1)S(1)}, u32[]{:S(2)}, u32[]{:S(2)}) async-start(bf16[16,8,3712]{2,1,0:T(8,128)(2,1)} %pack.1.refs_2_), calls=%async_computation | async-start | bytes 1900544 | tf_op jit(solution)/shard_map/all_to_all | solution.py:780
  16.7 1.3 %places.1 = (f32[176,128]{1,0:T(8,128)S(1)}, f32[176,128]{1,0:T(8,128)S(1)}) custom-call(s32[256]{0:T(256)S(1)} %copy-done.5, f32[2,256]{1,0:T(2,128)S(1)} %bitcast.46, bf16[16,8,3712]{2,1,0:T(8,128)(2,1)S(1)} %copy-done), custom_call_target="tpu_custom_call" | custom-call | flops 4000000000 | bytes 180224 | tf_op jit(solution)/shard_map/places/pallas_call | solution.py:782
  18.0 0.1 pad_maximum_fusion
  18.1 2.0 %collective-permute-start.3 = (bf16[4,2,8,1536]{3,2,1,0:T(8,128)(2,1)S(1)}, bf16[4,2,8,1536]{3,2,1,0:T(8,128)(2,1)S(1)}, u32[]{:S(2)}, u32[]{:S(2)}) collective-permute-start(bf16[4,2,8,1536]{3,2,1,0:T(8,128)(2,1)S(1)} %get-tuple-element.49), channel_id=1, source_target_pairs={{0,2},{1,3},{2,0},{3,1},{4,6},{5,7},{6,4},{7,5},{8,10},{9,11},{10,... | collective-permute-start | bytes 589832 | tf_op jit(solution)/shard_map/ppermute | solution.py:681
  20.1 18.3 %predict.1 = (f32[2560,128]{1,0:T(8,128)S(1)}, bf16[2560,128]{1,0:T(8,128)(2,1)S(1)}) custom-call(f32[176,128]{1,0:T(8,128)S(1)} %get-tuple-element.30.refs_0_, f32[176,128]{1,0:T(8,128)S(1)} %get-tuple-element.35.refs_1_, f32[2,512]{1,0:T(2,128)S(1)} %copy-done.6, f32[1,512]{1,0:T(1,128)S(1)} %bitcast.47), custom_call_target="tpu_custom_call" | custom-call | flops 6442450944 | bytes 3145728 | tf_op jit(solution)/shard_map/predict/pallas_call | solution.py:797
  38.6 0.1 collective-permute-start.4
  38.7 1.4 %collective-permute-done.4 = bf16[8,1,8,1536]{3,2,0,1:T(8,128)(2,1)S(1)} collective-permute-done((bf16[8,1,8,1536]{3,2,0,1:T(8,128)(2,1)S(1)}, bf16[8,1,8,1536]{3,2,0,1:T(8,128)(2,1)S(1)}, u32[]{:S(2)}, u32[]{:S(2)}) %collective-permute-start.4) | collective-permute-done | bytes 196640 | tf_op jit(solution)/shard_map/ppermute | solution.py:681
  40.2 1.0 %late_stats.1 = (f32[112,128]{1,0:T(8,128)S(1)}, bf16[3584,128]{1,0:T(8,128)(2,1)S(1)}, f32[224,512]{1,0:T(8,128)S(1)}, f32[128,128]{1,0:T(8,128)S(1)}) custom-call(bf16[16,8,3712]{2,1,0:T(8,128)(2,1)S(1)} %all-to-all-done.refs_0_.refs_1_, f32[2560,128]{1,0:T(8,128)S(1)} %get-tuple-element.36.refs_1_.refs_3_, ...), custom_call_target="tpu_custom_call" | custom-call | bytes 3670016 | tf_op jit(solution)/shard_map/late_stats/pallas_call | solution.py:826
  41.2 0.5 early_stats.1
  41.7 2.4 %collective-permute-start.5 = (bf16[160,128]{1,0:T(8,128)(2,1)S(1)}, bf16[160,128]{1,0:T(8,128)(2,1)S(1)}, u32[]{:S(2)}, u32[]{:S(2)}) collective-permute-start(bf16[160,128]{1,0:T(8,128)(2,1)S(1)} %get-tuple-element.41), channel_id=1, source_target_pairs={{0,8},{1,9},{2,10},{3,11},{4,12},{5,13},{6,14},{7,15},{8,0},{9,1},... | collective-permute-start | bytes 122888 | tf_op jit(solution)/shard_map/ppermute | solution.py:681
  44.2 1.5 %collective-permute-start.6 = (bf16[160,128]{1,0:T(8,128)(2,1)S(1)}, bf16[160,128]{1,0:T(8,128)(2,1)S(1)}, u32[]{:S(2)}, u32[]{:S(2)}) collective-permute-start(bf16[160,128]{1,0:T(8,128)(2,1)S(1)} %get-tuple-element.41), channel_id=1, source_target_pairs={{0,12},{1,13},{2,14},{3,15},{4,8},{5,9},{6,10},{7,11},{8,4},{9,5},... | collective-permute-start | bytes 122888 | tf_op jit(solution)/shard_map/ppermute | solution.py:681
  45.6 0.0 collective-permute-start.7
  45.6 1.5 %collective-permute-done.5 = bf16[160,128]{1,0:T(8,128)(2,1)S(1)} collective-permute-done((bf16[160,128]{1,0:T(8,128)(2,1)S(1)}, bf16[160,128]{1,0:T(8,128)(2,1)S(1)}, u32[]{:S(2)}, u32[]{:S(2)}) %collective-permute-start.5) | collective-permute-done | bytes 40992 | tf_op jit(solution)/shard_map/ppermute | solution.py:681
  47.1 2.9 %collective-permute-done.6 = bf16[160,128]{1,0:T(8,128)(2,1)S(1)} collective-permute-done((bf16[160,128]{1,0:T(8,128)(2,1)S(1)}, bf16[160,128]{1,0:T(8,128)(2,1)S(1)}, u32[]{:S(2)}, u32[]{:S(2)}) %collective-permute-start.6) | collective-permute-done | bytes 40992 | tf_op jit(solution)/shard_map/ppermute | solution.py:681
  50.1 1.0 %collective-permute-start.8 = (bf16[4,160,128]{2,1,0:T(8,128)(2,1)S(1)}, bf16[4,160,128]{2,1,0:T(8,128)(2,1)S(1)}, u32[]{:S(2)}, u32[]{:S(2)}) collective-permute-start(bf16[4,160,128]{2,1,0:T(8,128)(2,1)S(1)} %pad_maximum_fusion.3), channel_id=1, source_target_pairs={{0,2},{1,3},{2,0},{3,1},{4,6},{5,7},{6,4},{7,5},{8,10},{9,11},{10,... | collective-permute-start | bytes 491528 | tf_op jit(solution)/shard_map/ppermute | solution.py:681
  51.1 4.4 %collective-permute-done.8 = bf16[4,160,128]{2,1,0:T(8,128)(2,1)S(1)} collective-permute-done((bf16[4,160,128]{2,1,0:T(8,128)(2,1)S(1)}, bf16[4,160,128]{2,1,0:T(8,128)(2,1)S(1)}, u32[]{:S(2)}, u32[]{:S(2)}) %collective-permute-start.8) | collective-permute-done | bytes 163872 | tf_op jit(solution)/shard_map/ppermute | solution.py:681
  55.5 0.1 constant_dynamic-update-slice_fusion
  55.6 0.1 collective-permute-start.9
  55.6 1.6 %collective-permute-done.9 = bf16[8,160,128]{2,1,0:T(8,128)(2,1)S(1)} collective-permute-done((bf16[8,160,128]{2,1,0:T(8,128)(2,1)S(1)}, bf16[8,160,128]{2,1,0:T(8,128)(2,1)S(1)}, u32[]{:S(2)}, u32[]{:S(2)}) %collective-permute-start.9) | collective-permute-done | bytes 327712 | tf_op jit(solution)/shard_map/ppermute | solution.py:681
  57.3 6.1 %solve.1 = (f32[2,256]{1,0:T(2,128)}, bf16[2,1,128,2560]{3,2,1,0:T(8,128)(2,1)}) custom-call(bf16[16,160,128]{2,1,0:T(8,128)(2,1)S(1)} %constant_dynamic-update-slice_fusion.5.refs_0_, bf16[16,8,3712]{2,1,0:T(8,128)(2,1)S(1)} %all-to-all-done.refs_0_.refs_1_, bf16[16,8,1536]{2,1,0:T(8,128)(2,1)S(1)} %bitcast.37, ...), custom_call_target="tpu_custom_call" | custom-call | bytes 3932160 | tf_op jit(solution)/shard_map/solve/pallas_call | solution.py:849
  (38 shorter events, 0.4 us)
Async XLA Ops:
  2.6 7.8 %collective-permute-start = (bf16[4,8,1536]{2,1,0:T(8,128)(2,1)}, bf16[4,8,1536]{2,1,0:T(8,128)(2,1)S(1)}, u32[]{:S(2)}, u32[]{:S(2)}) collective-permute-start(bf16[4,8,1536]{2,1,0:T(8,128)(2,1)} %get-tuple-element.25), channel_id=1, source_target_pairs={{0,4},{1,5},{2,6},{3,7},{4,0},{5,1},{6,2},{7,3},{8,12},{9,13},{10,... | collective-permute-start | bytes 294920 | tf_op jit(solution)/shard_map/ppermute | solution.py:681
  5.7 12.4 %collective-permute-start.1 = (bf16[4,8,1536]{2,1,0:T(8,128)(2,1)}, bf16[4,8,1536]{2,1,0:T(8,128)(2,1)S(1)}, u32[]{:S(2)}, u32[]{:S(2)}) collective-permute-start(bf16[4,8,1536]{2,1,0:T(8,128)(2,1)} %get-tuple-element.27), channel_id=1, source_target_pairs={{0,8},{1,9},{2,10},{3,11},{4,12},{5,13},{6,14},{7,15},{8,0},{9,1},... | collective-permute-start | bytes 294920 | tf_op jit(solution)/shard_map/ppermute | solution.py:681
  8.2 9.8 %collective-permute-start.2 = (bf16[4,8,1536]{2,1,0:T(8,128)(2,1)}, bf16[4,8,1536]{2,1,0:T(8,128)(2,1)S(1)}, u32[]{:S(2)}, u32[]{:S(2)}) collective-permute-start(bf16[4,8,1536]{2,1,0:T(8,128)(2,1)} %get-tuple-element.28), channel_id=1, source_target_pairs={{0,12},{1,13},{2,14},{3,15},{4,8},{5,9},{6,10},{7,11},{8,4},{9,5},... | collective-permute-start | bytes 294920 | tf_op jit(solution)/shard_map/ppermute | solution.py:681
  10.3 6.4 %copy-start = (bf16[16,8,3712]{2,1,0:T(8,128)(2,1)S(1)}, bf16[16,8,3712]{2,1,0:T(8,128)(2,1)}, u32[]{:S(2)}) copy-start(bf16[16,8,3712]{2,1,0:T(8,128)(2,1)} %pack.1.refs_2_) | copy-start | bytes 2850820
  10.3 6.4 %copy-start.5 = (s32[256]{0:T(256)S(1)}, s32[256]{0:T(256)}, u32[]{:S(2)}) copy-start(s32[256]{0:T(256)} %refs_0_.1) | copy-start | bytes 3076
  10.3 6.4 %copy-start.7 = (f32[1,2,256]{2,1,0:T(2,128)S(1)}, f32[1,2,256]{2,1,0:T(2,128)}, u32[]{:S(2)}) copy-start(f32[1,2,256]{2,1,0:T(2,128)} %param.14) | copy-start | bytes 6148
  10.4 29.8 %all-to-all-start = ((bf16[16,8,3712]{2,1,0:T(8,128)(2,1)}), bf16[16,8,3712]{2,1,0:T(8,128)(2,1)S(1)}, u32[]{:S(2)}, u32[]{:S(2)}) async-start(bf16[16,8,3712]{2,1,0:T(8,128)(2,1)} %pack.1.refs_2_), calls=%async_computation | async-start | bytes 1900544 | tf_op jit(solution)/shard_map/all_to_all | solution.py:780
  16.7 1.3 %copy-start.9 = (bf16[4,8,1536]{2,1,0:T(8,128)(2,1)S(1)}, bf16[4,8,1536]{2,1,0:T(8,128)(2,1)}, u32[]{:S(2)}) copy-start(bf16[4,8,1536]{2,1,0:T(8,128)(2,1)} %get-tuple-element.31.refs_2_) | copy-start | bytes 294916
  18.0 2.1 %copy-start.6 = (f32[2,512]{1,0:T(2,128)S(1)}, f32[2,512]{1,0:T(2,128)}, u32[]{:S(2)}) copy-start(f32[2,512]{1,0:T(2,128)} %refs_2_.1) | copy-start | bytes 12292
  18.0 2.1 %copy-start.8 = (f32[512]{0:T(512)S(1)}, f32[512]{0:T(512)}, u32[]{:S(2)}) copy-start(f32[512]{0:T(512)} %param.16) | copy-start | bytes 6148
  18.1 20.3 %collective-permute-start.3 = (bf16[4,2,8,1536]{3,2,1,0:T(8,128)(2,1)S(1)}, bf16[4,2,8,1536]{3,2,1,0:T(8,128)(2,1)S(1)}, u32[]{:S(2)}, u32[]{:S(2)}) collective-permute-start(bf16[4,2,8,1536]{3,2,1,0:T(8,128)(2,1)S(1)} %get-tuple-element.49), channel_id=1, source_target_pairs={{0,2},{1,3},{2,0},{3,1},{4,6},{5,7},{6,4},{7,5},{8,10},{9,11},{10,... | collective-permute-start | bytes 589832 | tf_op jit(solution)/shard_map/ppermute | solution.py:681
  38.5 1.7 %copy-start.1 = (s32[40960]{0:T(1024)S(1)}, s32[40960]{0:T(1024)}, u32[]{:S(2)}) copy-start(s32[40960]{0:T(1024)} %param.11) | copy-start | bytes 491524
  38.5 1.7 %copy-start.2 = (s32[2560]{0:T(1024)S(1)}, s32[2560]{0:T(1024)}, u32[]{:S(2)}) copy-start(s32[2560]{0:T(1024)} %param.12) | copy-start | bytes 30724
  38.5 1.7 %copy-start.4 = (bf16[32,128]{1,0:T(8,128)(2,1)S(1)}, bf16[32,128]{1,0:T(8,128)(2,1)}, u32[]{:S(2)}) copy-start(bf16[32,128]{1,0:T(8,128)(2,1)} %constant.4.clone.refs_5_.refs_7_) | copy-start | bytes 24580
  38.6 1.5 %collective-permute-start.4 = (bf16[8,1,8,1536]{3,2,0,1:T(8,128)(2,1)S(1)}, bf16[8,1,8,1536]{3,2,0,1:T(8,128)(2,1)S(1)}, u32[]{:S(2)}, u32[]{:S(2)}) collective-permute-start(bf16[8,1,8,1536]{3,2,0,1:T(8,128)(2,1)S(1)} %get-tuple-element.47), channel_id=1, source_target_pairs={{0,1},{1,0},{2,3},{3,2},{4,5},{5,4},{6,7},{7,6},{8,9},{9,8},{10,11... | collective-permute-start | bytes 589832 | tf_op jit(solution)/shard_map/ppermute | solution.py:681
  41.7 15.6 %copy-start.3 = (bf16[128,48]{1,0:T(8,128)(2,1)S(1)}, bf16[128,48]{1,0:T(8,128)(2,1)}, u32[]{:S(2)}) copy-start(bf16[128,48]{1,0:T(8,128)(2,1)} %constant.5.clone.refs_10_) | copy-start | bytes 36868
  41.7 5.4 %collective-permute-start.5 = (bf16[160,128]{1,0:T(8,128)(2,1)S(1)}, bf16[160,128]{1,0:T(8,128)(2,1)S(1)}, u32[]{:S(2)}, u32[]{:S(2)}) collective-permute-start(bf16[160,128]{1,0:T(8,128)(2,1)S(1)} %get-tuple-element.41), channel_id=1, source_target_pairs={{0,8},{1,9},{2,10},{3,11},{4,12},{5,13},{6,14},{7,15},{8,0},{9,1},... | collective-permute-start | bytes 122888 | tf_op jit(solution)/shard_map/ppermute | solution.py:681
  44.2 5.9 %collective-permute-start.6 = (bf16[160,128]{1,0:T(8,128)(2,1)S(1)}, bf16[160,128]{1,0:T(8,128)(2,1)S(1)}, u32[]{:S(2)}, u32[]{:S(2)}) collective-permute-start(bf16[160,128]{1,0:T(8,128)(2,1)S(1)} %get-tuple-element.41), channel_id=1, source_target_pairs={{0,12},{1,13},{2,14},{3,15},{4,8},{5,9},{6,10},{7,11},{8,4},{9,5},... | collective-permute-start | bytes 122888 | tf_op jit(solution)/shard_map/ppermute | solution.py:681
  45.6 4.4 %collective-permute-start.7 = (bf16[160,128]{1,0:T(8,128)(2,1)S(1)}, bf16[160,128]{1,0:T(8,128)(2,1)S(1)}, u32[]{:S(2)}, u32[]{:S(2)}) collective-permute-start(bf16[160,128]{1,0:T(8,128)(2,1)S(1)} %get-tuple-element.41), channel_id=1, source_target_pairs={{0,4},{1,5},{2,6},{3,7},{4,0},{5,1},{6,2},{7,3},{8,12},{9,13},{10,... | collective-permute-start | bytes 122888 | tf_op jit(solution)/shard_map/ppermute | solution.py:681
  50.1 5.4 %collective-permute-start.8 = (bf16[4,160,128]{2,1,0:T(8,128)(2,1)S(1)}, bf16[4,160,128]{2,1,0:T(8,128)(2,1)S(1)}, u32[]{:S(2)}, u32[]{:S(2)}) collective-permute-start(bf16[4,160,128]{2,1,0:T(8,128)(2,1)S(1)} %pad_maximum_fusion.3), channel_id=1, source_target_pairs={{0,2},{1,3},{2,0},{3,1},{4,6},{5,7},{6,4},{7,5},{8,10},{9,11},{10,... | collective-permute-start | bytes 491528 | tf_op jit(solution)/shard_map/ppermute | solution.py:681
  55.6 1.7 %collective-permute-start.9 = (bf16[8,160,128]{2,1,0:T(8,128)(2,1)S(1)}, bf16[8,160,128]{2,1,0:T(8,128)(2,1)S(1)}, u32[]{:S(2)}, u32[]{:S(2)}) collective-permute-start(bf16[8,160,128]{2,1,0:T(8,128)(2,1)S(1)} %get-tuple-element.50), channel_id=1, source_target_pairs={{0,1},{1,0},{2,3},{3,2},{4,5},{5,4},{6,7},{7,6},{8,9},{9,8},{10,11... | collective-permute-start | bytes 983048 | tf_op jit(solution)/shard_map/ppermute | solution.py:681

commit v6 on v5

--- a/solution.py
+++ b/solution.py
@@ -436,7 +436,7 @@
         odd = jnp.where(first_half, pltpu.roll(one_stat, GROUP, 1), other)
         paired[pl.ds(2 * tiles * pair, tiles, stride=2), :] = even
         paired[pl.ds(2 * tiles * pair + 1, tiles, stride=2), :] = odd
-    stats[...] = paired[...].astype(BF16)
+    stats[...] = paired[0 : PAIRS * 2 * tiles, :].astype(BF16)
 
 
 def solve_kernel(
@@ -839,7 +839,7 @@
     stats, early_model, early_modes = call(
         lambda *refs: early_stats_kernel(groups, tiles, by_flip, *refs),
         (jax.ShapeDtypeStruct((PAIRS * 2 * tiles, LANES), BF16), *tables(ahead)),
-        [pltpu.VMEM((tiles * 8, LANES), F32), pltpu.VMEM((PAIRS * 2 * tiles, LANES), F32)],
+        [pltpu.VMEM((padded * 8, LANES), F32), pltpu.VMEM((PAIRS * 2 * padded, LANES), F32)],
         "early_stats",
         [VMEM] * 8,
         12,

time: 63.6 us -> 63.6 us (level)
  no operation moved by 1% of the time
where the time goes in v6:
time: 63.6 us; the launch traced here: 63.4 us
  Pallas kernels  31.1 us (49%)
  starting transfers between devices  19 us (30%)
  waiting for transfers between devices  11.9 us (19%)
  between operations  0.95 us (1%)
    pallas_call x1, Pallas kernels, body(): call(lambda *refs: predict_kernel(groups, tiles, padded, *refs), (jax.Sha...  18.3 us
    ppermute x10, starting transfers between devices, exchange(): return lax.ppermute(block, 'wide', [(i, i ^ distance) for i in range(wide)])  12.7 us
    ppermute x10, waiting for transfers between devices, exchange(): return lax.ppermute(block, 'wide', [(i, i ^ distance) for i in range(wide)])  11.8 us
    all_to_all x1, starting transfers between devices, body(): observed = lax.all_to_all(packed, 'wide', 0, 0, tiled=True)  6.3 us
    pallas_call x1, Pallas kernels, body(): call(lambda *refs: solve_kernel(groups, tiles, by_flip, wide, *refs), (ja...  6.06 us
    pallas_call x1, Pallas kernels, body(): pl.pallas_call(lambda *refs: pack_kernel(wide, base, *refs), out_shape=ja...  2.06 us
    pallas_call x1, Pallas kernels, body(): pl.pallas_call(lambda *refs: pack_early_kernel(wide, base, *refs), out_sh...  1.93 us
  transfers between devices with their start and end apart: 11, of which 5 were waited for; matrix products, arithmetic and copies ran while one was open for 0% of the time, Pallas kernels for 34%

profile of v6, /device:TPU:0, one launch (start us, length us, event | category | flops | bytes accessed | tf_op | source)
XLA Modules:
  0.0 63.4 jit_solution(13204001490791732554)
XLA Ops:
  0.6 1.9 %pack_early.1 = (bf16[4,8,1536]{2,1,0:T(8,128)(2,1)}, bf16[4,8,1536]{2,1,0:T(8,128)(2,1)}, bf16[4,8,1536]{2,1,0:T(8,128)(2,1)}, bf16[4,8,1536]{2,1,0:T(8,128)(2,1)}) custom-call(bf16[2,16,8,2560]{3,2,1,0:T(8,128)(2,1)} %bitcast.48), custom_call_target="tpu_custom_call" | custom-call | tf_op jit(solution)/shard_map/pack_early/pallas_call | solution.py:749
  2.6 3.1 %collective-permute-start = (bf16[4,8,1536]{2,1,0:T(8,128)(2,1)}, bf16[4,8,1536]{2,1,0:T(8,128)(2,1)S(1)}, u32[]{:S(2)}, u32[]{:S(2)}) collective-permute-start(bf16[4,8,1536]{2,1,0:T(8,128)(2,1)} %get-tuple-element.25), channel_id=1, source_target_pairs={{0,4},{1,5},{2,6},{3,7},{4,0},{5,1},{6,2},{7,3},{8,12},{9,13},{10,... | collective-permute-start | bytes 294920 | tf_op jit(solution)/shard_map/ppermute | solution.py:681
  5.7 2.6 %collective-permute-start.1 = (bf16[4,8,1536]{2,1,0:T(8,128)(2,1)}, bf16[4,8,1536]{2,1,0:T(8,128)(2,1)S(1)}, u32[]{:S(2)}, u32[]{:S(2)}) collective-permute-start(bf16[4,8,1536]{2,1,0:T(8,128)(2,1)} %get-tuple-element.27), channel_id=1, source_target_pairs={{0,8},{1,9},{2,10},{3,11},{4,12},{5,13},{6,14},{7,15},{8,0},{9,1},... | collective-permute-start | bytes 294920 | tf_op jit(solution)/shard_map/ppermute | solution.py:681
  8.2 2.1 %pack.1.refs_2_ = bf16[16,8,3712]{2,1,0:T(8,128)(2,1)} custom-call(bf16[2,16,8,2560]{3,2,1,0:T(8,128)(2,1)} %bitcast.49, f32[8]{0:T(128)} %refs_1_.1, bf16[4,8,1536]{2,1,0:T(8,128)(2,1)} %get-tuple-element.31.refs_2_), custom_call_target="tpu_custom_call" | custom-call | tf_op jit(solution)/shard_map/pack/pallas_call | solution.py:763
  10.4 6.3 %all-to-all-start = ((bf16[16,8,3712]{2,1,0:T(8,128)(2,1)}), bf16[16,8,3712]{2,1,0:T(8,128)(2,1)S(1)}, u32[]{:S(2)}, u32[]{:S(2)}) async-start(bf16[16,8,3712]{2,1,0:T(8,128)(2,1)} %pack.1.refs_2_), calls=%async_computation | async-start | bytes 1900544 | tf_op jit(solution)/shard_map/all_to_all | solution.py:780
  16.7 1.3 %places.1 = (f32[176,128]{1,0:T(8,128)S(1)}, f32[176,128]{1,0:T(8,128)S(1)}) custom-call(s32[256]{0:T(256)S(1)} %copy-done.5, f32[2,256]{1,0:T(2,128)S(1)} %bitcast.46, bf16[16,8,3712]{2,1,0:T(8,128)(2,1)S(1)} %copy-done), custom_call_target="tpu_custom_call" | custom-call | flops 4000000000 | bytes 180224 | tf_op jit(solution)/shard_map/places/pallas_call | solution.py:782
  18.0 0.1 pad_maximum_fusion
  18.1 2.0 %collective-permute-start.3 = (bf16[4,2,8,1536]{3,2,1,0:T(8,128)(2,1)S(1)}, bf16[4,2,8,1536]{3,2,1,0:T(8,128)(2,1)S(1)}, u32[]{:S(2)}, u32[]{:S(2)}) collective-permute-start(bf16[4,2,8,1536]{3,2,1,0:T(8,128)(2,1)S(1)} %get-tuple-element.49), channel_id=1, source_target_pairs={{0,2},{1,3},{2,0},{3,1},{4,6},{5,7},{6,4},{7,5},{8,10},{9,11},{10,... | collective-permute-start | bytes 589832 | tf_op jit(solution)/shard_map/ppermute | solution.py:681
  20.1 18.3 %predict.1 = (f32[2560,128]{1,0:T(8,128)S(1)}, bf16[2560,128]{1,0:T(8,128)(2,1)S(1)}) custom-call(f32[176,128]{1,0:T(8,128)S(1)} %get-tuple-element.30.refs_0_, f32[176,128]{1,0:T(8,128)S(1)} %get-tuple-element.35.refs_1_, f32[2,512]{1,0:T(2,128)S(1)} %copy-done.6, f32[1,512]{1,0:T(1,128)S(1)} %bitcast.47), custom_call_target="tpu_custom_call" | custom-call | flops 6442450944 | bytes 3145728 | tf_op jit(solution)/shard_map/predict/pallas_call | solution.py:797
  38.6 0.1 collective-permute-start.4
  38.7 1.4 %collective-permute-done.4 = bf16[8,1,8,1536]{3,2,0,1:T(8,128)(2,1)S(1)} collective-permute-done((bf16[8,1,8,1536]{3,2,0,1:T(8,128)(2,1)S(1)}, bf16[8,1,8,1536]{3,2,0,1:T(8,128)(2,1)S(1)}, u32[]{:S(2)}, u32[]{:S(2)}) %collective-permute-start.4) | collective-permute-done | bytes 196640 | tf_op jit(solution)/shard_map/ppermute | solution.py:681
  40.2 1.0 %late_stats.1 = (f32[112,128]{1,0:T(8,128)S(1)}, bf16[3584,128]{1,0:T(8,128)(2,1)S(1)}, f32[224,512]{1,0:T(8,128)S(1)}, f32[128,128]{1,0:T(8,128)S(1)}) custom-call(bf16[16,8,3712]{2,1,0:T(8,128)(2,1)S(1)} %all-to-all-done.refs_0_.refs_1_, f32[2560,128]{1,0:T(8,128)S(1)} %get-tuple-element.36.refs_1_.refs_3_, ...), custom_call_target="tpu_custom_call" | custom-call | bytes 3670016 | tf_op jit(solution)/shard_map/late_stats/pallas_call | solution.py:826
  41.2 0.5 early_stats.1
  41.7 2.4 %collective-permute-start.5 = (bf16[160,128]{1,0:T(8,128)(2,1)S(1)}, bf16[160,128]{1,0:T(8,128)(2,1)S(1)}, u32[]{:S(2)}, u32[]{:S(2)}) collective-permute-start(bf16[160,128]{1,0:T(8,128)(2,1)S(1)} %get-tuple-element.41), channel_id=1, source_target_pairs={{0,8},{1,9},{2,10},{3,11},{4,12},{5,13},{6,14},{7,15},{8,0},{9,1},... | collective-permute-start | bytes 122888 | tf_op jit(solution)/shard_map/ppermute | solution.py:681
  44.2 1.5 %collective-permute-start.6 = (bf16[160,128]{1,0:T(8,128)(2,1)S(1)}, bf16[160,128]{1,0:T(8,128)(2,1)S(1)}, u32[]{:S(2)}, u32[]{:S(2)}) collective-permute-start(bf16[160,128]{1,0:T(8,128)(2,1)S(1)} %get-tuple-element.41), channel_id=1, source_target_pairs={{0,12},{1,13},{2,14},{3,15},{4,8},{5,9},{6,10},{7,11},{8,4},{9,5},... | collective-permute-start | bytes 122888 | tf_op jit(solution)/shard_map/ppermute | solution.py:681
  45.6 0.0 collective-permute-start.7
  45.6 1.5 %collective-permute-done.5 = bf16[160,128]{1,0:T(8,128)(2,1)S(1)} collective-permute-done((bf16[160,128]{1,0:T(8,128)(2,1)S(1)}, bf16[160,128]{1,0:T(8,128)(2,1)S(1)}, u32[]{:S(2)}, u32[]{:S(2)}) %collective-permute-start.5) | collective-permute-done | bytes 40992 | tf_op jit(solution)/shard_map/ppermute | solution.py:681
  47.1 2.9 %collective-permute-done.6 = bf16[160,128]{1,0:T(8,128)(2,1)S(1)} collective-permute-done((bf16[160,128]{1,0:T(8,128)(2,1)S(1)}, bf16[160,128]{1,0:T(8,128)(2,1)S(1)}, u32[]{:S(2)}, u32[]{:S(2)}) %collective-permute-start.6) | collective-permute-done | bytes 40992 | tf_op jit(solution)/shard_map/ppermute | solution.py:681
  50.1 1.0 %collective-permute-start.8 = (bf16[4,160,128]{2,1,0:T(8,128)(2,1)S(1)}, bf16[4,160,128]{2,1,0:T(8,128)(2,1)S(1)}, u32[]{:S(2)}, u32[]{:S(2)}) collective-permute-start(bf16[4,160,128]{2,1,0:T(8,128)(2,1)S(1)} %pad_maximum_fusion.3), channel_id=1, source_target_pairs={{0,2},{1,3},{2,0},{3,1},{4,6},{5,7},{6,4},{7,5},{8,10},{9,11},{10,... | collective-permute-start | bytes 491528 | tf_op jit(solution)/shard_map/ppermute | solution.py:681
  51.1 4.4 %collective-permute-done.8 = bf16[4,160,128]{2,1,0:T(8,128)(2,1)S(1)} collective-permute-done((bf16[4,160,128]{2,1,0:T(8,128)(2,1)S(1)}, bf16[4,160,128]{2,1,0:T(8,128)(2,1)S(1)}, u32[]{:S(2)}, u32[]{:S(2)}) %collective-permute-start.8) | collective-permute-done | bytes 163872 | tf_op jit(solution)/shard_map/ppermute | solution.py:681
  55.5 0.1 constant_dynamic-update-slice_fusion
  55.6 0.1 collective-permute-start.9
  55.6 1.6 %collective-permute-done.9 = bf16[8,160,128]{2,1,0:T(8,128)(2,1)S(1)} collective-permute-done((bf16[8,160,128]{2,1,0:T(8,128)(2,1)S(1)}, bf16[8,160,128]{2,1,0:T(8,128)(2,1)S(1)}, u32[]{:S(2)}, u32[]{:S(2)}) %collective-permute-start.9) | collective-permute-done | bytes 327712 | tf_op jit(solution)/shard_map/ppermute | solution.py:681
  57.3 6.1 %solve.1 = (f32[2,256]{1,0:T(2,128)}, bf16[2,1,128,2560]{3,2,1,0:T(8,128)(2,1)}) custom-call(bf16[16,160,128]{2,1,0:T(8,128)(2,1)S(1)} %constant_dynamic-update-slice_fusion.5.refs_0_, bf16[16,8,3712]{2,1,0:T(8,128)(2,1)S(1)} %all-to-all-done.refs_0_.refs_1_, bf16[16,8,1536]{2,1,0:T(8,128)(2,1)S(1)} %bitcast.37, ...), custom_call_target="tpu_custom_call" | custom-call | bytes 3932160 | tf_op jit(solution)/shard_map/solve/pallas_call | solution.py:849
  (38 shorter events, 0.4 us)
Async XLA Ops:
  2.6 7.8 %collective-permute-start = (bf16[4,8,1536]{2,1,0:T(8,128)(2,1)}, bf16[4,8,1536]{2,1,0:T(8,128)(2,1)S(1)}, u32[]{:S(2)}, u32[]{:S(2)}) collective-permute-start(bf16[4,8,1536]{2,1,0:T(8,128)(2,1)} %get-tuple-element.25), channel_id=1, source_target_pairs={{0,4},{1,5},{2,6},{3,7},{4,0},{5,1},{6,2},{7,3},{8,12},{9,13},{10,... | collective-permute-start | bytes 294920 | tf_op jit(solution)/shard_map/ppermute | solution.py:681
  5.7 12.4 %collective-permute-start.1 = (bf16[4,8,1536]{2,1,0:T(8,128)(2,1)}, bf16[4,8,1536]{2,1,0:T(8,128)(2,1)S(1)}, u32[]{:S(2)}, u32[]{:S(2)}) collective-permute-start(bf16[4,8,1536]{2,1,0:T(8,128)(2,1)} %get-tuple-element.27), channel_id=1, source_target_pairs={{0,8},{1,9},{2,10},{3,11},{4,12},{5,13},{6,14},{7,15},{8,0},{9,1},... | collective-permute-start | bytes 294920 | tf_op jit(solution)/shard_map/ppermute | solution.py:681
  8.2 9.8 %collective-permute-start.2 = (bf16[4,8,1536]{2,1,0:T(8,128)(2,1)}, bf16[4,8,1536]{2,1,0:T(8,128)(2,1)S(1)}, u32[]{:S(2)}, u32[]{:S(2)}) collective-permute-start(bf16[4,8,1536]{2,1,0:T(8,128)(2,1)} %get-tuple-element.28), channel_id=1, source_target_pairs={{0,12},{1,13},{2,14},{3,15},{4,8},{5,9},{6,10},{7,11},{8,4},{9,5},... | collective-permute-start | bytes 294920 | tf_op jit(solution)/shard_map/ppermute | solution.py:681
  10.3 6.4 %copy-start = (bf16[16,8,3712]{2,1,0:T(8,128)(2,1)S(1)}, bf16[16,8,3712]{2,1,0:T(8,128)(2,1)}, u32[]{:S(2)}) copy-start(bf16[16,8,3712]{2,1,0:T(8,128)(2,1)} %pack.1.refs_2_) | copy-start | bytes 2850820
  10.3 6.4 %copy-start.5 = (s32[256]{0:T(256)S(1)}, s32[256]{0:T(256)}, u32[]{:S(2)}) copy-start(s32[256]{0:T(256)} %refs_0_.1) | copy-start | bytes 3076
  10.3 6.4 %copy-start.7 = (f32[1,2,256]{2,1,0:T(2,128)S(1)}, f32[1,2,256]{2,1,0:T(2,128)}, u32[]{:S(2)}) copy-start(f32[1,2,256]{2,1,0:T(2,128)} %param.14) | copy-start | bytes 6148
  10.4 29.8 %all-to-all-start = ((bf16[16,8,3712]{2,1,0:T(8,128)(2,1)}), bf16[16,8,3712]{2,1,0:T(8,128)(2,1)S(1)}, u32[]{:S(2)}, u32[]{:S(2)}) async-start(bf16[16,8,3712]{2,1,0:T(8,128)(2,1)} %pack.1.refs_2_), calls=%async_computation | async-start | bytes 1900544 | tf_op jit(solution)/shard_map/all_to_all | solution.py:780
  16.7 1.3 %copy-start.9 = (bf16[4,8,1536]{2,1,0:T(8,128)(2,1)S(1)}, bf16[4,8,1536]{2,1,0:T(8,128)(2,1)}, u32[]{:S(2)}) copy-start(bf16[4,8,1536]{2,1,0:T(8,128)(2,1)} %get-tuple-element.31.refs_2_) | copy-start | bytes 294916
  18.0 2.1 %copy-start.6 = (f32[2,512]{1,0:T(2,128)S(1)}, f32[2,512]{1,0:T(2,128)}, u32[]{:S(2)}) copy-start(f32[2,512]{1,0:T(2,128)} %refs_2_.1) | copy-start | bytes 12292
  18.0 2.1 %copy-start.8 = (f32[512]{0:T(512)S(1)}, f32[512]{0:T(512)}, u32[]{:S(2)}) copy-start(f32[512]{0:T(512)} %param.16) | copy-start | bytes 6148
  18.1 20.3 %collective-permute-start.3 = (bf16[4,2,8,1536]{3,2,1,0:T(8,128)(2,1)S(1)}, bf16[4,2,8,1536]{3,2,1,0:T(8,128)(2,1)S(1)}, u32[]{:S(2)}, u32[]{:S(2)}) collective-permute-start(bf16[4,2,8,1536]{3,2,1,0:T(8,128)(2,1)S(1)} %get-tuple-element.49), channel_id=1, source_target_pairs={{0,2},{1,3},{2,0},{3,1},{4,6},{5,7},{6,4},{7,5},{8,10},{9,11},{10,... | collective-permute-start | bytes 589832 | tf_op jit(solution)/shard_map/ppermute | solution.py:681
  38.5 1.7 %copy-start.1 = (s32[40960]{0:T(1024)S(1)}, s32[40960]{0:T(1024)}, u32[]{:S(2)}) copy-start(s32[40960]{0:T(1024)} %param.11) | copy-start | bytes 491524
  38.5 1.7 %copy-start.2 = (s32[2560]{0:T(1024)S(1)}, s32[2560]{0:T(1024)}, u32[]{:S(2)}) copy-start(s32[2560]{0:T(1024)} %param.12) | copy-start | bytes 30724
  38.5 1.7 %copy-start.4 = (bf16[32,128]{1,0:T(8,128)(2,1)S(1)}, bf16[32,128]{1,0:T(8,128)(2,1)}, u32[]{:S(2)}) copy-start(bf16[32,128]{1,0:T(8,128)(2,1)} %constant.4.clone.refs_5_.refs_7_) | copy-start | bytes 24580
  38.6 1.5 %collective-permute-start.4 = (bf16[8,1,8,1536]{3,2,0,1:T(8,128)(2,1)S(1)}, bf16[8,1,8,1536]{3,2,0,1:T(8,128)(2,1)S(1)}, u32[]{:S(2)}, u32[]{:S(2)}) collective-permute-start(bf16[8,1,8,1536]{3,2,0,1:T(8,128)(2,1)S(1)} %get-tuple-element.47), channel_id=1, source_target_pairs={{0,1},{1,0},{2,3},{3,2},{4,5},{5,4},{6,7},{7,6},{8,9},{9,8},{10,11... | collective-permute-start | bytes 589832 | tf_op jit(solution)/shard_map/ppermute | solution.py:681
  41.7 15.6 %copy-start.3 = (bf16[128,48]{1,0:T(8,128)(2,1)S(1)}, bf16[128,48]{1,0:T(8,128)(2,1)}, u32[]{:S(2)}) copy-start(bf16[128,48]{1,0:T(8,128)(2,1)} %constant.5.clone.refs_10_) | copy-start | bytes 36868
  41.7 5.4 %collective-permute-start.5 = (bf16[160,128]{1,0:T(8,128)(2,1)S(1)}, bf16[160,128]{1,0:T(8,128)(2,1)S(1)}, u32[]{:S(2)}, u32[]{:S(2)}) collective-permute-start(bf16[160,128]{1,0:T(8,128)(2,1)S(1)} %get-tuple-element.41), channel_id=1, source_target_pairs={{0,8},{1,9},{2,10},{3,11},{4,12},{5,13},{6,14},{7,15},{8,0},{9,1},... | collective-permute-start | bytes 122888 | tf_op jit(solution)/shard_map/ppermute | solution.py:681
  44.2 5.9 %collective-permute-start.6 = (bf16[160,128]{1,0:T(8,128)(2,1)S(1)}, bf16[160,128]{1,0:T(8,128)(2,1)S(1)}, u32[]{:S(2)}, u32[]{:S(2)}) collective-permute-start(bf16[160,128]{1,0:T(8,128)(2,1)S(1)} %get-tuple-element.41), channel_id=1, source_target_pairs={{0,12},{1,13},{2,14},{3,15},{4,8},{5,9},{6,10},{7,11},{8,4},{9,5},... | collective-permute-start | bytes 122888 | tf_op jit(solution)/shard_map/ppermute | solution.py:681
  45.6 4.4 %collective-permute-start.7 = (bf16[160,128]{1,0:T(8,128)(2,1)S(1)}, bf16[160,128]{1,0:T(8,128)(2,1)S(1)}, u32[]{:S(2)}, u32[]{:S(2)}) collective-permute-start(bf16[160,128]{1,0:T(8,128)(2,1)S(1)} %get-tuple-element.41), channel_id=1, source_target_pairs={{0,4},{1,5},{2,6},{3,7},{4,0},{5,1},{6,2},{7,3},{8,12},{9,13},{10,... | collective-permute-start | bytes 122888 | tf_op jit(solution)/shard_map/ppermute | solution.py:681
  50.1 5.4 %collective-permute-start.8 = (bf16[4,160,128]{2,1,0:T(8,128)(2,1)S(1)}, bf16[4,160,128]{2,1,0:T(8,128)(2,1)S(1)}, u32[]{:S(2)}, u32[]{:S(2)}) collective-permute-start(bf16[4,160,128]{2,1,0:T(8,128)(2,1)S(1)} %pad_maximum_fusion.3), channel_id=1, source_target_pairs={{0,2},{1,3},{2,0},{3,1},{4,6},{5,7},{6,4},{7,5},{8,10},{9,11},{10,... | collective-permute-start | bytes 491528 | tf_op jit(solution)/shard_map/ppermute | solution.py:681
  55.6 1.7 %collective-permute-start.9 = (bf16[8,160,128]{2,1,0:T(8,128)(2,1)S(1)}, bf16[8,160,128]{2,1,0:T(8,128)(2,1)S(1)}, u32[]{:S(2)}, u32[]{:S(2)}) collective-permute-start(bf16[8,160,128]{2,1,0:T(8,128)(2,1)S(1)} %get-tuple-element.50), channel_id=1, source_target_pairs={{0,1},{1,0},{2,3},{3,2},{4,5},{5,4},{6,7},{7,6},{8,9},{9,8},{10,11... | collective-permute-start | bytes 983048 | tf_op jit(solution)/shard_map/ppermute | solution.py:681
